TPU v7x, 32 devices: a whole 2x2x4 slice. The times are simulated.
32 devices in a mesh: groups: 2 (over y), ep: 16 (over z, x, core).
Axes of the slice: x: 2, y: 2, z: 4, core: 2. Of those that a mesh axis runs over, the one named last changes fastest.
Arguments:
- tokens: bfloat16 [2048, 2880], P(('groups', 'ep')), parts along dimension 0, may hold values from -6 to 6
- expert_ids: int32 [2048, 4], P(('groups', 'ep')), parts along dimension 0, may hold values from 0 to 15, all different within a row; in each aligned block of 64 rows (0 to 63, 64 to 127, ...) at most 18 rows name the same one
- gate_ints: int32 [2048, 4], P(('groups', 'ep')), parts along dimension 0, may hold values from 1 to 255
- norm_gain: float32 [2880], replicated, may hold values from 0.5 to 2
- weight_in: bfloat16 [16, 2880, 5760], P('ep'), may hold values from -0.109375 to 0.109375
- bias_in: float32 [16, 5760], P('ep'), may hold values from -3 to 3
- weight_out: bfloat16 [16, 2880, 2880], P('ep'), may hold values from -0.109375 to 0.109375
- bias_out: float32 [16, 2880], replicated, may hold values from -3 to 3
Outputs:
- mixed: bfloat16 [2048, 2880], P(('groups', 'ep')), parts along dimension 0
There are 2 independent parts, one for each index of `groups`. A program takes and returns all parts, laid end to end along the dimension named above; an argument that names none is the same for every part. Nothing has to cross between parts.
Inputs may be any that keep to these rules, and one draw needn't show every extreme that they name: `expert_ids`: each row names 4 different experts. Within the rows of one device (aligned blocks of 64 rows) no expert is named more than 18 times.
All inputs are finite; a program needn't handle non-finite values.
Results may differ from a plain program's by a relative error of at most 0.0065.
Values may be sent and summed in bfloat16 or wider, within the bound.
No kernel may reach another device: no remote copies, remote signals or barrier semaphores. Data moves between devices by JAX's collectives and lax.ppermute only.
A program may use at most 256 MiB of HBM per device.

v0:
```python
import functools

import jax
import jax.numpy as jnp
from jax import lax
from jax.experimental import pallas as pl
from jax.experimental.pallas import tpu as pltpu
from jax.sharding import PartitionSpec as P

CAP = 18
LANES = 128
BLOCK = 768
NORM_MIB = 16
SMALL_MIB = 16
EXPERT_MIB = 50
COLUMNS = 1152
LEAD = -1
ACT_COLS = 256


def route_weights(gate_ints):
    int_gates = gate_ints.astype(jnp.float32)
    return int_gates / jnp.sum(int_gates, axis=1, keepdims=True)


def normalize(tokens, norm_gain):
    tok_float = tokens.astype(jnp.float32)
    row_scale = lax.rsqrt(jnp.mean(tok_float * tok_float, axis=1, keepdims=True) + 1e-05)
    return (tok_float * row_scale * norm_gain[None, :]).astype(jnp.bfloat16)


def exchange_shards(tokens, expert_ids, gate_ints, norm_gain, weight_in, bias_in, weight_out, bias_out):
    device_count = lax.axis_size("ep")
    expert_count = bias_out.shape[0]
    part_count = device_count // expert_count
    row_count, model_width = tokens.shape
    top_count = expert_ids.shape[1]
    capacity = CAP
    tok_float = tokens.astype(jnp.float32)
    normed = normalize(tokens, norm_gain)
    route_weight = route_weights(gate_ints)
    flat_ids = expert_ids.reshape(row_count * top_count)
    one_hot = (flat_ids[:, None] == jnp.arange(expert_count, dtype=jnp.int32)[None, :]).astype(jnp.int32)
    slot_rank = jnp.sum((jnp.cumsum(one_hot, axis=0) - one_hot) * one_hot, axis=1)
    slot_target = (flat_ids * capacity + slot_rank).reshape(row_count, top_count)
    slot_ids = jnp.arange(expert_count * capacity, dtype=jnp.int32)
    slot_match = slot_target[None, :, :] == slot_ids[:, None, None]
    picker = jnp.any(slot_match, axis=2).astype(jnp.bfloat16)
    placed = jnp.dot(picker, normed, preferred_element_type=jnp.float32).astype(jnp.bfloat16)
    combiner = jnp.transpose(jnp.sum(jnp.where(slot_match, route_weight[None, :, :], 0.0), axis=2))
    outgoing = jnp.broadcast_to(
        placed.reshape(expert_count, 1, capacity, model_width),
        (expert_count, part_count, capacity, model_width),
    ).reshape(device_count, capacity, model_width)
    arrived = lax.all_to_all(outgoing, "ep", split_axis=0, concat_axis=0, tiled=True)
    source_count, slot_count = arrived.shape[:2]
    flat_rows = arrived.reshape(source_count * slot_count, model_width)
    pre_act = jnp.dot(flat_rows, weight_in[0], preferred_element_type=jnp.float32) + bias_in[0][None, :]
    half_width = pre_act.shape[1] // 2
    gate_part = pre_act[:, :half_width]
    up_part = pre_act[:, half_width:]
    activated = (gate_part * jax.nn.sigmoid(1.702 * gate_part) * (up_part + 1.0)).astype(jnp.bfloat16)
    result = jnp.dot(activated, weight_out[0], preferred_element_type=jnp.float32).astype(jnp.bfloat16)
    returned = lax.all_to_all(
        result.reshape(source_count, slot_count, model_width), "ep", split_axis=0, concat_axis=0, tiled=True
    )
    part_sum = jnp.sum(
        returned.reshape(expert_count, part_count, capacity, model_width), axis=1, dtype=jnp.float32
    ).reshape(expert_count * capacity, model_width)
    moe_rows = jnp.dot(combiner, part_sum, precision=lax.Precision.HIGHEST)
    expert_hot = expert_ids[:, :, None] == jnp.arange(expert_count, dtype=jnp.int32)[None, None, :]
    expert_weight = jnp.sum(jnp.where(expert_hot, route_weight[:, :, None], 0.0), axis=1)
    bias_term = jnp.dot(expert_weight, bias_out, precision=lax.Precision.HIGHEST)
    return (tok_float + moe_rows + bias_term).astype(jnp.bfloat16)


def norm_kernel(top, tokens_ref, ids_ref, gates_ref, gain_ref, first_ref, second_ref):
    f32, bf16 = jnp.float32, jnp.bfloat16
    tok = tokens_ref[...].astype(f32)
    scale = lax.rsqrt(jnp.mean(tok * tok, axis=1, keepdims=True) + 1e-05)
    normed = (tok * scale * gain_ref[...][None, :]).astype(bf16)
    cut = tok.shape[1] - second_ref.shape[1]
    spare = first_ref.shape[1] - cut
    sub = lax.broadcasted_iota(jnp.int32, (top, spare), 0)
    lane = lax.broadcasted_iota(jnp.int32, (top, spare), 1)
    turn = (((0,), (0,)), ((), ()))
    tail = lax.dot_general(
        ids_ref[...].astype(f32), jnp.where(lane == sub, 1.0, 0.0), turn, preferred_element_type=f32
    ) + lax.dot_general(
        gates_ref[...].astype(f32), jnp.where(lane == sub + top, 1.0, 0.0), turn, preferred_element_type=f32
    )
    first_ref[:, :cut] = normed[:, :cut]
    first_ref[:, cut:] = tail.astype(bf16)
    second_ref[...] = normed[:, cut:]


def gather_rows(pieces, held):
    at = 0
    for ref in pieces:
        held[at : at + ref.shape[0]] = ref[...]
        at += ref.shape[0]


def route_kernel(top, cut, count, experts_ref, *refs):
    f32, bf16 = jnp.float32, jnp.bfloat16
    own_out, mate_out, picker_out, placer_out, held = refs[count:]
    gather_rows(refs[:count], held)
    tail = held[:, cut:]
    slots = own_out.shape[0]
    rows = tail.shape[0]
    sub = lax.broadcasted_iota(jnp.int32, (16, tail.shape[1]), 0)
    lane = lax.broadcasted_iota(jnp.int32, (16, tail.shape[1]), 1)
    pick_id = jnp.where((sub == lane) & (sub < top), 1.0, 0.0).astype(bf16)
    ids = lax.dot_general(pick_id, tail, (((1,), (1,)), ((), ())), preferred_element_type=f32)
    entry = lax.broadcasted_iota(jnp.int32, ids.shape, 0)
    first = lax.broadcasted_iota(jnp.int32, (rows, rows), 0)
    second = lax.broadcasted_iota(jnp.int32, (rows, rows), 1)
    upper = jnp.where(first <= second, 1.0, 0.0).astype(bf16)
    lower = jnp.where(first >= second, 1.0, 0.0).astype(bf16)
    tail_float = tail.astype(f32)
    tail_lane = lax.broadcasted_iota(jnp.int32, tail.shape, 1)
    slot = lax.broadcasted_iota(jnp.int32, (slots, rows), 0).astype(f32) + 1.0
    slot_lane = lax.broadcasted_iota(jnp.int32, (rows, slots), 1).astype(f32) + 1.0
    placers = []
    for i, out in enumerate((own_out, mate_out)):
        expert = experts_ref[0, i].astype(f32)
        named = jnp.sum(jnp.where((ids == expert) & (entry < top), 1.0, 0.0), axis=0, keepdims=True)
        number = jnp.dot(jnp.broadcast_to(named, (16, rows)).astype(bf16), upper, preferred_element_type=f32)[:1]
        picker = jnp.where((number == slot) & (named > 0.5), 1.0, 0.0).astype(bf16)
        picker_out[i * slots : (i + 1) * slots] = picker
        out[...] = jnp.dot(picker, held[...], preferred_element_type=f32).astype(bf16)
        named = jnp.sum(jnp.where((tail_float == expert) & (tail_lane < top), 1.0, 0.0), axis=1, keepdims=True)
        number = jnp.dot(lower, jnp.broadcast_to(named, (rows, LANES)).astype(bf16), preferred_element_type=f32)
        placers.append(jnp.where((number[:, :1] == slot_lane) & (named > 0.5), 1.0, 0.0))
    placer_out[...] = jnp.concatenate(placers, axis=1).astype(bf16)


def pick_kernel(count, picker_ref, *refs):
    own_out, mate_out, held = refs[count:]
    gather_rows(refs[:count], held)
    rows = jnp.dot(picker_ref[...], held[...], preferred_element_type=jnp.float32).astype(jnp.bfloat16)
    slots = own_out.shape[0]
    own_out[...] = rows[:slots]
    mate_out[...] = rows[slots:]


def slot_weights(tail, top, expert):
    f32 = jnp.float32
    lane = lax.broadcasted_iota(jnp.int32, tail.shape, 1)
    spare = tail.shape[1]
    first = lax.broadcasted_iota(jnp.int32, (spare, spare), 0)
    second = lax.broadcasted_iota(jnp.int32, (spare, spare), 1)
    shift = jnp.where((first == second + top) & (second < top), 1.0, 0.0).astype(jnp.bfloat16)
    gates = jnp.dot(tail, shift, preferred_element_type=f32)
    hit = (tail.astype(f32) == expert) & (lane < top)
    total = jnp.sum(gates, axis=1, keepdims=True)
    return jnp.sum(jnp.where(hit, gates, 0.0), axis=1, keepdims=True) / jnp.maximum(total, 1.0)


def activate(pre, act, start, end):
    hidden = act.shape[1]
    for at in range(start, end, ACT_COLS):
        to = min(at + ACT_COLS, end)
        gate = pre[:, at:to]
        up = pre[:, hidden + at : hidden + to]
        act[:, at:to] = (gate * jax.nn.sigmoid(1.702 * gate) * (up + 1.0)).astype(act.dtype)


def expert_kernel(
    top, steps_in, spans, experts_ref, own_first, mate_first, own_second, mate_second, win_ref, bin_ref, wout_hbm,
    bout_ref, own_a, mate_a, own_b, mate_b, rows_first, rows_second, pre, act, slot_weight, sems, *held,
):
    step = pl.program_id(0)
    f32, bf16 = jnp.float32, jnp.bfloat16
    slots, hidden, block = own_first.shape[0], act.shape[1], win_ref.shape[2]
    width = win_ref.shape[1]
    cut = width - own_second.shape[1]
    early = max((steps_in - 1) * block - hidden, 0) // LANES * LANES
    copies = [
        pltpu.make_async_copy(wout_hbm.at[0, :, pl.ds(at, size)], ref, sems.at[i])
        for i, ((at, size), ref) in enumerate(zip(spans, held))
    ]

    @pl.when(step == 0)
    def _():
        expert = experts_ref[0, 0].astype(f32)
        for i, (low, high) in enumerate(((own_first, own_second), (mate_first, mate_second))):
            rows_first[i * slots : (i + 1) * slots] = low[...]
            rows_second[i * slots : (i + 1) * slots] = high[...]
            weight = slot_weights(low[:, cut:], top, expert)
            slot_weight[i * slots : (i + 1) * slots] = jnp.broadcast_to(weight, (slots, LANES))

    for i, copy in enumerate(copies):

        @pl.when(step == max(steps_in - len(copies) + i - LEAD, 0))
        def _():
            copy.start()

    def first_layer(at):
        total = jnp.dot(rows_first[:, :cut], win_ref[0, :cut], preferred_element_type=f32)
        total += jnp.dot(rows_second[...], win_ref[0, cut:], preferred_element_type=f32)
        pre[:, pl.ds(at, block)] = total + bin_ref[...]

    @pl.when(step < steps_in - 1)
    def _():
        first_layer(pl.multiple_of(step * block, block))

    @pl.when(step == steps_in - 1)
    def _():
        first_layer((steps_in - 1) * block)
        activate(pre, act, 0, early)

    @pl.when(step == steps_in)
    def _():
        activate(pre, act, early, hidden)
        edge = own_a.shape[1]
        for copy, ref, (at, size) in zip(copies, held, spans):
            copy.wait()
            result = jnp.dot(act[:, :early], ref[:early], preferred_element_type=f32)
            result += jnp.dot(act[:, early:], ref[early:], preferred_element_type=f32)
            result = ((result + bout_ref[:, at : at + size]) * slot_weight[:, :1]).astype(bf16)
            inside = min(max(edge - at, 0), size)
            for row, low, high in ((0, own_a, own_b), (slots, mate_a, mate_b)):
                if inside:
                    low[:, at : at + inside] = result[row : row + slots, :inside]
                if inside < size:
                    high[:, at + inside - edge : at + size - edge] = result[row : row + slots, inside:]
        for ref in (own_b, mate_b):
            ref[:, width - edge :] = jnp.zeros((slots, ref.shape[1] - (width - edge)), bf16)


def spread_kernel(placer_ref, own_ref, mate_ref, *out_refs):
    slots = own_ref.shape[0]
    f32 = jnp.float32
    total = jnp.dot(placer_ref[:, :slots], own_ref[...], preferred_element_type=f32)
    total += jnp.dot(placer_ref[:, slots:], mate_ref[...], preferred_element_type=f32)
    at = 0
    for ref in out_refs:
        ref[...] = total[at : at + ref.shape[0]].astype(ref.dtype)
        at += ref.shape[0]


def params(mib):
    return pltpu.CompilerParams(vmem_limit_bytes=mib * 2**20)


def cost(macs, moved):
    return pl.CostEstimate(flops=2 * macs, bytes_accessed=moved, transcendentals=0)


def ring_shards(tokens, expert_ids, gate_ints, norm_gain, weight_in, bias_in, weight_out, bias_out):
    device_count = lax.axis_size("ep")
    chips = device_count // 2
    reach = chips // 2
    ring = list(range(0, chips, 2)) + list(range(chips - 1, 0, -2))
    right = [(ring[i] * 2 + k, ring[(i + 1) % chips] * 2 + k) for i in range(chips) for k in range(2)]
    left = [(b, a) for a, b in right]
    mate = [(i, i ^ 1) for i in range(device_count)]
    send = lambda value, pairs: lax.ppermute(value, "ep", pairs)
    bf16, f32 = jnp.bfloat16, jnp.float32
    row_count, width = tokens.shape
    top = expert_ids.shape[1]
    hidden = weight_out.shape[1]
    half = row_count // 2
    lanes = [2 * BLOCK, width + -width % LANES - 2 * BLOCK]
    cut = width - lanes[1]
    slots, all_rows = chips * CAP, chips * row_count
    vmem = pl.BlockSpec(memory_space=pltpu.VMEM)
    smem = pl.BlockSpec(memory_space=pltpu.SMEM)
    shape = lambda rows, cols, dtype=bf16: jax.ShapeDtypeStruct((rows, cols), dtype)

    chains = pl.pallas_call(
        functools.partial(norm_kernel, top),
        in_specs=[vmem] * 4,
        out_specs=[vmem] * 2,
        out_shape=[shape(row_count, w) for w in lanes],
        compiler_params=params(NORM_MIB),
    )(tokens, expert_ids.T, gate_ints.T, norm_gain)
    me = lax.axis_index("ep").astype(jnp.int32)
    experts = jnp.stack([me, me ^ 1]).reshape(1, 2)
    bias_row = lax.dynamic_slice_in_dim(bias_out, me, 1, axis=0)

    held = [[chain] for chain in chains]
    going = [(chain, chain) for chain in chains]
    for hop in range(1, reach + 1):
        for c in range(len(chains)):
            to_right, to_left = going[c]
            if hop == reach:
                to_right, to_left = to_right[:half], to_left[half:]
                if c:
                    to_right, to_left, _ = lax.optimization_barrier((to_right, to_left, waited))
                waited = going[c]
            going[c] = send(to_right, right), send(to_left, left)
            held[c] += going[c]
    order = [0]
    for hop in range(1, reach):
        order += [-hop, hop]
    own_first, mate_first, picker, placer = pl.pallas_call(
        functools.partial(route_kernel, top, cut, len(held[0])),
        in_specs=[smem] + [vmem] * len(held[0]),
        out_specs=[vmem] * 4,
        out_shape=[shape(slots, lanes[0])] * 2 + [shape(2 * slots, all_rows), shape(all_rows, 2 * slots)],
        scratch_shapes=[pltpu.VMEM((all_rows, lanes[0]), bf16)],
        cost_estimate=cost(2 * slots * all_rows * lanes[0], 2**20),
        compiler_params=params(SMALL_MIB),
    )(experts, *held[0])
    mate_first = send(mate_first, mate)
    own_second, mate_second = pl.pallas_call(
        functools.partial(pick_kernel, len(held[1])),
        in_specs=[vmem] * (1 + len(held[1])),
        out_specs=[vmem] * 2,
        out_shape=[shape(slots, lanes[1])] * 2,
        scratch_shapes=[pltpu.VMEM((all_rows, lanes[1]), bf16)],
        cost_estimate=cost(2 * slots * all_rows * lanes[1], 2**20),
        compiler_params=params(SMALL_MIB),
    )(picker, *held[1])
    mate_second = send(mate_second, mate)

    steps_in = pl.cdiv(2 * hidden, COLUMNS)
    spans = [(at, min(COLUMNS, width - at)) for at in range(0, width, COLUMNS)]
    first = lambda j: jnp.minimum(j, steps_in - 1)
    whole = lambda rows, cols: pl.BlockSpec((rows, cols), lambda j: (0, 0), pipeline_mode=pl.Buffered(1))
    own_a, mate_a, own_b, mate_b = pl.pallas_call(
        functools.partial(expert_kernel, top, steps_in, spans),
        grid=(steps_in + 1,),
        in_specs=[
            smem, whole(slots, lanes[0]), whole(slots, lanes[0]), whole(slots, lanes[1]), whole(slots, lanes[1]),
            pl.BlockSpec((1, width, COLUMNS), lambda j: (0, 0, first(j))),
            pl.BlockSpec((1, COLUMNS), lambda j: (0, first(j))),
            pl.BlockSpec(memory_space=pl.ANY),
            whole(1, width),
        ],
        out_specs=[whole(slots, w) for w in (lanes[0], lanes[0], lanes[1], lanes[1])],
        out_shape=[shape(slots, w) for w in (lanes[0], lanes[0], lanes[1], lanes[1])],
        scratch_shapes=[
            pltpu.VMEM((2 * slots, lanes[0]), bf16),
            pltpu.VMEM((2 * slots, lanes[1]), bf16),
            pltpu.VMEM((2 * slots, steps_in * COLUMNS), f32),
            pltpu.VMEM((2 * slots, hidden), bf16),
            pltpu.VMEM((2 * slots, LANES), f32),
            pltpu.SemaphoreType.DMA((len(spans),)),
        ]
        + [pltpu.VMEM((hidden, size), bf16) for _, size in spans],
        cost_estimate=cost(2 * slots * width * 3 * hidden, 6 * width * hidden),
        compiler_params=params(EXPERT_MIB),
    )(experts, own_first, mate_first, own_second, mate_second, weight_in, bias_in, weight_out, bias_row)

    heights = [row_count] * (chips - 1) + [half, half]
    add = lambda a, b: (a.astype(f32) + b.astype(f32)).astype(bf16)

    def spread(own, other):
        sums = pl.pallas_call(
            spread_kernel,
            in_specs=[vmem] * 3,
            out_specs=[vmem] * len(heights),
            out_shape=[shape(rows, own.shape[1]) for rows in heights],
            cost_estimate=cost(2 * slots * all_rows * own.shape[1], 2**20),
            compiler_params=params(SMALL_MIB),
        )(placer, own, send(other, mate))
        return dict(zip(order + ["right", "left"], sums))

    owed = [spread(own_a, mate_a), spread(own_b, mate_b)]
    going = [(o["right"], o["left"]) for o in owed]
    for hop in range(reach - 1, -1, -1):
        for c in range(len(owed)):
            up, down = send(going[c][0], right), send(going[c][1], left)
            if hop == reach - 1:
                ahead, behind = owed[c][hop], owed[c][-hop]
                up = jnp.concatenate([add(ahead[:half], up), ahead[half:]], axis=0)
                down = jnp.concatenate([behind[:half], add(behind[half:], down)], axis=0)
            elif hop:
                up, down = add(owed[c][hop], up), add(owed[c][-hop], down)
            going[c] = up, down
    moe = [o[0].astype(f32) + up.astype(f32) + down.astype(f32) for o, (up, down) in zip(owed, going)]
    return (tokens.astype(f32) + jnp.concatenate(moe, axis=1)[:, :width]).astype(bf16)


def solution(mesh):
    ep = mesh.shape["ep"]

    def shards(*arrays):
        whole_experts = arrays[-1].shape[0] == ep and ep == 16
        return (ring_shards if whole_experts else exchange_shards)(*arrays)

    return jax.shard_map(
        shards,
        mesh=mesh,
        in_specs=(
            P(("groups", "ep"), None),
            P(("groups", "ep"), None),
            P(("groups", "ep"), None),
            P(),
            P("ep", None, None),
            P("ep", None),
            P("ep", None, None),
            P(),
        ),
        out_specs=P(("groups", "ep"), None),
        check_vma=False,
    )
```

profile of v0, /device:TPU:0, one launch (start us, length us, event | category | flops | bytes accessed | tf_op | source)
XLA Modules:
  0.0 108.7 jit_solution(7858696985919010955)
XLA Ops:
  3.4 3.1 %collective-permute-start = (bf16[64,1536]{1,0:T(8,128)(2,1)S(1)}, bf16[64,1536]{1,0:T(8,128)(2,1)S(1)}, u32[]{:S(2)}, u32[]{:S(2)}) collective-permute-start(bf16[64,1536]{1,0:T(8,128)(2,1)S(1)} %get-tuple-element.37.refs_0_), channel_id=1, source_target_pairs={{0,4},{1,5},{4,8},{5,9},{8,12},{9,13},{12,14},{13,15},{14,10},{15,... | collective-permute-start | bytes 589832 | tf_op jit(solution)/shard_map/ppermute | solution.py:259
  6.5 2.0 %collective-permute-start.9 = (bf16[64,1408]{1,0:T(8,128)(2,1)S(1)}, bf16[64,1408]{1,0:T(8,128)(2,1)S(1)}, u32[]{:S(2)}, u32[]{:S(2)}) collective-permute-start(bf16[64,1408]{1,0:T(8,128)(2,1)S(1)} %get-tuple-element.42.refs_0_), channel_id=1, source_target_pairs={{0,4},{1,5},{4,8},{5,9},{8,12},{9,13},{12,14},{13,15},{14,10},{15,... | collective-permute-start | bytes 540680 | tf_op jit(solution)/shard_map/ppermute | solution.py:259
  8.5 3.6 %collective-permute-done.refs_1_ = bf16[64,1536]{1,0:T(8,128)(2,1)S(1)} collective-permute-done((bf16[64,1536]{1,0:T(8,128)(2,1)S(1)}, bf16[64,1536]{1,0:T(8,128)(2,1)S(1)}, u32[]{:S(2)}, u32[]{:S(2)}) %collective-permute-start) | collective-permute-done | bytes 196640 | tf_op jit(solution)/shard_map/ppermute | solution.py:259
  12.1 2.1 %collective-permute-start.2 = (bf16[64,1536]{1,0:T(8,128)(2,1)S(1)}, bf16[64,1536]{1,0:T(8,128)(2,1)S(1)}, u32[]{:S(2)}, u32[]{:S(2)}) collective-permute-start(bf16[64,1536]{1,0:T(8,128)(2,1)S(1)} %collective-permute-done.refs_1_), channel_id=1, source_target_pairs={{0,4},{1,5},{4,8},{5,9},{8,12},{9,13},{12,14},{13,15},{14,10},{15,... | collective-permute-start | bytes 589832 | tf_op jit(solution)/shard_map/ppermute | solution.py:259
  14.3 1.7 %collective-permute-done.9.refs_1_ = bf16[64,1408]{1,0:T(8,128)(2,1)S(1)} collective-permute-done((bf16[64,1408]{1,0:T(8,128)(2,1)S(1)}, bf16[64,1408]{1,0:T(8,128)(2,1)S(1)}, u32[]{:S(2)}, u32[]{:S(2)}) %collective-permute-start.9) | collective-permute-done | bytes 180256 | tf_op jit(solution)/shard_map/ppermute | solution.py:259
  16.0 2.1 %collective-permute-start.11 = (bf16[64,1408]{1,0:T(8,128)(2,1)S(1)}, bf16[64,1408]{1,0:T(8,128)(2,1)S(1)}, u32[]{:S(2)}, u32[]{:S(2)}) collective-permute-start(bf16[64,1408]{1,0:T(8,128)(2,1)S(1)} %collective-permute-done.9.refs_1_), channel_id=1, source_target_pairs={{0,4},{1,5},{4,8},{5,9},{8,12},{9,13},{12,14},{13,15},{14,10},{15,... | collective-permute-start | bytes 540680 | tf_op jit(solution)/shard_map/ppermute | solution.py:259
  18.2 2.0 %collective-permute-done.2.refs_3_ = bf16[64,1536]{1,0:T(8,128)(2,1)S(1)} collective-permute-done((bf16[64,1536]{1,0:T(8,128)(2,1)S(1)}, bf16[64,1536]{1,0:T(8,128)(2,1)S(1)}, u32[]{:S(2)}, u32[]{:S(2)}) %collective-permute-start.2) | collective-permute-done | bytes 196640 | tf_op jit(solution)/shard_map/ppermute | solution.py:259
  20.2 2.1 %collective-permute-start.4 = (bf16[64,1536]{1,0:T(8,128)(2,1)S(1)}, bf16[64,1536]{1,0:T(8,128)(2,1)S(1)}, u32[]{:S(2)}, u32[]{:S(2)}) collective-permute-start(bf16[64,1536]{1,0:T(8,128)(2,1)S(1)} %collective-permute-done.2.refs_3_), channel_id=1, source_target_pairs={{0,4},{1,5},{4,8},{5,9},{8,12},{9,13},{12,14},{13,15},{14,10},{15,... | collective-permute-start | bytes 589832 | tf_op jit(solution)/shard_map/ppermute | solution.py:259
  22.4 1.7 %collective-permute-done.11.refs_3_ = bf16[64,1408]{1,0:T(8,128)(2,1)S(1)} collective-permute-done((bf16[64,1408]{1,0:T(8,128)(2,1)S(1)}, bf16[64,1408]{1,0:T(8,128)(2,1)S(1)}, u32[]{:S(2)}, u32[]{:S(2)}) %collective-permute-start.11) | collective-permute-done | bytes 180256 | tf_op jit(solution)/shard_map/ppermute | solution.py:259
  24.1 2.1 %collective-permute-start.13 = (bf16[64,1408]{1,0:T(8,128)(2,1)S(1)}, bf16[64,1408]{1,0:T(8,128)(2,1)S(1)}, u32[]{:S(2)}, u32[]{:S(2)}) collective-permute-start(bf16[64,1408]{1,0:T(8,128)(2,1)S(1)} %collective-permute-done.11.refs_3_), channel_id=1, source_target_pairs={{0,4},{1,5},{4,8},{5,9},{8,12},{9,13},{12,14},{13,15},{14,10},{15,... | collective-permute-start | bytes 540680 | tf_op jit(solution)/shard_map/ppermute | solution.py:259
  26.2 5.1 %collective-permute-done.13.refs_5_ = bf16[64,1408]{1,0:T(8,128)(2,1)S(1)} collective-permute-done((bf16[64,1408]{1,0:T(8,128)(2,1)S(1)}, bf16[64,1408]{1,0:T(8,128)(2,1)S(1)}, u32[]{:S(2)}, u32[]{:S(2)}) %collective-permute-start.13) | collective-permute-done | bytes 180256 | tf_op jit(solution)/shard_map/ppermute | solution.py:259
  31.3 1.5 %collective-permute-done.14.refs_6_ = bf16[64,1408]{1,0:T(8,128)(2,1)S(1)} collective-permute-done((bf16[64,1408]{1,0:T(8,128)(2,1)S(1)}, bf16[64,1408]{1,0:T(8,128)(2,1)S(1)}, u32[]{:S(2)}, u32[]{:S(2)}) %collective-permute-start.14) | collective-permute-done | bytes 180256 | tf_op jit(solution)/shard_map/ppermute | solution.py:259
  32.9 1.6 %collective-permute-start.6 = (bf16[32,1536]{1,0:T(8,128)(2,1)S(1)}, bf16[32,1536]{1,0:T(8,128)(2,1)S(1)}, u32[]{:S(2)}, u32[]{:S(2)}) collective-permute-start(bf16[32,1536]{1,0:T(8,128)(2,1)S(1)} %slice.52), channel_id=1, source_target_pairs={{0,4},{1,5},{4,8},{5,9},{8,12},{9,13},{12,14},{13,15},{14,10},{15,... | collective-permute-start | bytes 294920 | tf_op jit(solution)/shard_map/ppermute | solution.py:259
  35.0 1.6 %collective-permute-start.15 = (bf16[32,1408]{1,0:T(8,128)(2,1)S(1)}, bf16[32,1408]{1,0:T(8,128)(2,1)S(1)}, u32[]{:S(2)}, u32[]{:S(2)}) collective-permute-start(bf16[32,1408]{1,0:T(8,128)(2,1)S(1)} %slice.54), channel_id=1, source_target_pairs={{0,4},{1,5},{4,8},{5,9},{8,12},{9,13},{12,14},{13,15},{14,10},{15,... | collective-permute-start | bytes 270344 | tf_op jit(solution)/shard_map/ppermute | solution.py:259
  37.7 1.5 %collective-permute-done.7.refs_8_ = bf16[32,1536]{1,0:T(8,128)(2,1)S(1)} collective-permute-done((bf16[32,1536]{1,0:T(8,128)(2,1)S(1)}, bf16[32,1536]{1,0:T(8,128)(2,1)S(1)}, u32[]{:S(2)}, u32[]{:S(2)}) %collective-permute-start.7) | collective-permute-done | bytes 98336 | tf_op jit(solution)/shard_map/ppermute | solution.py:259
  39.2 2.0 %shard_map.83 = (bf16[144,1536]{1,0:T(8,128)(2,1)S(1)}, bf16[144,1536]{1,0:T(8,128)(2,1)S(1)}, bf16[288,512]{1,0:T(8,128)(2,1)S(1)}, bf16[512,288]{1,0:T(8,128)(2,1)S(1)}) custom-call(s32[1,2]{1,0:T(1,128)S(1)} %add_bitcast_fusion.experts_ref, bf16[64,1536]{1,0:T(8,128)(2,1)S(1)} %get-tuple-element.37.refs_0_, ...), custom_call_target="tpu_custom_call" | custom-call | flops 452984832 | bytes 1048576 | tf_op jit(solution)/shard_map/pallas_call | solution.py:298
  42.6 1.3 %collective-permute-done.17.mate_second = bf16[144,1408]{1,0:T(8,128)(2,1)S(1)} collective-permute-done((bf16[144,1408]{1,0:T(8,128)(2,1)S(1)}, bf16[144,1408]{1,0:T(8,128)(2,1)S(1)}, u32[]{:S(2)}, u32[]{:S(2)}) %collective-permute-start.17) | collective-permute-done | bytes 405536 | tf_op jit(solution)/shard_map/ppermute | solution.py:259
  45.7 26.6 %shard_map.85 = (bf16[144,1536]{1,0:T(8,128)(2,1)S(1)}, bf16[144,1536]{1,0:T(8,128)(2,1)S(1)}, bf16[144,1408]{1,0:T(8,128)(2,1)S(1)}, bf16[144,1408]{1,0:T(8,128)(2,1)S(1)}) custom-call(s32[1,2]{1,0:T(1,128)S(1)} %add_bitcast_fusion.experts_ref, bf16[144,1536]{1,0:T(8,128)(2,1)S(1)} %copy-done.8, bf16[144,1536]{1,0:T(8,128)(2,1)S(1)} %collective-permute-done.8.mate_first, ...), custom_call_target="tpu_custom_call" | custom-call | flops 14332723200 | bytes 49766400 | tf_op jit(solution)/shard_map/pallas_call | solution.py:323
  75.7 1.6 %collective-permute-start.28 = (bf16[32,1408]{1,0:T(8,128)(2,1)S(1)}, bf16[32,1408]{1,0:T(8,128)(2,1)S(1)}, u32[]{:S(2)}, u32[]{:S(2)}) collective-permute-start(bf16[32,1408]{1,0:T(8,128)(2,1)S(1)} %get-tuple-element.64), channel_id=1, source_target_pairs={{0,4},{1,5},{4,8},{5,9},{8,12},{9,13},{12,14},{13,15},{14,10},{15,... | collective-permute-start | bytes 270344 | tf_op jit(solution)/shard_map/ppermute | solution.py:259
  78.9 1.6 %collective-permute-start.19 = (bf16[32,1536]{1,0:T(8,128)(2,1)S(1)}, bf16[32,1536]{1,0:T(8,128)(2,1)S(1)}, u32[]{:S(2)}, u32[]{:S(2)}) collective-permute-start(bf16[32,1536]{1,0:T(8,128)(2,1)S(1)} %get-tuple-element.53), channel_id=1, source_target_pairs={{0,4},{1,5},{4,8},{5,9},{8,12},{9,13},{12,14},{13,15},{14,10},{15,... | collective-permute-start | bytes 294920 | tf_op jit(solution)/shard_map/ppermute | solution.py:259
  81.1 1.6 %collective-permute-start.29 = (bf16[64,1408]{1,0:T(8,128)(2,1)S(1)}, bf16[64,1408]{1,0:T(8,128)(2,1)S(1)}, u32[]{:S(2)}, u32[]{:S(2)}) collective-permute-start(bf16[64,1408]{1,0:T(8,128)(2,1)S(1)} %pad_maximum_fusion.3), channel_id=1, source_target_pairs={{0,4},{1,5},{4,8},{5,9},{8,12},{9,13},{12,14},{13,15},{14,10},{15,... | collective-permute-start | bytes 540680 | tf_op jit(solution)/shard_map/ppermute | solution.py:259
  84.4 1.6 %collective-permute-start.20 = (bf16[64,1536]{1,0:T(8,128)(2,1)S(1)}, bf16[64,1536]{1,0:T(8,128)(2,1)S(1)}, u32[]{:S(2)}, u32[]{:S(2)}) collective-permute-start(bf16[64,1536]{1,0:T(8,128)(2,1)S(1)} %pad_maximum_fusion.1), channel_id=1, source_target_pairs={{0,4},{1,5},{4,8},{5,9},{8,12},{9,13},{12,14},{13,15},{14,10},{15,... | collective-permute-start | bytes 589832 | tf_op jit(solution)/shard_map/ppermute | solution.py:259
  86.0 2.1 %collective-permute-done.33 = bf16[64,1408]{1,0:T(8,128)(2,1)S(1)} collective-permute-done((bf16[64,1408]{1,0:T(8,128)(2,1)S(1)}, bf16[64,1408]{1,0:T(8,128)(2,1)S(1)}, u32[]{:S(2)}, u32[]{:S(2)}) %collective-permute-start.33) | collective-permute-done | bytes 180256 | tf_op jit(solution)/shard_map/ppermute | solution.py:259
  88.7 1.6 %collective-permute-start.30 = (bf16[64,1408]{1,0:T(8,128)(2,1)S(1)}, bf16[64,1408]{1,0:T(8,128)(2,1)S(1)}, u32[]{:S(2)}, u32[]{:S(2)}) collective-permute-start(bf16[64,1408]{1,0:T(8,128)(2,1)S(1)} %add_convert_fusion.7), channel_id=1, source_target_pairs={{0,4},{1,5},{4,8},{5,9},{8,12},{9,13},{12,14},{13,15},{14,10},{15,... | collective-permute-start | bytes 540680 | tf_op jit(solution)/shard_map/ppermute | solution.py:259
  90.3 2.0 %collective-permute-done.24 = bf16[64,1536]{1,0:T(8,128)(2,1)S(1)} collective-permute-done((bf16[64,1536]{1,0:T(8,128)(2,1)S(1)}, bf16[64,1536]{1,0:T(8,128)(2,1)S(1)}, u32[]{:S(2)}, u32[]{:S(2)}) %collective-permute-start.24) | collective-permute-done | bytes 196640 | tf_op jit(solution)/shard_map/ppermute | solution.py:259
  92.9 1.6 %collective-permute-start.21 = (bf16[64,1536]{1,0:T(8,128)(2,1)S(1)}, bf16[64,1536]{1,0:T(8,128)(2,1)S(1)}, u32[]{:S(2)}, u32[]{:S(2)}) collective-permute-start(bf16[64,1536]{1,0:T(8,128)(2,1)S(1)} %add_convert_fusion.3), channel_id=1, source_target_pairs={{0,4},{1,5},{4,8},{5,9},{8,12},{9,13},{12,14},{13,15},{14,10},{15,... | collective-permute-start | bytes 589832 | tf_op jit(solution)/shard_map/ppermute | solution.py:259
  94.6 1.6 %collective-permute-done.34 = bf16[64,1408]{1,0:T(8,128)(2,1)S(1)} collective-permute-done((bf16[64,1408]{1,0:T(8,128)(2,1)S(1)}, bf16[64,1408]{1,0:T(8,128)(2,1)S(1)}, u32[]{:S(2)}, u32[]{:S(2)}) %collective-permute-start.34) | collective-permute-done | bytes 180256 | tf_op jit(solution)/shard_map/ppermute | solution.py:259
  96.8 1.6 %collective-permute-start.31 = (bf16[64,1408]{1,0:T(8,128)(2,1)S(1)}, bf16[64,1408]{1,0:T(8,128)(2,1)S(1)}, u32[]{:S(2)}, u32[]{:S(2)}) collective-permute-start(bf16[64,1408]{1,0:T(8,128)(2,1)S(1)} %add_convert_fusion.6), channel_id=1, source_target_pairs={{0,4},{1,5},{4,8},{5,9},{8,12},{9,13},{12,14},{13,15},{14,10},{15,... | collective-permute-start | bytes 540680 | tf_op jit(solution)/shard_map/ppermute | solution.py:259
  98.4 2.0 %collective-permute-done.25 = bf16[64,1536]{1,0:T(8,128)(2,1)S(1)} collective-permute-done((bf16[64,1536]{1,0:T(8,128)(2,1)S(1)}, bf16[64,1536]{1,0:T(8,128)(2,1)S(1)}, u32[]{:S(2)}, u32[]{:S(2)}) %collective-permute-start.25) | collective-permute-done | bytes 196640 | tf_op jit(solution)/shard_map/ppermute | solution.py:259
  101.0 1.6 %collective-permute-start.22 = (bf16[64,1536]{1,0:T(8,128)(2,1)S(1)}, bf16[64,1536]{1,0:T(8,128)(2,1)S(1)}, u32[]{:S(2)}, u32[]{:S(2)}) collective-permute-start(bf16[64,1536]{1,0:T(8,128)(2,1)S(1)} %add_convert_fusion.2), channel_id=1, source_target_pairs={{0,4},{1,5},{4,8},{5,9},{8,12},{9,13},{12,14},{13,15},{14,10},{15,... | collective-permute-start | bytes 589832 | tf_op jit(solution)/shard_map/ppermute | solution.py:259
  102.6 1.6 %collective-permute-done.35 = bf16[64,1408]{1,0:T(8,128)(2,1)S(1)} collective-permute-done((bf16[64,1408]{1,0:T(8,128)(2,1)S(1)}, bf16[64,1408]{1,0:T(8,128)(2,1)S(1)}, u32[]{:S(2)}, u32[]{:S(2)}) %collective-permute-start.35) | collective-permute-done | bytes 180256 | tf_op jit(solution)/shard_map/ppermute | solution.py:259
  104.9 2.4 %collective-permute-done.26 = bf16[64,1536]{1,0:T(8,128)(2,1)S(1)} collective-permute-done((bf16[64,1536]{1,0:T(8,128)(2,1)S(1)}, bf16[64,1536]{1,0:T(8,128)(2,1)S(1)}, u32[]{:S(2)}, u32[]{:S(2)}) %collective-permute-start.26) | collective-permute-done | bytes 196640 | tf_op jit(solution)/shard_map/ppermute | solution.py:259
  (97 shorter events, 19.8 us)
Async XLA Ops:
  3.4 8.7 %collective-permute-start = (bf16[64,1536]{1,0:T(8,128)(2,1)S(1)}, bf16[64,1536]{1,0:T(8,128)(2,1)S(1)}, u32[]{:S(2)}, u32[]{:S(2)}) collective-permute-start(bf16[64,1536]{1,0:T(8,128)(2,1)S(1)} %get-tuple-element.37.refs_0_), channel_id=1, source_target_pairs={{0,4},{1,5},{4,8},{5,9},{8,12},{9,13},{12,14},{13,15},{14,10},{15,... | collective-permute-start | bytes 589832 | tf_op jit(solution)/shard_map/ppermute | solution.py:259
  6.5 7.8 %collective-permute-start.1 = (bf16[64,1536]{1,0:T(8,128)(2,1)S(1)}, bf16[64,1536]{1,0:T(8,128)(2,1)S(1)}, u32[]{:S(2)}, u32[]{:S(2)}) collective-permute-start(bf16[64,1536]{1,0:T(8,128)(2,1)S(1)} %get-tuple-element.37.refs_0_), channel_id=1, source_target_pairs={{4,0},{5,1},{8,4},{9,5},{12,8},{13,9},{14,12},{15,13},{10,14},{11,... | collective-permute-start | bytes 589832 | tf_op jit(solution)/shard_map/ppermute | solution.py:259
  6.5 9.5 %collective-permute-start.9 = (bf16[64,1408]{1,0:T(8,128)(2,1)S(1)}, bf16[64,1408]{1,0:T(8,128)(2,1)S(1)}, u32[]{:S(2)}, u32[]{:S(2)}) collective-permute-start(bf16[64,1408]{1,0:T(8,128)(2,1)S(1)} %get-tuple-element.42.refs_0_), channel_id=1, source_target_pairs={{0,4},{1,5},{4,8},{5,9},{8,12},{9,13},{12,14},{13,15},{14,10},{15,... | collective-permute-start | bytes 540680 | tf_op jit(solution)/shard_map/ppermute | solution.py:259
  8.5 9.7 %collective-permute-start.10 = (bf16[64,1408]{1,0:T(8,128)(2,1)S(1)}, bf16[64,1408]{1,0:T(8,128)(2,1)S(1)}, u32[]{:S(2)}, u32[]{:S(2)}) collective-permute-start(bf16[64,1408]{1,0:T(8,128)(2,1)S(1)} %get-tuple-element.42.refs_0_), channel_id=1, source_target_pairs={{4,0},{5,1},{8,4},{9,5},{12,8},{13,9},{14,12},{15,13},{10,14},{11,... | collective-permute-start | bytes 540680 | tf_op jit(solution)/shard_map/ppermute | solution.py:259
  12.1 8.1 %collective-permute-start.2 = (bf16[64,1536]{1,0:T(8,128)(2,1)S(1)}, bf16[64,1536]{1,0:T(8,128)(2,1)S(1)}, u32[]{:S(2)}, u32[]{:S(2)}) collective-permute-start(bf16[64,1536]{1,0:T(8,128)(2,1)S(1)} %collective-permute-done.refs_1_), channel_id=1, source_target_pairs={{0,4},{1,5},{4,8},{5,9},{8,12},{9,13},{12,14},{13,15},{14,10},{15,... | collective-permute-start | bytes 589832 | tf_op jit(solution)/shard_map/ppermute | solution.py:259
  14.3 8.1 %collective-permute-start.3 = (bf16[64,1536]{1,0:T(8,128)(2,1)S(1)}, bf16[64,1536]{1,0:T(8,128)(2,1)S(1)}, u32[]{:S(2)}, u32[]{:S(2)}) collective-permute-start(bf16[64,1536]{1,0:T(8,128)(2,1)S(1)} %collective-permute-done.1.refs_2_), channel_id=1, source_target_pairs={{4,0},{5,1},{8,4},{9,5},{12,8},{13,9},{14,12},{15,13},{10,14},{11,... | collective-permute-start | bytes 589832 | tf_op jit(solution)/shard_map/ppermute | solution.py:259
  16.0 8.1 %collective-permute-start.11 = (bf16[64,1408]{1,0:T(8,128)(2,1)S(1)}, bf16[64,1408]{1,0:T(8,128)(2,1)S(1)}, u32[]{:S(2)}, u32[]{:S(2)}) collective-permute-start(bf16[64,1408]{1,0:T(8,128)(2,1)S(1)} %collective-permute-done.9.refs_1_), channel_id=1, source_target_pairs={{0,4},{1,5},{4,8},{5,9},{8,12},{9,13},{12,14},{13,15},{14,10},{15,... | collective-permute-start | bytes 540680 | tf_op jit(solution)/shard_map/ppermute | solution.py:259
  18.2 8.1 %collective-permute-start.12 = (bf16[64,1408]{1,0:T(8,128)(2,1)S(1)}, bf16[64,1408]{1,0:T(8,128)(2,1)S(1)}, u32[]{:S(2)}, u32[]{:S(2)}) collective-permute-start(bf16[64,1408]{1,0:T(8,128)(2,1)S(1)} %collective-permute-done.10.refs_2_), channel_id=1, source_target_pairs={{4,0},{5,1},{8,4},{9,5},{12,8},{13,9},{14,12},{15,13},{10,14},{11,... | collective-permute-start | bytes 540680 | tf_op jit(solution)/shard_map/ppermute | solution.py:259
  20.2 12.7 %collective-permute-start.4 = (bf16[64,1536]{1,0:T(8,128)(2,1)S(1)}, bf16[64,1536]{1,0:T(8,128)(2,1)S(1)}, u32[]{:S(2)}, u32[]{:S(2)}) collective-permute-start(bf16[64,1536]{1,0:T(8,128)(2,1)S(1)} %collective-permute-done.2.refs_3_), channel_id=1, source_target_pairs={{0,4},{1,5},{4,8},{5,9},{8,12},{9,13},{12,14},{13,15},{14,10},{15,... | collective-permute-start | bytes 589832 | tf_op jit(solution)/shard_map/ppermute | solution.py:259
  22.4 12.1 %collective-permute-start.5 = (bf16[64,1536]{1,0:T(8,128)(2,1)S(1)}, bf16[64,1536]{1,0:T(8,128)(2,1)S(1)}, u32[]{:S(2)}, u32[]{:S(2)}) collective-permute-start(bf16[64,1536]{1,0:T(8,128)(2,1)S(1)} %collective-permute-done.3.refs_4_), channel_id=1, source_target_pairs={{4,0},{5,1},{8,4},{9,5},{12,8},{13,9},{14,12},{15,13},{10,14},{11,... | collective-permute-start | bytes 589832 | tf_op jit(solution)/shard_map/ppermute | solution.py:259
  24.1 7.2 %collective-permute-start.13 = (bf16[64,1408]{1,0:T(8,128)(2,1)S(1)}, bf16[64,1408]{1,0:T(8,128)(2,1)S(1)}, u32[]{:S(2)}, u32[]{:S(2)}) collective-permute-start(bf16[64,1408]{1,0:T(8,128)(2,1)S(1)} %collective-permute-done.11.refs_3_), channel_id=1, source_target_pairs={{0,4},{1,5},{4,8},{5,9},{8,12},{9,13},{12,14},{13,15},{14,10},{15,... | collective-permute-start | bytes 540680 | tf_op jit(solution)/shard_map/ppermute | solution.py:259
  26.2 6.6 %collective-permute-start.14 = (bf16[64,1408]{1,0:T(8,128)(2,1)S(1)}, bf16[64,1408]{1,0:T(8,128)(2,1)S(1)}, u32[]{:S(2)}, u32[]{:S(2)}) collective-permute-start(bf16[64,1408]{1,0:T(8,128)(2,1)S(1)} %collective-permute-done.12.refs_4_), channel_id=1, source_target_pairs={{4,0},{5,1},{8,4},{9,5},{12,8},{13,9},{14,12},{15,13},{10,14},{11,... | collective-permute-start | bytes 540680 | tf_op jit(solution)/shard_map/ppermute | solution.py:259
  32.9 4.8 %collective-permute-start.6 = (bf16[32,1536]{1,0:T(8,128)(2,1)S(1)}, bf16[32,1536]{1,0:T(8,128)(2,1)S(1)}, u32[]{:S(2)}, u32[]{:S(2)}) collective-permute-start(bf16[32,1536]{1,0:T(8,128)(2,1)S(1)} %slice.52), channel_id=1, source_target_pairs={{0,4},{1,5},{4,8},{5,9},{8,12},{9,13},{12,14},{13,15},{14,10},{15,... | collective-permute-start | bytes 294920 | tf_op jit(solution)/shard_map/ppermute | solution.py:259
  34.5 4.7 %collective-permute-start.7 = (bf16[32,1536]{1,0:T(8,128)(2,1)S(1)}, bf16[32,1536]{1,0:T(8,128)(2,1)S(1)}, u32[]{:S(2)}, u32[]{:S(2)}) collective-permute-start(bf16[32,1536]{1,0:T(8,128)(2,1)S(1)} %slice.53), channel_id=1, source_target_pairs={{4,0},{5,1},{8,4},{9,5},{12,8},{13,9},{14,12},{15,13},{10,14},{11,... | collective-permute-start | bytes 294920 | tf_op jit(solution)/shard_map/ppermute | solution.py:259
  35.0 6.3 %collective-permute-start.15 = (bf16[32,1408]{1,0:T(8,128)(2,1)S(1)}, bf16[32,1408]{1,0:T(8,128)(2,1)S(1)}, u32[]{:S(2)}, u32[]{:S(2)}) collective-permute-start(bf16[32,1408]{1,0:T(8,128)(2,1)S(1)} %slice.54), channel_id=1, source_target_pairs={{0,4},{1,5},{4,8},{5,9},{8,12},{9,13},{12,14},{13,15},{14,10},{15,... | collective-permute-start | bytes 270344 | tf_op jit(solution)/shard_map/ppermute | solution.py:259
  36.6 4.8 %collective-permute-start.16 = (bf16[32,1408]{1,0:T(8,128)(2,1)S(1)}, bf16[32,1408]{1,0:T(8,128)(2,1)S(1)}, u32[]{:S(2)}, u32[]{:S(2)}) collective-permute-start(bf16[32,1408]{1,0:T(8,128)(2,1)S(1)} %slice.55), channel_id=1, source_target_pairs={{4,0},{5,1},{8,4},{9,5},{12,8},{13,9},{14,12},{15,13},{10,14},{11,... | collective-permute-start | bytes 270344 | tf_op jit(solution)/shard_map/ppermute | solution.py:259
  75.1 5.4 %collective-permute-start.32 = (bf16[32,1408]{1,0:T(8,128)(2,1)S(1)}, bf16[32,1408]{1,0:T(8,128)(2,1)S(1)}, u32[]{:S(2)}, u32[]{:S(2)}) collective-permute-start(bf16[32,1408]{1,0:T(8,128)(2,1)S(1)} %get-tuple-element.68), channel_id=1, source_target_pairs={{4,0},{5,1},{8,4},{9,5},{12,8},{13,9},{14,12},{15,13},{10,14},{11,... | collective-permute-start | bytes 270344 | tf_op jit(solution)/shard_map/ppermute | solution.py:259
  75.7 5.4 %collective-permute-start.28 = (bf16[32,1408]{1,0:T(8,128)(2,1)S(1)}, bf16[32,1408]{1,0:T(8,128)(2,1)S(1)}, u32[]{:S(2)}, u32[]{:S(2)}) collective-permute-start(bf16[32,1408]{1,0:T(8,128)(2,1)S(1)} %get-tuple-element.64), channel_id=1, source_target_pairs={{0,4},{1,5},{4,8},{5,9},{8,12},{9,13},{12,14},{13,15},{14,10},{15,... | collective-permute-start | bytes 270344 | tf_op jit(solution)/shard_map/ppermute | solution.py:259
  78.4 5.3 %collective-permute-start.23 = (bf16[32,1536]{1,0:T(8,128)(2,1)S(1)}, bf16[32,1536]{1,0:T(8,128)(2,1)S(1)}, u32[]{:S(2)}, u32[]{:S(2)}) collective-permute-start(bf16[32,1536]{1,0:T(8,128)(2,1)S(1)} %get-tuple-element.57), channel_id=1, source_target_pairs={{4,0},{5,1},{8,4},{9,5},{12,8},{13,9},{14,12},{15,13},{10,14},{11,... | collective-permute-start | bytes 294920 | tf_op jit(solution)/shard_map/ppermute | solution.py:259
  78.9 5.5 %collective-permute-start.19 = (bf16[32,1536]{1,0:T(8,128)(2,1)S(1)}, bf16[32,1536]{1,0:T(8,128)(2,1)S(1)}, u32[]{:S(2)}, u32[]{:S(2)}) collective-permute-start(bf16[32,1536]{1,0:T(8,128)(2,1)S(1)} %get-tuple-element.53), channel_id=1, source_target_pairs={{0,4},{1,5},{4,8},{5,9},{8,12},{9,13},{12,14},{13,15},{14,10},{15,... | collective-permute-start | bytes 294920 | tf_op jit(solution)/shard_map/ppermute | solution.py:259
  80.6 7.5 %collective-permute-start.33 = (bf16[64,1408]{1,0:T(8,128)(2,1)S(1)}, bf16[64,1408]{1,0:T(8,128)(2,1)S(1)}, u32[]{:S(2)}, u32[]{:S(2)}) collective-permute-start(bf16[64,1408]{1,0:T(8,128)(2,1)S(1)} %pad_maximum_fusion.4), channel_id=1, source_target_pairs={{4,0},{5,1},{8,4},{9,5},{12,8},{13,9},{14,12},{15,13},{10,14},{11,... | collective-permute-start | bytes 540680 | tf_op jit(solution)/shard_map/ppermute | solution.py:259
  81.1 7.5 %collective-permute-start.29 = (bf16[64,1408]{1,0:T(8,128)(2,1)S(1)}, bf16[64,1408]{1,0:T(8,128)(2,1)S(1)}, u32[]{:S(2)}, u32[]{:S(2)}) collective-permute-start(bf16[64,1408]{1,0:T(8,128)(2,1)S(1)} %pad_maximum_fusion.3), channel_id=1, source_target_pairs={{0,4},{1,5},{4,8},{5,9},{8,12},{9,13},{12,14},{13,15},{14,10},{15,... | collective-permute-start | bytes 540680 | tf_op jit(solution)/shard_map/ppermute | solution.py:259
  83.7 8.6 %collective-permute-start.24 = (bf16[64,1536]{1,0:T(8,128)(2,1)S(1)}, bf16[64,1536]{1,0:T(8,128)(2,1)S(1)}, u32[]{:S(2)}, u32[]{:S(2)}) collective-permute-start(bf16[64,1536]{1,0:T(8,128)(2,1)S(1)} %pad_maximum_fusion.2), channel_id=1, source_target_pairs={{4,0},{5,1},{8,4},{9,5},{12,8},{13,9},{14,12},{15,13},{10,14},{11,... | collective-permute-start | bytes 589832 | tf_op jit(solution)/shard_map/ppermute | solution.py:259
  84.4 8.5 %collective-permute-start.20 = (bf16[64,1536]{1,0:T(8,128)(2,1)S(1)}, bf16[64,1536]{1,0:T(8,128)(2,1)S(1)}, u32[]{:S(2)}, u32[]{:S(2)}) collective-permute-start(bf16[64,1536]{1,0:T(8,128)(2,1)S(1)} %pad_maximum_fusion.1), channel_id=1, source_target_pairs={{0,4},{1,5},{4,8},{5,9},{8,12},{9,13},{12,14},{13,15},{14,10},{15,... | collective-permute-start | bytes 589832 | tf_op jit(solution)/shard_map/ppermute | solution.py:259
  88.1 8.0 %collective-permute-start.34 = (bf16[64,1408]{1,0:T(8,128)(2,1)S(1)}, bf16[64,1408]{1,0:T(8,128)(2,1)S(1)}, u32[]{:S(2)}, u32[]{:S(2)}) collective-permute-start(bf16[64,1408]{1,0:T(8,128)(2,1)S(1)} %add_convert_fusion.5), channel_id=1, source_target_pairs={{4,0},{5,1},{8,4},{9,5},{12,8},{13,9},{14,12},{15,13},{10,14},{11,... | collective-permute-start | bytes 540680 | tf_op jit(solution)/shard_map/ppermute | solution.py:259
  88.7 8.0 %collective-permute-start.30 = (bf16[64,1408]{1,0:T(8,128)(2,1)S(1)}, bf16[64,1408]{1,0:T(8,128)(2,1)S(1)}, u32[]{:S(2)}, u32[]{:S(2)}) collective-permute-start(bf16[64,1408]{1,0:T(8,128)(2,1)S(1)} %add_convert_fusion.7), channel_id=1, source_target_pairs={{0,4},{1,5},{4,8},{5,9},{8,12},{9,13},{12,14},{13,15},{14,10},{15,... | collective-permute-start | bytes 540680 | tf_op jit(solution)/shard_map/ppermute | solution.py:259
  92.4 8.0 %collective-permute-start.25 = (bf16[64,1536]{1,0:T(8,128)(2,1)S(1)}, bf16[64,1536]{1,0:T(8,128)(2,1)S(1)}, u32[]{:S(2)}, u32[]{:S(2)}) collective-permute-start(bf16[64,1536]{1,0:T(8,128)(2,1)S(1)} %add_convert_fusion.1), channel_id=1, source_target_pairs={{4,0},{5,1},{8,4},{9,5},{12,8},{13,9},{14,12},{15,13},{10,14},{11,... | collective-permute-start | bytes 589832 | tf_op jit(solution)/shard_map/ppermute | solution.py:259
  92.9 8.0 %collective-permute-start.21 = (bf16[64,1536]{1,0:T(8,128)(2,1)S(1)}, bf16[64,1536]{1,0:T(8,128)(2,1)S(1)}, u32[]{:S(2)}, u32[]{:S(2)}) collective-permute-start(bf16[64,1536]{1,0:T(8,128)(2,1)S(1)} %add_convert_fusion.3), channel_id=1, source_target_pairs={{0,4},{1,5},{4,8},{5,9},{8,12},{9,13},{12,14},{13,15},{14,10},{15,... | collective-permute-start | bytes 589832 | tf_op jit(solution)/shard_map/ppermute | solution.py:259
  96.2 8.0 %collective-permute-start.35 = (bf16[64,1408]{1,0:T(8,128)(2,1)S(1)}, bf16[64,1408]{1,0:T(8,128)(2,1)S(1)}, u32[]{:S(2)}, u32[]{:S(2)}) collective-permute-start(bf16[64,1408]{1,0:T(8,128)(2,1)S(1)} %add_convert_fusion.4), channel_id=1, source_target_pairs={{4,0},{5,1},{8,4},{9,5},{12,8},{13,9},{14,12},{15,13},{10,14},{11,... | collective-permute-start | bytes 540680 | tf_op jit(solution)/shard_map/ppermute | solution.py:259
  96.8 8.0 %collective-permute-start.31 = (bf16[64,1408]{1,0:T(8,128)(2,1)S(1)}, bf16[64,1408]{1,0:T(8,128)(2,1)S(1)}, u32[]{:S(2)}, u32[]{:S(2)}) collective-permute-start(bf16[64,1408]{1,0:T(8,128)(2,1)S(1)} %add_convert_fusion.6), channel_id=1, source_target_pairs={{0,4},{1,5},{4,8},{5,9},{8,12},{9,13},{12,14},{13,15},{14,10},{15,... | collective-permute-start | bytes 540680 | tf_op jit(solution)/shard_map/ppermute | solution.py:259
  100.4 6.8 %collective-permute-start.26 = (bf16[64,1536]{1,0:T(8,128)(2,1)S(1)}, bf16[64,1536]{1,0:T(8,128)(2,1)S(1)}, u32[]{:S(2)}, u32[]{:S(2)}) collective-permute-start(bf16[64,1536]{1,0:T(8,128)(2,1)S(1)} %add_convert_fusion), channel_id=1, source_target_pairs={{4,0},{5,1},{8,4},{9,5},{12,8},{13,9},{14,12},{15,13},{10,14},{11,... | collective-permute-start | bytes 589832 | tf_op jit(solution)/shard_map/ppermute | solution.py:259
  101.0 6.8 %collective-permute-start.22 = (bf16[64,1536]{1,0:T(8,128)(2,1)S(1)}, bf16[64,1536]{1,0:T(8,128)(2,1)S(1)}, u32[]{:S(2)}, u32[]{:S(2)}) collective-permute-start(bf16[64,1536]{1,0:T(8,128)(2,1)S(1)} %add_convert_fusion.2), channel_id=1, source_target_pairs={{0,4},{1,5},{4,8},{5,9},{8,12},{9,13},{12,14},{13,15},{14,10},{15,... | collective-permute-start | bytes 589832 | tf_op jit(solution)/shard_map/ppermute | solution.py:259
  (15 other events, 154.2 us)
where the time goes:
time: 109 us
  starting transfers between devices  36 us (33%)
  waiting for transfers between devices  34.2 us (31%)
  Pallas kernels  31.6 us (29%)
  local copies, waits for them, and re-layouts  5.07 us (5%)
  other arithmetic  1.59 us (1%)
    ppermute x36, starting transfers between devices, ring_shards(): send = lambda value, pairs: lax.ppermute(value, 'ep', pairs)  36 us
    ppermute x36, waiting for transfers between devices, ring_shards(): send = lambda value, pairs: lax.ppermute(value, 'ep', pairs)  34.2 us
    pallas_call x1, Pallas kernels, ring_shards(): pl.pallas_call(functools.partial(expert_kernel, top, steps_in, spans), gr...  26.6 us
    unnamed x22, local copies, waits for them, and re-layouts  4.99 us
  transfers between devices with their start and end apart: 36, of which 20 were waited for; matrix products, arithmetic and copies ran while one was open for 1% of the time, Pallas kernels for 4%

commit v1 on v0

--- a/solution.py
+++ b/solution.py
@@ -12,9 +12,9 @@
 BLOCK = 768
 NORM_MIB = 16
 SMALL_MIB = 16
+PICK_MIB = 16
 EXPERT_MIB = 50
 COLUMNS = 1152
-LEAD = -1
 ACT_COLS = 256
 
 
@@ -135,12 +135,13 @@
     placer_out[...] = jnp.concatenate(placers, axis=1).astype(bf16)
 
 
-def pick_kernel(count, picker_ref, *refs):
+def pick_kernel(count, picker_ref, first_ref, *refs):
     own_out, mate_out, held = refs[count:]
     gather_rows(refs[:count], held)
     rows = jnp.dot(picker_ref[...], held[...], preferred_element_type=jnp.float32).astype(jnp.bfloat16)
-    slots = own_out.shape[0]
-    own_out[...] = rows[:slots]
+    slots, edge = first_ref.shape
+    own_out[:, :edge] = first_ref[...]
+    own_out[:, edge:] = rows[:slots]
     mate_out[...] = rows[slots:]
 
 
@@ -167,14 +168,15 @@
 
 
 def expert_kernel(
-    top, steps_in, spans, experts_ref, own_first, mate_first, own_second, mate_second, win_ref, bin_ref, wout_hbm,
-    bout_ref, own_a, mate_a, own_b, mate_b, rows_first, rows_second, pre, act, slot_weight, sems, *held,
+    top, steps_in, spans, experts_ref, own_rows, mate_first, mate_second, win_ref, bias_ref, wout_hbm,
+    own_a, mate_a, own_b, mate_b, rows_first, rows_second, pre, act, slot_weight, sems, *held,
 ):
     step = pl.program_id(0)
     f32, bf16 = jnp.float32, jnp.bfloat16
-    slots, hidden, block = own_first.shape[0], act.shape[1], win_ref.shape[2]
+    slots, hidden, block = mate_first.shape[0], act.shape[1], win_ref.shape[2]
     width = win_ref.shape[1]
-    cut = width - own_second.shape[1]
+    edge = mate_first.shape[1]
+    cut = width - mate_second.shape[1]
     early = max((steps_in - 1) * block - hidden, 0) // LANES * LANES
     copies = [
         pltpu.make_async_copy(wout_hbm.at[0, :, pl.ds(at, size)], ref, sems.at[i])
@@ -184,22 +186,24 @@
     @pl.when(step == 0)
     def _():
         expert = experts_ref[0, 0].astype(f32)
-        for i, (low, high) in enumerate(((own_first, own_second), (mate_first, mate_second))):
-            rows_first[i * slots : (i + 1) * slots] = low[...]
-            rows_second[i * slots : (i + 1) * slots] = high[...]
-            weight = slot_weights(low[:, cut:], top, expert)
+        rows_first[:slots] = own_rows[:, :edge]
+        rows_first[slots:] = mate_first[...]
+        rows_second[:slots] = own_rows[:, edge:]
+        rows_second[slots:] = mate_second[...]
+        for i in range(2):
+            weight = slot_weights(rows_first[i * slots : (i + 1) * slots, cut:], top, expert)
             slot_weight[i * slots : (i + 1) * slots] = jnp.broadcast_to(weight, (slots, LANES))
 
     for i, copy in enumerate(copies):
 
-        @pl.when(step == max(steps_in - len(copies) + i - LEAD, 0))
+        @pl.when(step == steps_in - (1 if i == 0 else 0))
         def _():
             copy.start()
 
     def first_layer(at):
         total = jnp.dot(rows_first[:, :cut], win_ref[0, :cut], preferred_element_type=f32)
         total += jnp.dot(rows_second[...], win_ref[0, cut:], preferred_element_type=f32)
-        pre[:, pl.ds(at, block)] = total + bin_ref[...]
+        pre[:, pl.ds(at, block)] = total + bias_ref[:, pl.ds(at, block)]
 
     @pl.when(step < steps_in - 1)
     def _():
@@ -215,10 +219,14 @@
         activate(pre, act, early, hidden)
         edge = own_a.shape[1]
         for copy, ref, (at, size) in zip(copies, held, spans):
-            copy.wait()
+            if at == 0:
+                copy.wait()
+            elif at == spans[1][0]:
+                for later in copies[1:]:
+                    later.wait()
             result = jnp.dot(act[:, :early], ref[:early], preferred_element_type=f32)
             result += jnp.dot(act[:, early:], ref[early:], preferred_element_type=f32)
-            result = ((result + bout_ref[:, at : at + size]) * slot_weight[:, :1]).astype(bf16)
+            result = ((result + bias_ref[:, 2 * hidden + at : 2 * hidden + at + size]) * slot_weight[:, :1]).astype(bf16)
             inside = min(max(edge - at, 0), size)
             for row, low, high in ((0, own_a, own_b), (slots, mate_a, mate_b)):
                 if inside:
@@ -261,7 +269,6 @@
     row_count, width = tokens.shape
     top = expert_ids.shape[1]
     hidden = weight_out.shape[1]
-    half = row_count // 2
     lanes = [2 * BLOCK, width + -width % LANES - 2 * BLOCK]
     cut = width - lanes[1]
     slots, all_rows = chips * CAP, chips * row_count
@@ -278,23 +285,20 @@
     )(tokens, expert_ids.T, gate_ints.T, norm_gain)
     me = lax.axis_index("ep").astype(jnp.int32)
     experts = jnp.stack([me, me ^ 1]).reshape(1, 2)
-    bias_row = lax.dynamic_slice_in_dim(bias_out, me, 1, axis=0)
+    biases = jnp.concatenate([bias_in, lax.dynamic_slice_in_dim(bias_out, me, 1, axis=0)], axis=1)
 
     held = [[chain] for chain in chains]
-    going = [(chain, chain) for chain in chains]
+    going = [[chain, chain] for chain in chains]
     for hop in range(1, reach + 1):
         for c in range(len(chains)):
-            to_right, to_left = going[c]
-            if hop == reach:
-                to_right, to_left = to_right[:half], to_left[half:]
-                if c:
-                    to_right, to_left, _ = lax.optimization_barrier((to_right, to_left, waited))
-                waited = going[c]
-            going[c] = send(to_right, right), send(to_left, left)
-            held[c] += going[c]
+            for way, pairs in enumerate((right, left)):
+                if hop < reach or way == c:
+                    going[c][way] = send(going[c][way], pairs)
+                    held[c].append(going[c][way])
     order = [0]
     for hop in range(1, reach):
         order += [-hop, hop]
+    order.append(reach)
     own_first, mate_first, picker, placer = pl.pallas_call(
         functools.partial(route_kernel, top, cut, len(held[0])),
         in_specs=[smem] + [vmem] * len(held[0]),
@@ -302,18 +306,18 @@
         out_shape=[shape(slots, lanes[0])] * 2 + [shape(2 * slots, all_rows), shape(all_rows, 2 * slots)],
         scratch_shapes=[pltpu.VMEM((all_rows, lanes[0]), bf16)],
         cost_estimate=cost(2 * slots * all_rows * lanes[0], 2**20),
-        compiler_params=params(SMALL_MIB),
+        compiler_params=params(PICK_MIB),
     )(experts, *held[0])
     mate_first = send(mate_first, mate)
-    own_second, mate_second = pl.pallas_call(
+    own_rows, mate_second = pl.pallas_call(
         functools.partial(pick_kernel, len(held[1])),
-        in_specs=[vmem] * (1 + len(held[1])),
+        in_specs=[vmem] * (2 + len(held[1])),
         out_specs=[vmem] * 2,
-        out_shape=[shape(slots, lanes[1])] * 2,
+        out_shape=[shape(slots, sum(lanes)), shape(slots, lanes[1])],
         scratch_shapes=[pltpu.VMEM((all_rows, lanes[1]), bf16)],
         cost_estimate=cost(2 * slots * all_rows * lanes[1], 2**20),
-        compiler_params=params(SMALL_MIB),
-    )(picker, *held[1])
+        compiler_params=params(PICK_MIB),
+    )(picker, own_first, *held[1])
     mate_second = send(mate_second, mate)
 
     steps_in = pl.cdiv(2 * hidden, COLUMNS)
@@ -324,11 +328,10 @@
         functools.partial(expert_kernel, top, steps_in, spans),
         grid=(steps_in + 1,),
         in_specs=[
-            smem, whole(slots, lanes[0]), whole(slots, lanes[0]), whole(slots, lanes[1]), whole(slots, lanes[1]),
+            smem, whole(slots, sum(lanes)), whole(slots, lanes[0]), whole(slots, lanes[1]),
             pl.BlockSpec((1, width, COLUMNS), lambda j: (0, 0, first(j))),
-            pl.BlockSpec((1, COLUMNS), lambda j: (0, first(j))),
+            whole(1, 2 * hidden + width),
             pl.BlockSpec(memory_space=pl.ANY),
-            whole(1, width),
         ],
         out_specs=[whole(slots, w) for w in (lanes[0], lanes[0], lanes[1], lanes[1])],
         out_shape=[shape(slots, w) for w in (lanes[0], lanes[0], lanes[1], lanes[1])],
@@ -343,34 +346,28 @@
         + [pltpu.VMEM((hidden, size), bf16) for _, size in spans],
         cost_estimate=cost(2 * slots * width * 3 * hidden, 6 * width * hidden),
         compiler_params=params(EXPERT_MIB),
-    )(experts, own_first, mate_first, own_second, mate_second, weight_in, bias_in, weight_out, bias_row)
-
-    heights = [row_count] * (chips - 1) + [half, half]
+    )(experts, own_rows, mate_first, mate_second, weight_in, biases, weight_out)
+
     add = lambda a, b: (a.astype(f32) + b.astype(f32)).astype(bf16)
-
-    def spread(own, other):
+    owed = []
+    for own, other in ((own_a, mate_a), (own_b, mate_b)):
         sums = pl.pallas_call(
             spread_kernel,
             in_specs=[vmem] * 3,
-            out_specs=[vmem] * len(heights),
-            out_shape=[shape(rows, own.shape[1]) for rows in heights],
+            out_specs=[vmem] * chips,
+            out_shape=[shape(row_count, own.shape[1])] * chips,
             cost_estimate=cost(2 * slots * all_rows * own.shape[1], 2**20),
             compiler_params=params(SMALL_MIB),
         )(placer, own, send(other, mate))
-        return dict(zip(order + ["right", "left"], sums))
-
-    owed = [spread(own_a, mate_a), spread(own_b, mate_b)]
-    going = [(o["right"], o["left"]) for o in owed]
-    for hop in range(reach - 1, -1, -1):
+        owed.append(dict(zip(order, sums)))
+    going = [[None, None] for _ in owed]
+    for hop in range(reach, 0, -1):
         for c in range(len(owed)):
-            up, down = send(going[c][0], right), send(going[c][1], left)
-            if hop == reach - 1:
-                ahead, behind = owed[c][hop], owed[c][-hop]
-                up = jnp.concatenate([add(ahead[:half], up), ahead[half:]], axis=0)
-                down = jnp.concatenate([behind[:half], add(behind[half:], down)], axis=0)
-            elif hop:
-                up, down = add(owed[c][hop], up), add(owed[c][-hop], down)
-            going[c] = up, down
+            for way, pairs in enumerate((right, left)):
+                if hop < reach or way == c:
+                    mine = owed[c][hop if way == 0 or hop == reach else -hop]
+                    passed = mine if going[c][way] is None else add(mine, going[c][way])
+                    going[c][way] = send(passed, pairs)
     moe = [o[0].astype(f32) + up.astype(f32) + down.astype(f32) for o, (up, down) in zip(owed, going)]
     return (tokens.astype(f32) + jnp.concatenate(moe, axis=1)[:, :width]).astype(bf16)
 

time: 109 us -> 106 us (0.972)
  starting transfers between devices: 36 us -> 32.8 us
  waiting for transfers between devices: 34.2 us -> 37.4 us
  local copies, waits for them, and re-layouts: 5.07 us -> 3.12 us
  Pallas kernels: 31.6 us -> 29.8 us
    ppermute x36 -> x32, waiting for transfers between devices: 34.2 us -> 37.4 us  [ring_shards(): send = lambda value, pairs: lax.ppermute(value, 'ep', pairs)]
    ppermute x36 -> x32, starting transfers between devices: 36 us -> 32.8 us  [ring_shards(): send = lambda value, pairs: lax.ppermute(value, 'ep', pairs)]
    unnamed x22 -> x12, local copies, waits for them, and re-layouts: 4.99 us -> 3.11 us
    pallas_call x1, Pallas kernels: 26.6 us -> 24.8 us  [ring_shards(): pl.pallas_call(functools.partial(expert_kernel, top, steps_in, spans), gr...]
  transfers between devices with their start and end apart: 36 -> 32, of which waited for: 20 -> 18; matrix products, arithmetic and copies ran while one was open for 1% -> 1% of each run, Pallas kernels for 4% -> 4%
where the time goes in v1:
time: 106 us
  waiting for transfers between devices  37.4 us (35%)
  starting transfers between devices  32.8 us (31%)
  Pallas kernels  29.8 us (28%)
  local copies, waits for them, and re-layouts  3.12 us (3%)
  other arithmetic  2.3 us (2%)
    ppermute x32, waiting for transfers between devices, ring_shards(): send = lambda value, pairs: lax.ppermute(value, 'ep', pairs)  37.4 us
    ppermute x32, starting transfers between devices, ring_shards(): send = lambda value, pairs: lax.ppermute(value, 'ep', pairs)  32.8 us
    pallas_call x1, Pallas kernels, ring_shards(): pl.pallas_call(functools.partial(expert_kernel, top, steps_in, spans), gr...  24.8 us
    unnamed x12, local copies, waits for them, and re-layouts  3.11 us
  transfers between devices with their start and end apart: 32, of which 18 were waited for; matrix products, arithmetic and copies ran while one was open for 1% of the time, Pallas kernels for 4%

profile of v1, /device:TPU:0, one launch (start us, length us, event | category | flops | bytes accessed | tf_op | source)
XLA Modules:
  0.0 105.6 jit_solution(9862812172103098541)
XLA Ops:
  3.4 3.1 %collective-permute-start = (bf16[64,1536]{1,0:T(8,128)(2,1)S(1)}, bf16[64,1536]{1,0:T(8,128)(2,1)S(1)}, u32[]{:S(2)}, u32[]{:S(2)}) collective-permute-start(bf16[64,1536]{1,0:T(8,128)(2,1)S(1)} %get-tuple-element.33.refs_0_), channel_id=1, source_target_pairs={{0,4},{1,5},{4,8},{5,9},{8,12},{9,13},{12,14},{13,15},{14,10},{15,... | collective-permute-start | bytes 589832 | tf_op jit(solution)/shard_map/ppermute | solution.py:267
  6.5 1.9 %collective-permute-start.1 = (bf16[64,1536]{1,0:T(8,128)(2,1)S(1)}, bf16[64,1536]{1,0:T(8,128)(2,1)S(1)}, u32[]{:S(2)}, u32[]{:S(2)}) collective-permute-start(bf16[64,1536]{1,0:T(8,128)(2,1)S(1)} %get-tuple-element.33.refs_0_), channel_id=1, source_target_pairs={{4,0},{5,1},{8,4},{9,5},{12,8},{13,9},{14,12},{15,13},{10,14},{11,... | collective-permute-start | bytes 589832 | tf_op jit(solution)/shard_map/ppermute | solution.py:267
  8.4 2.9 %collective-permute-done.refs_1_ = bf16[64,1536]{1,0:T(8,128)(2,1)S(1)} collective-permute-done((bf16[64,1536]{1,0:T(8,128)(2,1)S(1)}, bf16[64,1536]{1,0:T(8,128)(2,1)S(1)}, u32[]{:S(2)}, u32[]{:S(2)}) %collective-permute-start) | collective-permute-done | bytes 196640 | tf_op jit(solution)/shard_map/ppermute | solution.py:267
  11.3 1.8 %collective-permute-start.2 = (bf16[64,1536]{1,0:T(8,128)(2,1)S(1)}, bf16[64,1536]{1,0:T(8,128)(2,1)S(1)}, u32[]{:S(2)}, u32[]{:S(2)}) collective-permute-start(bf16[64,1536]{1,0:T(8,128)(2,1)S(1)} %collective-permute-done.refs_1_), channel_id=1, source_target_pairs={{0,4},{1,5},{4,8},{5,9},{8,12},{9,13},{12,14},{13,15},{14,10},{15,... | collective-permute-start | bytes 589832 | tf_op jit(solution)/shard_map/ppermute | solution.py:267
  13.1 1.6 %collective-permute-start.7 = (bf16[64,1408]{1,0:T(8,128)(2,1)S(1)}, bf16[64,1408]{1,0:T(8,128)(2,1)S(1)}, u32[]{:S(2)}, u32[]{:S(2)}) collective-permute-start(bf16[64,1408]{1,0:T(8,128)(2,1)S(1)} %get-tuple-element.37.refs_0_), channel_id=1, source_target_pairs={{0,4},{1,5},{4,8},{5,9},{8,12},{9,13},{12,14},{13,15},{14,10},{15,... | collective-permute-start | bytes 540680 | tf_op jit(solution)/shard_map/ppermute | solution.py:267
  15.1 2.5 %collective-permute-done.1.refs_2_ = bf16[64,1536]{1,0:T(8,128)(2,1)S(1)} collective-permute-done((bf16[64,1536]{1,0:T(8,128)(2,1)S(1)}, bf16[64,1536]{1,0:T(8,128)(2,1)S(1)}, u32[]{:S(2)}, u32[]{:S(2)}) %collective-permute-start.1) | collective-permute-done | bytes 196640 | tf_op jit(solution)/shard_map/ppermute | solution.py:267
  17.7 1.4 %collective-permute-done.2.refs_3_ = bf16[64,1536]{1,0:T(8,128)(2,1)S(1)} collective-permute-done((bf16[64,1536]{1,0:T(8,128)(2,1)S(1)}, bf16[64,1536]{1,0:T(8,128)(2,1)S(1)}, u32[]{:S(2)}, u32[]{:S(2)}) %collective-permute-start.2) | collective-permute-done | bytes 196640 | tf_op jit(solution)/shard_map/ppermute | solution.py:267
  19.1 1.8 %collective-permute-start.4 = (bf16[64,1536]{1,0:T(8,128)(2,1)S(1)}, bf16[64,1536]{1,0:T(8,128)(2,1)S(1)}, u32[]{:S(2)}, u32[]{:S(2)}) collective-permute-start(bf16[64,1536]{1,0:T(8,128)(2,1)S(1)} %collective-permute-done.2.refs_3_), channel_id=1, source_target_pairs={{0,4},{1,5},{4,8},{5,9},{8,12},{9,13},{12,14},{13,15},{14,10},{15,... | collective-permute-start | bytes 589832 | tf_op jit(solution)/shard_map/ppermute | solution.py:267
  21.0 2.0 %collective-permute-done.7.refs_1_ = bf16[64,1408]{1,0:T(8,128)(2,1)S(1)} collective-permute-done((bf16[64,1408]{1,0:T(8,128)(2,1)S(1)}, bf16[64,1408]{1,0:T(8,128)(2,1)S(1)}, u32[]{:S(2)}, u32[]{:S(2)}) %collective-permute-start.7) | collective-permute-done | bytes 180256 | tf_op jit(solution)/shard_map/ppermute | solution.py:267
  23.0 1.8 %collective-permute-start.9 = (bf16[64,1408]{1,0:T(8,128)(2,1)S(1)}, bf16[64,1408]{1,0:T(8,128)(2,1)S(1)}, u32[]{:S(2)}, u32[]{:S(2)}) collective-permute-start(bf16[64,1408]{1,0:T(8,128)(2,1)S(1)} %collective-permute-done.7.refs_1_), channel_id=1, source_target_pairs={{0,4},{1,5},{4,8},{5,9},{8,12},{9,13},{12,14},{13,15},{14,10},{15,... | collective-permute-start | bytes 540680 | tf_op jit(solution)/shard_map/ppermute | solution.py:267
  25.0 4.3 %collective-permute-done.9.refs_3_ = bf16[64,1408]{1,0:T(8,128)(2,1)S(1)} collective-permute-done((bf16[64,1408]{1,0:T(8,128)(2,1)S(1)}, bf16[64,1408]{1,0:T(8,128)(2,1)S(1)}, u32[]{:S(2)}, u32[]{:S(2)}) %collective-permute-start.9) | collective-permute-done | bytes 180256 | tf_op jit(solution)/shard_map/ppermute | solution.py:267
  29.3 1.5 %collective-permute-start.11 = (bf16[64,1408]{1,0:T(8,128)(2,1)S(1)}, bf16[64,1408]{1,0:T(8,128)(2,1)S(1)}, u32[]{:S(2)}, u32[]{:S(2)}) collective-permute-start(bf16[64,1408]{1,0:T(8,128)(2,1)S(1)} %collective-permute-done.9.refs_3_), channel_id=1, source_target_pairs={{0,4},{1,5},{4,8},{5,9},{8,12},{9,13},{12,14},{13,15},{14,10},{15,... | collective-permute-start | bytes 540680 | tf_op jit(solution)/shard_map/ppermute | solution.py:267
  31.3 1.4 %collective-permute-start.13 = (bf16[64,1408]{1,0:T(8,128)(2,1)S(1)}, bf16[64,1408]{1,0:T(8,128)(2,1)S(1)}, u32[]{:S(2)}, u32[]{:S(2)}) collective-permute-start(bf16[64,1408]{1,0:T(8,128)(2,1)S(1)} %collective-permute-done.12.refs_6_), channel_id=1, source_target_pairs={{4,0},{5,1},{8,4},{9,5},{12,8},{13,9},{14,12},{15,13},{10,14},{11,... | collective-permute-start | bytes 540680 | tf_op jit(solution)/shard_map/ppermute | solution.py:267
  33.5 3.8 %collective-permute-done.5.refs_6_ = bf16[64,1536]{1,0:T(8,128)(2,1)S(1)} collective-permute-done((bf16[64,1536]{1,0:T(8,128)(2,1)S(1)}, bf16[64,1536]{1,0:T(8,128)(2,1)S(1)}, u32[]{:S(2)}, u32[]{:S(2)}) %collective-permute-start.5) | collective-permute-done | bytes 196640 | tf_op jit(solution)/shard_map/ppermute | solution.py:267
  37.3 1.4 %collective-permute-done.6.refs_7_ = bf16[64,1536]{1,0:T(8,128)(2,1)S(1)} collective-permute-done((bf16[64,1536]{1,0:T(8,128)(2,1)S(1)}, bf16[64,1536]{1,0:T(8,128)(2,1)S(1)}, u32[]{:S(2)}, u32[]{:S(2)}) %collective-permute-start.6) | collective-permute-done | bytes 196640 | tf_op jit(solution)/shard_map/ppermute | solution.py:267
  38.7 2.1 %shard_map.83 = (bf16[144,1536]{1,0:T(8,128)(2,1)S(1)}, bf16[144,1536]{1,0:T(8,128)(2,1)S(1)}, bf16[288,512]{1,0:T(8,128)(2,1)S(1)}, bf16[512,288]{1,0:T(8,128)(2,1)S(1)}) custom-call(s32[1,2]{1,0:T(1,128)S(1)} %add_bitcast_fusion.experts_ref, bf16[64,1536]{1,0:T(8,128)(2,1)S(1)} %get-tuple-element.33.refs_0_, ...), custom_call_target="tpu_custom_call" | custom-call | flops 452984832 | bytes 1048576 | tf_op jit(solution)/shard_map/pallas_call | solution.py:302
  43.9 24.8 %shard_map.85 = (bf16[144,1536]{1,0:T(8,128)(2,1)S(1)}, bf16[144,1536]{1,0:T(8,128)(2,1)S(1)}, bf16[144,1408]{1,0:T(8,128)(2,1)S(1)}, bf16[144,1408]{1,0:T(8,128)(2,1)S(1)}) custom-call(s32[1,2]{1,0:T(1,128)S(1)} %add_bitcast_fusion.experts_ref, bf16[144,2944]{1,0:T(8,128)(2,1)S(1)} %get-tuple-element.38.own_rows, ...), custom_call_target="tpu_custom_call" | custom-call | flops 14332723200 | bytes 49766400 | tf_op jit(solution)/shard_map/pallas_call | solution.py:327
  69.2 1.2 %collective-permute-done.24.mate_ref = bf16[144,1408]{1,0:T(8,128)(2,1)S(1)} collective-permute-done((bf16[144,1408]{1,0:T(8,128)(2,1)S(1)}, bf16[144,1408]{1,0:T(8,128)(2,1)S(1)}, u32[]{:S(2)}, u32[]{:S(2)}) %collective-permute-start.24) | collective-permute-done | bytes 405536 | tf_op jit(solution)/shard_map/ppermute | solution.py:267
  72.5 1.1 %collective-permute-start.28 = (bf16[64,1408]{1,0:T(8,128)(2,1)S(1)}, bf16[64,1408]{1,0:T(8,128)(2,1)S(1)}, u32[]{:S(2)}, u32[]{:S(2)}) collective-permute-start(bf16[64,1408]{1,0:T(8,128)(2,1)S(1)} %get-tuple-element.60), channel_id=1, source_target_pairs={{4,0},{5,1},{8,4},{9,5},{12,8},{13,9},{14,12},{15,13},{10,14},{11,... | collective-permute-start | bytes 540680 | tf_op jit(solution)/shard_map/ppermute | solution.py:267
  76.7 2.2 %collective-permute-done.25 = bf16[64,1408]{1,0:T(8,128)(2,1)S(1)} collective-permute-done((bf16[64,1408]{1,0:T(8,128)(2,1)S(1)}, bf16[64,1408]{1,0:T(8,128)(2,1)S(1)}, u32[]{:S(2)}, u32[]{:S(2)}) %collective-permute-start.25) | collective-permute-done | bytes 180256 | tf_op jit(solution)/shard_map/ppermute | solution.py:267
  80.0 1.2 %collective-permute-start.29 = (bf16[64,1408]{1,0:T(8,128)(2,1)S(1)}, bf16[64,1408]{1,0:T(8,128)(2,1)S(1)}, u32[]{:S(2)}, u32[]{:S(2)}) collective-permute-start(bf16[64,1408]{1,0:T(8,128)(2,1)S(1)} %add_convert_fusion.7), channel_id=1, source_target_pairs={{4,0},{5,1},{8,4},{9,5},{12,8},{13,9},{14,12},{15,13},{10,14},{11,... | collective-permute-start | bytes 540680 | tf_op jit(solution)/shard_map/ppermute | solution.py:267
  81.2 2.0 %collective-permute-done.17 = bf16[64,1536]{1,0:T(8,128)(2,1)S(1)} collective-permute-done((bf16[64,1536]{1,0:T(8,128)(2,1)S(1)}, bf16[64,1536]{1,0:T(8,128)(2,1)S(1)}, u32[]{:S(2)}, u32[]{:S(2)}) %collective-permute-start.17) | collective-permute-done | bytes 196640 | tf_op jit(solution)/shard_map/ppermute | solution.py:267
  84.2 1.2 %collective-permute-start.22 = (bf16[64,1536]{1,0:T(8,128)(2,1)S(1)}, bf16[64,1536]{1,0:T(8,128)(2,1)S(1)}, u32[]{:S(2)}, u32[]{:S(2)}) collective-permute-start(bf16[64,1536]{1,0:T(8,128)(2,1)S(1)} %add_convert_fusion.1), channel_id=1, source_target_pairs={{4,0},{5,1},{8,4},{9,5},{12,8},{13,9},{14,12},{15,13},{10,14},{11,... | collective-permute-start | bytes 589832 | tf_op jit(solution)/shard_map/ppermute | solution.py:267
  85.4 1.6 %collective-permute-done.26 = bf16[64,1408]{1,0:T(8,128)(2,1)S(1)} collective-permute-done((bf16[64,1408]{1,0:T(8,128)(2,1)S(1)}, bf16[64,1408]{1,0:T(8,128)(2,1)S(1)}, u32[]{:S(2)}, u32[]{:S(2)}) %collective-permute-start.26) | collective-permute-done | bytes 180256 | tf_op jit(solution)/shard_map/ppermute | solution.py:267
  88.1 1.2 %collective-permute-start.30 = (bf16[64,1408]{1,0:T(8,128)(2,1)S(1)}, bf16[64,1408]{1,0:T(8,128)(2,1)S(1)}, u32[]{:S(2)}, u32[]{:S(2)}) collective-permute-start(bf16[64,1408]{1,0:T(8,128)(2,1)S(1)} %add_convert_fusion.6), channel_id=1, source_target_pairs={{4,0},{5,1},{8,4},{9,5},{12,8},{13,9},{14,12},{15,13},{10,14},{11,... | collective-permute-start | bytes 540680 | tf_op jit(solution)/shard_map/ppermute | solution.py:267
  89.3 2.0 %collective-permute-done.18 = bf16[64,1536]{1,0:T(8,128)(2,1)S(1)} collective-permute-done((bf16[64,1536]{1,0:T(8,128)(2,1)S(1)}, bf16[64,1536]{1,0:T(8,128)(2,1)S(1)}, u32[]{:S(2)}, u32[]{:S(2)}) %collective-permute-start.18) | collective-permute-done | bytes 196640 | tf_op jit(solution)/shard_map/ppermute | solution.py:267
  92.3 1.2 %collective-permute-start.23 = (bf16[64,1536]{1,0:T(8,128)(2,1)S(1)}, bf16[64,1536]{1,0:T(8,128)(2,1)S(1)}, u32[]{:S(2)}, u32[]{:S(2)}) collective-permute-start(bf16[64,1536]{1,0:T(8,128)(2,1)S(1)} %add_convert_fusion), channel_id=1, source_target_pairs={{4,0},{5,1},{8,4},{9,5},{12,8},{13,9},{14,12},{15,13},{10,14},{11,... | collective-permute-start | bytes 589832 | tf_op jit(solution)/shard_map/ppermute | solution.py:267
  93.5 2.6 %collective-permute-done.30 = bf16[64,1408]{1,0:T(8,128)(2,1)S(1)} collective-permute-done((bf16[64,1408]{1,0:T(8,128)(2,1)S(1)}, bf16[64,1408]{1,0:T(8,128)(2,1)S(1)}, u32[]{:S(2)}, u32[]{:S(2)}) %collective-permute-start.30) | collective-permute-done | bytes 180256 | tf_op jit(solution)/shard_map/ppermute | solution.py:267
  96.1 1.2 %collective-permute-start.31 = (bf16[64,1408]{1,0:T(8,128)(2,1)S(1)}, bf16[64,1408]{1,0:T(8,128)(2,1)S(1)}, u32[]{:S(2)}, u32[]{:S(2)}) collective-permute-start(bf16[64,1408]{1,0:T(8,128)(2,1)S(1)} %add_convert_fusion.5), channel_id=1, source_target_pairs={{4,0},{5,1},{8,4},{9,5},{12,8},{13,9},{14,12},{15,13},{10,14},{11,... | collective-permute-start | bytes 540680 | tf_op jit(solution)/shard_map/ppermute | solution.py:267
  97.3 1.2 %collective-permute-done.19 = bf16[64,1536]{1,0:T(8,128)(2,1)S(1)} collective-permute-done((bf16[64,1536]{1,0:T(8,128)(2,1)S(1)}, bf16[64,1536]{1,0:T(8,128)(2,1)S(1)}, u32[]{:S(2)}, u32[]{:S(2)}) %collective-permute-start.19) | collective-permute-done | bytes 196640 | tf_op jit(solution)/shard_map/ppermute | solution.py:267
  99.5 3.5 %collective-permute-done.31 = bf16[64,1408]{1,0:T(8,128)(2,1)S(1)} collective-permute-done((bf16[64,1408]{1,0:T(8,128)(2,1)S(1)}, bf16[64,1408]{1,0:T(8,128)(2,1)S(1)}, u32[]{:S(2)}, u32[]{:S(2)}) %collective-permute-start.31) | collective-permute-done | bytes 180256 | tf_op jit(solution)/shard_map/ppermute | solution.py:267
  103.1 1.6 %collective-permute-done.20 = bf16[64,1536]{1,0:T(8,128)(2,1)S(1)} collective-permute-done((bf16[64,1536]{1,0:T(8,128)(2,1)S(1)}, bf16[64,1536]{1,0:T(8,128)(2,1)S(1)}, u32[]{:S(2)}, u32[]{:S(2)}) %collective-permute-start.20) | collective-permute-done | bytes 196640 | tf_op jit(solution)/shard_map/ppermute | solution.py:267
  (66 shorter events, 20.5 us)
Async XLA Ops:
  3.4 7.9 %collective-permute-start = (bf16[64,1536]{1,0:T(8,128)(2,1)S(1)}, bf16[64,1536]{1,0:T(8,128)(2,1)S(1)}, u32[]{:S(2)}, u32[]{:S(2)}) collective-permute-start(bf16[64,1536]{1,0:T(8,128)(2,1)S(1)} %get-tuple-element.33.refs_0_), channel_id=1, source_target_pairs={{0,4},{1,5},{4,8},{5,9},{8,12},{9,13},{12,14},{13,15},{14,10},{15,... | collective-permute-start | bytes 589832 | tf_op jit(solution)/shard_map/ppermute | solution.py:267
  6.5 8.2 %collective-permute-start.8 = (bf16[64,1408]{1,0:T(8,128)(2,1)S(1)}, bf16[64,1408]{1,0:T(8,128)(2,1)S(1)}, u32[]{:S(2)}, u32[]{:S(2)}) collective-permute-start(bf16[64,1408]{1,0:T(8,128)(2,1)S(1)} %get-tuple-element.37.refs_0_), channel_id=1, source_target_pairs={{4,0},{5,1},{8,4},{9,5},{12,8},{13,9},{14,12},{15,13},{10,14},{11,... | collective-permute-start | bytes 540680 | tf_op jit(solution)/shard_map/ppermute | solution.py:267
  6.5 11.2 %collective-permute-start.1 = (bf16[64,1536]{1,0:T(8,128)(2,1)S(1)}, bf16[64,1536]{1,0:T(8,128)(2,1)S(1)}, u32[]{:S(2)}, u32[]{:S(2)}) collective-permute-start(bf16[64,1536]{1,0:T(8,128)(2,1)S(1)} %get-tuple-element.33.refs_0_), channel_id=1, source_target_pairs={{4,0},{5,1},{8,4},{9,5},{12,8},{13,9},{14,12},{15,13},{10,14},{11,... | collective-permute-start | bytes 589832 | tf_op jit(solution)/shard_map/ppermute | solution.py:267
  11.3 7.8 %collective-permute-start.2 = (bf16[64,1536]{1,0:T(8,128)(2,1)S(1)}, bf16[64,1536]{1,0:T(8,128)(2,1)S(1)}, u32[]{:S(2)}, u32[]{:S(2)}) collective-permute-start(bf16[64,1536]{1,0:T(8,128)(2,1)S(1)} %collective-permute-done.refs_1_), channel_id=1, source_target_pairs={{0,4},{1,5},{4,8},{5,9},{8,12},{9,13},{12,14},{13,15},{14,10},{15,... | collective-permute-start | bytes 589832 | tf_op jit(solution)/shard_map/ppermute | solution.py:267
  13.1 9.9 %collective-permute-start.7 = (bf16[64,1408]{1,0:T(8,128)(2,1)S(1)}, bf16[64,1408]{1,0:T(8,128)(2,1)S(1)}, u32[]{:S(2)}, u32[]{:S(2)}) collective-permute-start(bf16[64,1408]{1,0:T(8,128)(2,1)S(1)} %get-tuple-element.37.refs_0_), channel_id=1, source_target_pairs={{0,4},{1,5},{4,8},{5,9},{8,12},{9,13},{12,14},{13,15},{14,10},{15,... | collective-permute-start | bytes 540680 | tf_op jit(solution)/shard_map/ppermute | solution.py:267
  14.7 10.1 %collective-permute-start.10 = (bf16[64,1408]{1,0:T(8,128)(2,1)S(1)}, bf16[64,1408]{1,0:T(8,128)(2,1)S(1)}, u32[]{:S(2)}, u32[]{:S(2)}) collective-permute-start(bf16[64,1408]{1,0:T(8,128)(2,1)S(1)} %collective-permute-done.8.refs_2_), channel_id=1, source_target_pairs={{4,0},{5,1},{8,4},{9,5},{12,8},{13,9},{14,12},{15,13},{10,14},{11,... | collective-permute-start | bytes 540680 | tf_op jit(solution)/shard_map/ppermute | solution.py:267
  17.6 13.2 %collective-permute-start.3 = (bf16[64,1536]{1,0:T(8,128)(2,1)S(1)}, bf16[64,1536]{1,0:T(8,128)(2,1)S(1)}, u32[]{:S(2)}, u32[]{:S(2)}) collective-permute-start(bf16[64,1536]{1,0:T(8,128)(2,1)S(1)} %collective-permute-done.1.refs_2_), channel_id=1, source_target_pairs={{4,0},{5,1},{8,4},{9,5},{12,8},{13,9},{14,12},{15,13},{10,14},{11,... | collective-permute-start | bytes 589832 | tf_op jit(solution)/shard_map/ppermute | solution.py:267
  19.1 13.6 %collective-permute-start.4 = (bf16[64,1536]{1,0:T(8,128)(2,1)S(1)}, bf16[64,1536]{1,0:T(8,128)(2,1)S(1)}, u32[]{:S(2)}, u32[]{:S(2)}) collective-permute-start(bf16[64,1536]{1,0:T(8,128)(2,1)S(1)} %collective-permute-done.2.refs_3_), channel_id=1, source_target_pairs={{0,4},{1,5},{4,8},{5,9},{8,12},{9,13},{12,14},{13,15},{14,10},{15,... | collective-permute-start | bytes 589832 | tf_op jit(solution)/shard_map/ppermute | solution.py:267
  23.0 6.3 %collective-permute-start.9 = (bf16[64,1408]{1,0:T(8,128)(2,1)S(1)}, bf16[64,1408]{1,0:T(8,128)(2,1)S(1)}, u32[]{:S(2)}, u32[]{:S(2)}) collective-permute-start(bf16[64,1408]{1,0:T(8,128)(2,1)S(1)} %collective-permute-done.7.refs_1_), channel_id=1, source_target_pairs={{0,4},{1,5},{4,8},{5,9},{8,12},{9,13},{12,14},{13,15},{14,10},{15,... | collective-permute-start | bytes 540680 | tf_op jit(solution)/shard_map/ppermute | solution.py:267
  24.8 6.5 %collective-permute-start.12 = (bf16[64,1408]{1,0:T(8,128)(2,1)S(1)}, bf16[64,1408]{1,0:T(8,128)(2,1)S(1)}, u32[]{:S(2)}, u32[]{:S(2)}) collective-permute-start(bf16[64,1408]{1,0:T(8,128)(2,1)S(1)} %collective-permute-done.10.refs_4_), channel_id=1, source_target_pairs={{4,0},{5,1},{8,4},{9,5},{12,8},{13,9},{14,12},{15,13},{10,14},{11,... | collective-permute-start | bytes 540680 | tf_op jit(solution)/shard_map/ppermute | solution.py:267
  29.3 11.5 %collective-permute-start.11 = (bf16[64,1408]{1,0:T(8,128)(2,1)S(1)}, bf16[64,1408]{1,0:T(8,128)(2,1)S(1)}, u32[]{:S(2)}, u32[]{:S(2)}) collective-permute-start(bf16[64,1408]{1,0:T(8,128)(2,1)S(1)} %collective-permute-done.9.refs_3_), channel_id=1, source_target_pairs={{0,4},{1,5},{4,8},{5,9},{8,12},{9,13},{12,14},{13,15},{14,10},{15,... | collective-permute-start | bytes 540680 | tf_op jit(solution)/shard_map/ppermute | solution.py:267
  30.8 6.5 %collective-permute-start.5 = (bf16[64,1536]{1,0:T(8,128)(2,1)S(1)}, bf16[64,1536]{1,0:T(8,128)(2,1)S(1)}, u32[]{:S(2)}, u32[]{:S(2)}) collective-permute-start(bf16[64,1536]{1,0:T(8,128)(2,1)S(1)} %collective-permute-done.3.refs_4_), channel_id=1, source_target_pairs={{4,0},{5,1},{8,4},{9,5},{12,8},{13,9},{14,12},{15,13},{10,14},{11,... | collective-permute-start | bytes 589832 | tf_op jit(solution)/shard_map/ppermute | solution.py:267
  31.3 9.4 %collective-permute-start.13 = (bf16[64,1408]{1,0:T(8,128)(2,1)S(1)}, bf16[64,1408]{1,0:T(8,128)(2,1)S(1)}, u32[]{:S(2)}, u32[]{:S(2)}) collective-permute-start(bf16[64,1408]{1,0:T(8,128)(2,1)S(1)} %collective-permute-done.12.refs_6_), channel_id=1, source_target_pairs={{4,0},{5,1},{8,4},{9,5},{12,8},{13,9},{14,12},{15,13},{10,14},{11,... | collective-permute-start | bytes 540680 | tf_op jit(solution)/shard_map/ppermute | solution.py:267
  32.8 5.9 %collective-permute-start.6 = (bf16[64,1536]{1,0:T(8,128)(2,1)S(1)}, bf16[64,1536]{1,0:T(8,128)(2,1)S(1)}, u32[]{:S(2)}, u32[]{:S(2)}) collective-permute-start(bf16[64,1536]{1,0:T(8,128)(2,1)S(1)} %collective-permute-done.4.refs_5_), channel_id=1, source_target_pairs={{0,4},{1,5},{4,8},{5,9},{8,12},{9,13},{12,14},{13,15},{14,10},{15,... | collective-permute-start | bytes 589832 | tf_op jit(solution)/shard_map/ppermute | solution.py:267
  41.4 1.8 %collective-permute-start.15 = (bf16[144,1408]{1,0:T(8,128)(2,1)S(1)}, bf16[144,1408]{1,0:T(8,128)(2,1)S(1)}, u32[]{:S(2)}, u32[]{:S(2)}) collective-permute-start(bf16[144,1408]{1,0:T(8,128)(2,1)S(1)} %get-tuple-element.40), channel_id=1, source_target_pairs={{0,1},{1,0},{2,3},{3,2},{4,5},{5,4},{6,7},{7,6},{8,9},{9,8},{10,11... | collective-permute-start | bytes 1216520 | tf_op jit(solution)/shard_map/ppermute | solution.py:267
  41.5 2.4 %collective-permute-start.14 = (bf16[144,1536]{1,0:T(8,128)(2,1)S(1)}, bf16[144,1536]{1,0:T(8,128)(2,1)S(1)}, u32[]{:S(2)}, u32[]{:S(2)}) collective-permute-start(bf16[144,1536]{1,0:T(8,128)(2,1)S(1)} %get-tuple-element.39), channel_id=1, source_target_pairs={{0,1},{1,0},{2,3},{3,2},{4,5},{5,4},{6,7},{7,6},{8,9},{9,8},{10,11... | collective-permute-start | bytes 1327112 | tf_op jit(solution)/shard_map/ppermute | solution.py:267
  68.7 1.8 %collective-permute-start.24 = (bf16[144,1408]{1,0:T(8,128)(2,1)S(1)}, bf16[144,1408]{1,0:T(8,128)(2,1)S(1)}, u32[]{:S(2)}, u32[]{:S(2)}) collective-permute-start(bf16[144,1408]{1,0:T(8,128)(2,1)S(1)} %get-tuple-element.52), channel_id=1, source_target_pairs={{0,1},{1,0},{2,3},{3,2},{4,5},{5,4},{6,7},{7,6},{8,9},{9,8},{10,11... | collective-permute-start | bytes 1216520 | tf_op jit(solution)/shard_map/ppermute | solution.py:267
  68.9 4.7 %collective-permute-start.16 = (bf16[144,1536]{1,0:T(8,128)(2,1)S(1)}, bf16[144,1536]{1,0:T(8,128)(2,1)S(1)}, u32[]{:S(2)}, u32[]{:S(2)}) collective-permute-start(bf16[144,1536]{1,0:T(8,128)(2,1)S(1)} %get-tuple-element.42), channel_id=1, source_target_pairs={{0,1},{1,0},{2,3},{3,2},{4,5},{5,4},{6,7},{7,6},{8,9},{9,8},{10,11... | collective-permute-start | bytes 1327112 | tf_op jit(solution)/shard_map/ppermute | solution.py:267
  71.5 7.4 %collective-permute-start.25 = (bf16[64,1408]{1,0:T(8,128)(2,1)S(1)}, bf16[64,1408]{1,0:T(8,128)(2,1)S(1)}, u32[]{:S(2)}, u32[]{:S(2)}) collective-permute-start(bf16[64,1408]{1,0:T(8,128)(2,1)S(1)} %get-tuple-element.56), channel_id=1, source_target_pairs={{0,4},{1,5},{4,8},{5,9},{8,12},{9,13},{12,14},{13,15},{14,10},{15,... | collective-permute-start | bytes 540680 | tf_op jit(solution)/shard_map/ppermute | solution.py:267
  72.5 7.5 %collective-permute-start.28 = (bf16[64,1408]{1,0:T(8,128)(2,1)S(1)}, bf16[64,1408]{1,0:T(8,128)(2,1)S(1)}, u32[]{:S(2)}, u32[]{:S(2)}) collective-permute-start(bf16[64,1408]{1,0:T(8,128)(2,1)S(1)} %get-tuple-element.60), channel_id=1, source_target_pairs={{4,0},{5,1},{8,4},{9,5},{12,8},{13,9},{14,12},{15,13},{10,14},{11,... | collective-permute-start | bytes 540680 | tf_op jit(solution)/shard_map/ppermute | solution.py:267
  74.6 8.5 %collective-permute-start.17 = (bf16[64,1536]{1,0:T(8,128)(2,1)S(1)}, bf16[64,1536]{1,0:T(8,128)(2,1)S(1)}, u32[]{:S(2)}, u32[]{:S(2)}) collective-permute-start(bf16[64,1536]{1,0:T(8,128)(2,1)S(1)} %get-tuple-element.47), channel_id=1, source_target_pairs={{0,4},{1,5},{4,8},{5,9},{8,12},{9,13},{12,14},{13,15},{14,10},{15,... | collective-permute-start | bytes 589832 | tf_op jit(solution)/shard_map/ppermute | solution.py:267
  75.6 8.6 %collective-permute-start.21 = (bf16[64,1536]{1,0:T(8,128)(2,1)S(1)}, bf16[64,1536]{1,0:T(8,128)(2,1)S(1)}, u32[]{:S(2)}, u32[]{:S(2)}) collective-permute-start(bf16[64,1536]{1,0:T(8,128)(2,1)S(1)} %get-tuple-element.50), channel_id=1, source_target_pairs={{4,0},{5,1},{8,4},{9,5},{12,8},{13,9},{14,12},{15,13},{10,14},{11,... | collective-permute-start | bytes 589832 | tf_op jit(solution)/shard_map/ppermute | solution.py:267
  79.0 8.0 %collective-permute-start.26 = (bf16[64,1408]{1,0:T(8,128)(2,1)S(1)}, bf16[64,1408]{1,0:T(8,128)(2,1)S(1)}, u32[]{:S(2)}, u32[]{:S(2)}) collective-permute-start(bf16[64,1408]{1,0:T(8,128)(2,1)S(1)} %add_convert_fusion.9), channel_id=1, source_target_pairs={{0,4},{1,5},{4,8},{5,9},{8,12},{9,13},{12,14},{13,15},{14,10},{15,... | collective-permute-start | bytes 540680 | tf_op jit(solution)/shard_map/ppermute | solution.py:267
  80.0 8.0 %collective-permute-start.29 = (bf16[64,1408]{1,0:T(8,128)(2,1)S(1)}, bf16[64,1408]{1,0:T(8,128)(2,1)S(1)}, u32[]{:S(2)}, u32[]{:S(2)}) collective-permute-start(bf16[64,1408]{1,0:T(8,128)(2,1)S(1)} %add_convert_fusion.7), channel_id=1, source_target_pairs={{4,0},{5,1},{8,4},{9,5},{12,8},{13,9},{14,12},{15,13},{10,14},{11,... | collective-permute-start | bytes 540680 | tf_op jit(solution)/shard_map/ppermute | solution.py:267
  83.2 8.0 %collective-permute-start.18 = (bf16[64,1536]{1,0:T(8,128)(2,1)S(1)}, bf16[64,1536]{1,0:T(8,128)(2,1)S(1)}, u32[]{:S(2)}, u32[]{:S(2)}) collective-permute-start(bf16[64,1536]{1,0:T(8,128)(2,1)S(1)} %add_convert_fusion.4), channel_id=1, source_target_pairs={{0,4},{1,5},{4,8},{5,9},{8,12},{9,13},{12,14},{13,15},{14,10},{15,... | collective-permute-start | bytes 589832 | tf_op jit(solution)/shard_map/ppermute | solution.py:267
  84.2 8.0 %collective-permute-start.22 = (bf16[64,1536]{1,0:T(8,128)(2,1)S(1)}, bf16[64,1536]{1,0:T(8,128)(2,1)S(1)}, u32[]{:S(2)}, u32[]{:S(2)}) collective-permute-start(bf16[64,1536]{1,0:T(8,128)(2,1)S(1)} %add_convert_fusion.1), channel_id=1, source_target_pairs={{4,0},{5,1},{8,4},{9,5},{12,8},{13,9},{14,12},{15,13},{10,14},{11,... | collective-permute-start | bytes 589832 | tf_op jit(solution)/shard_map/ppermute | solution.py:267
  87.1 12.5 %collective-permute-start.27 = (bf16[64,1408]{1,0:T(8,128)(2,1)S(1)}, bf16[64,1408]{1,0:T(8,128)(2,1)S(1)}, u32[]{:S(2)}, u32[]{:S(2)}) collective-permute-start(bf16[64,1408]{1,0:T(8,128)(2,1)S(1)} %add_convert_fusion.8), channel_id=1, source_target_pairs={{0,4},{1,5},{4,8},{5,9},{8,12},{9,13},{12,14},{13,15},{14,10},{15,... | collective-permute-start | bytes 540680 | tf_op jit(solution)/shard_map/ppermute | solution.py:267
  88.1 8.0 %collective-permute-start.30 = (bf16[64,1408]{1,0:T(8,128)(2,1)S(1)}, bf16[64,1408]{1,0:T(8,128)(2,1)S(1)}, u32[]{:S(2)}, u32[]{:S(2)}) collective-permute-start(bf16[64,1408]{1,0:T(8,128)(2,1)S(1)} %add_convert_fusion.6), channel_id=1, source_target_pairs={{4,0},{5,1},{8,4},{9,5},{12,8},{13,9},{14,12},{15,13},{10,14},{11,... | collective-permute-start | bytes 540680 | tf_op jit(solution)/shard_map/ppermute | solution.py:267
  91.3 7.2 %collective-permute-start.19 = (bf16[64,1536]{1,0:T(8,128)(2,1)S(1)}, bf16[64,1536]{1,0:T(8,128)(2,1)S(1)}, u32[]{:S(2)}, u32[]{:S(2)}) collective-permute-start(bf16[64,1536]{1,0:T(8,128)(2,1)S(1)} %add_convert_fusion.3), channel_id=1, source_target_pairs={{0,4},{1,5},{4,8},{5,9},{8,12},{9,13},{12,14},{13,15},{14,10},{15,... | collective-permute-start | bytes 589832 | tf_op jit(solution)/shard_map/ppermute | solution.py:267
  92.3 10.8 %collective-permute-start.23 = (bf16[64,1536]{1,0:T(8,128)(2,1)S(1)}, bf16[64,1536]{1,0:T(8,128)(2,1)S(1)}, u32[]{:S(2)}, u32[]{:S(2)}) collective-permute-start(bf16[64,1536]{1,0:T(8,128)(2,1)S(1)} %add_convert_fusion), channel_id=1, source_target_pairs={{4,0},{5,1},{8,4},{9,5},{12,8},{13,9},{14,12},{15,13},{10,14},{11,... | collective-permute-start | bytes 589832 | tf_op jit(solution)/shard_map/ppermute | solution.py:267
  96.1 6.9 %collective-permute-start.31 = (bf16[64,1408]{1,0:T(8,128)(2,1)S(1)}, bf16[64,1408]{1,0:T(8,128)(2,1)S(1)}, u32[]{:S(2)}, u32[]{:S(2)}) collective-permute-start(bf16[64,1408]{1,0:T(8,128)(2,1)S(1)} %add_convert_fusion.5), channel_id=1, source_target_pairs={{4,0},{5,1},{8,4},{9,5},{12,8},{13,9},{14,12},{15,13},{10,14},{11,... | collective-permute-start | bytes 540680 | tf_op jit(solution)/shard_map/ppermute | solution.py:267
  98.6 6.2 %collective-permute-start.20 = (bf16[64,1536]{1,0:T(8,128)(2,1)S(1)}, bf16[64,1536]{1,0:T(8,128)(2,1)S(1)}, u32[]{:S(2)}, u32[]{:S(2)}) collective-permute-start(bf16[64,1536]{1,0:T(8,128)(2,1)S(1)} %add_convert_fusion.2), channel_id=1, source_target_pairs={{0,4},{1,5},{4,8},{5,9},{8,12},{9,13},{12,14},{13,15},{14,10},{15,... | collective-permute-start | bytes 589832 | tf_op jit(solution)/shard_map/ppermute | solution.py:267
  (6 other events, 100.5 us)

commit v2 on v1

--- a/solution.py
+++ b/solution.py
@@ -74,20 +74,21 @@
     return (tok_float + moe_rows + bias_term).astype(jnp.bfloat16)
 
 
-def norm_kernel(top, tokens_ref, ids_ref, gates_ref, gain_ref, first_ref, second_ref):
+def norm_kernel(tokens_ref, named_ref, gain_ref, first_ref, second_ref):
     f32, bf16 = jnp.float32, jnp.bfloat16
     tok = tokens_ref[...].astype(f32)
     scale = lax.rsqrt(jnp.mean(tok * tok, axis=1, keepdims=True) + 1e-05)
     normed = (tok * scale * gain_ref[...][None, :]).astype(bf16)
     cut = tok.shape[1] - second_ref.shape[1]
     spare = first_ref.shape[1] - cut
-    sub = lax.broadcasted_iota(jnp.int32, (top, spare), 0)
-    lane = lax.broadcasted_iota(jnp.int32, (top, spare), 1)
-    turn = (((0,), (0,)), ((), ()))
+    entries = named_ref.shape[0]
+    sub = lax.broadcasted_iota(jnp.int32, (entries, spare), 0)
+    lane = lax.broadcasted_iota(jnp.int32, (entries, spare), 1)
     tail = lax.dot_general(
-        ids_ref[...].astype(f32), jnp.where(lane == sub, 1.0, 0.0), turn, preferred_element_type=f32
-    ) + lax.dot_general(
-        gates_ref[...].astype(f32), jnp.where(lane == sub + top, 1.0, 0.0), turn, preferred_element_type=f32
+        named_ref[...].astype(f32),
+        jnp.where(lane == sub, 1.0, 0.0),
+        (((0,), (0,)), ((), ())),
+        preferred_element_type=f32,
     )
     first_ref[:, :cut] = normed[:, :cut]
     first_ref[:, cut:] = tail.astype(bf16)
@@ -121,17 +122,29 @@
     tail_lane = lax.broadcasted_iota(jnp.int32, tail.shape, 1)
     slot = lax.broadcasted_iota(jnp.int32, (slots, rows), 0).astype(f32) + 1.0
     slot_lane = lax.broadcasted_iota(jnp.int32, (rows, slots), 1).astype(f32) + 1.0
-    placers = []
-    for i, out in enumerate((own_out, mate_out)):
+    named_rows, named_cols = [], []
+    for i in range(2):
         expert = experts_ref[0, i].astype(f32)
-        named = jnp.sum(jnp.where((ids == expert) & (entry < top), 1.0, 0.0), axis=0, keepdims=True)
-        number = jnp.dot(jnp.broadcast_to(named, (16, rows)).astype(bf16), upper, preferred_element_type=f32)[:1]
-        picker = jnp.where((number == slot) & (named > 0.5), 1.0, 0.0).astype(bf16)
-        picker_out[i * slots : (i + 1) * slots] = picker
-        out[...] = jnp.dot(picker, held[...], preferred_element_type=f32).astype(bf16)
-        named = jnp.sum(jnp.where((tail_float == expert) & (tail_lane < top), 1.0, 0.0), axis=1, keepdims=True)
-        number = jnp.dot(lower, jnp.broadcast_to(named, (rows, LANES)).astype(bf16), preferred_element_type=f32)
-        placers.append(jnp.where((number[:, :1] == slot_lane) & (named > 0.5), 1.0, 0.0))
+        hit = jnp.where((ids == expert) & (entry < top), 1.0, 0.0)
+        named_rows.append(jnp.sum(hit, axis=0, keepdims=True))
+        hit = jnp.where((tail_float == expert) & (tail_lane < top), 1.0, 0.0)
+        named_cols.append(jnp.sum(hit, axis=1, keepdims=True))
+    stacked = jnp.where(entry < 8, named_rows[0], named_rows[1]).astype(bf16)
+    number = jnp.dot(stacked, upper, preferred_element_type=f32)
+    pickers = [
+        jnp.where((number[8 * i : 8 * i + 1] == slot) & (named_rows[i] > 0.5), 1.0, 0.0) for i in range(2)
+    ]
+    picker_out[...] = jnp.concatenate(pickers, axis=0).astype(bf16)
+    chosen = jnp.dot(picker_out[...], held[...], preferred_element_type=f32).astype(bf16)
+    own_out[...] = chosen[:slots]
+    mate_out[...] = chosen[slots:]
+    wide_lane = lax.broadcasted_iota(jnp.int32, (rows, LANES), 1)
+    stacked = jnp.where(wide_lane < LANES // 2, named_cols[0], named_cols[1]).astype(bf16)
+    number = jnp.dot(lower, stacked, preferred_element_type=f32)
+    placers = [
+        jnp.where((number[:, at : at + 1] == slot_lane) & (named > 0.5), 1.0, 0.0)
+        for at, named in zip((0, LANES // 2), named_cols)
+    ]
     placer_out[...] = jnp.concatenate(placers, axis=1).astype(bf16)
 
 
@@ -277,12 +290,12 @@
     shape = lambda rows, cols, dtype=bf16: jax.ShapeDtypeStruct((rows, cols), dtype)
 
     chains = pl.pallas_call(
-        functools.partial(norm_kernel, top),
-        in_specs=[vmem] * 4,
+        norm_kernel,
+        in_specs=[vmem] * 3,
         out_specs=[vmem] * 2,
         out_shape=[shape(row_count, w) for w in lanes],
         compiler_params=params(NORM_MIB),
-    )(tokens, expert_ids.T, gate_ints.T, norm_gain)
+    )(tokens, jnp.concatenate([expert_ids.T, gate_ints.T], axis=0), norm_gain)
     me = lax.axis_index("ep").astype(jnp.int32)
     experts = jnp.stack([me, me ^ 1]).reshape(1, 2)
     biases = jnp.concatenate([bias_in, lax.dynamic_slice_in_dim(bias_out, me, 1, axis=0)], axis=1)

time: 106 us -> 105 us (level)
  local copies, waits for them, and re-layouts: 3.12 us -> 1.71 us
    unnamed x12 -> x8, local copies, waits for them, and re-layouts: 3.11 us -> 1.7 us
where the time goes in v2:
time: 105 us
  waiting for transfers between devices  37.4 us (36%)
  starting transfers between devices  32.8 us (31%)
  Pallas kernels  29.7 us (28%)
  other arithmetic  3.05 us (3%)
  local copies, waits for them, and re-layouts  1.71 us (2%)
    ppermute x32, waiting for transfers between devices, ring_shards(): send = lambda value, pairs: lax.ppermute(value, 'ep', pairs)  37.4 us
    ppermute x32, starting transfers between devices, ring_shards(): send = lambda value, pairs: lax.ppermute(value, 'ep', pairs)  32.8 us
    pallas_call x1, Pallas kernels, ring_shards(): pl.pallas_call(functools.partial(expert_kernel, top, steps_in, spans), gr...  24.8 us
  transfers between devices with their start and end apart: 32, of which 18 were waited for; matrix products, arithmetic and copies ran while one was open for 1% of the time, Pallas kernels for 4%

profile of v2, /device:TPU:0, one launch (start us, length us, event | category | flops | bytes accessed | tf_op | source)
XLA Modules:
  0.0 104.9 jit_solution(14451243841098767261)
XLA Ops:
  2.7 3.1 %collective-permute-start = (bf16[64,1536]{1,0:T(8,128)(2,1)S(1)}, bf16[64,1536]{1,0:T(8,128)(2,1)S(1)}, u32[]{:S(2)}, u32[]{:S(2)}) collective-permute-start(bf16[64,1536]{1,0:T(8,128)(2,1)S(1)} %get-tuple-element.33.refs_0_), channel_id=1, source_target_pairs={{0,4},{1,5},{4,8},{5,9},{8,12},{9,13},{12,14},{13,15},{14,10},{15,... | collective-permute-start | bytes 589832 | tf_op jit(solution)/shard_map/ppermute | solution.py:280
  5.8 1.9 %collective-permute-start.1 = (bf16[64,1536]{1,0:T(8,128)(2,1)S(1)}, bf16[64,1536]{1,0:T(8,128)(2,1)S(1)}, u32[]{:S(2)}, u32[]{:S(2)}) collective-permute-start(bf16[64,1536]{1,0:T(8,128)(2,1)S(1)} %get-tuple-element.33.refs_0_), channel_id=1, source_target_pairs={{4,0},{5,1},{8,4},{9,5},{12,8},{13,9},{14,12},{15,13},{10,14},{11,... | collective-permute-start | bytes 589832 | tf_op jit(solution)/shard_map/ppermute | solution.py:280
  7.7 2.9 %collective-permute-done.refs_1_ = bf16[64,1536]{1,0:T(8,128)(2,1)S(1)} collective-permute-done((bf16[64,1536]{1,0:T(8,128)(2,1)S(1)}, bf16[64,1536]{1,0:T(8,128)(2,1)S(1)}, u32[]{:S(2)}, u32[]{:S(2)}) %collective-permute-start) | collective-permute-done | bytes 196640 | tf_op jit(solution)/shard_map/ppermute | solution.py:280
  10.6 1.8 %collective-permute-start.2 = (bf16[64,1536]{1,0:T(8,128)(2,1)S(1)}, bf16[64,1536]{1,0:T(8,128)(2,1)S(1)}, u32[]{:S(2)}, u32[]{:S(2)}) collective-permute-start(bf16[64,1536]{1,0:T(8,128)(2,1)S(1)} %collective-permute-done.refs_1_), channel_id=1, source_target_pairs={{0,4},{1,5},{4,8},{5,9},{8,12},{9,13},{12,14},{13,15},{14,10},{15,... | collective-permute-start | bytes 589832 | tf_op jit(solution)/shard_map/ppermute | solution.py:280
  12.4 1.6 %collective-permute-start.7 = (bf16[64,1408]{1,0:T(8,128)(2,1)S(1)}, bf16[64,1408]{1,0:T(8,128)(2,1)S(1)}, u32[]{:S(2)}, u32[]{:S(2)}) collective-permute-start(bf16[64,1408]{1,0:T(8,128)(2,1)S(1)} %get-tuple-element.37.refs_0_), channel_id=1, source_target_pairs={{0,4},{1,5},{4,8},{5,9},{8,12},{9,13},{12,14},{13,15},{14,10},{15,... | collective-permute-start | bytes 540680 | tf_op jit(solution)/shard_map/ppermute | solution.py:280
  14.5 2.5 %collective-permute-done.1.refs_2_ = bf16[64,1536]{1,0:T(8,128)(2,1)S(1)} collective-permute-done((bf16[64,1536]{1,0:T(8,128)(2,1)S(1)}, bf16[64,1536]{1,0:T(8,128)(2,1)S(1)}, u32[]{:S(2)}, u32[]{:S(2)}) %collective-permute-start.1) | collective-permute-done | bytes 196640 | tf_op jit(solution)/shard_map/ppermute | solution.py:280
  17.1 1.4 %collective-permute-done.2.refs_3_ = bf16[64,1536]{1,0:T(8,128)(2,1)S(1)} collective-permute-done((bf16[64,1536]{1,0:T(8,128)(2,1)S(1)}, bf16[64,1536]{1,0:T(8,128)(2,1)S(1)}, u32[]{:S(2)}, u32[]{:S(2)}) %collective-permute-start.2) | collective-permute-done | bytes 196640 | tf_op jit(solution)/shard_map/ppermute | solution.py:280
  18.5 1.8 %collective-permute-start.4 = (bf16[64,1536]{1,0:T(8,128)(2,1)S(1)}, bf16[64,1536]{1,0:T(8,128)(2,1)S(1)}, u32[]{:S(2)}, u32[]{:S(2)}) collective-permute-start(bf16[64,1536]{1,0:T(8,128)(2,1)S(1)} %collective-permute-done.2.refs_3_), channel_id=1, source_target_pairs={{0,4},{1,5},{4,8},{5,9},{8,12},{9,13},{12,14},{13,15},{14,10},{15,... | collective-permute-start | bytes 589832 | tf_op jit(solution)/shard_map/ppermute | solution.py:280
  20.3 2.0 %collective-permute-done.7.refs_1_ = bf16[64,1408]{1,0:T(8,128)(2,1)S(1)} collective-permute-done((bf16[64,1408]{1,0:T(8,128)(2,1)S(1)}, bf16[64,1408]{1,0:T(8,128)(2,1)S(1)}, u32[]{:S(2)}, u32[]{:S(2)}) %collective-permute-start.7) | collective-permute-done | bytes 180256 | tf_op jit(solution)/shard_map/ppermute | solution.py:280
  22.3 1.8 %collective-permute-start.9 = (bf16[64,1408]{1,0:T(8,128)(2,1)S(1)}, bf16[64,1408]{1,0:T(8,128)(2,1)S(1)}, u32[]{:S(2)}, u32[]{:S(2)}) collective-permute-start(bf16[64,1408]{1,0:T(8,128)(2,1)S(1)} %collective-permute-done.7.refs_1_), channel_id=1, source_target_pairs={{0,4},{1,5},{4,8},{5,9},{8,12},{9,13},{12,14},{13,15},{14,10},{15,... | collective-permute-start | bytes 540680 | tf_op jit(solution)/shard_map/ppermute | solution.py:280
  24.3 4.3 %collective-permute-done.9.refs_3_ = bf16[64,1408]{1,0:T(8,128)(2,1)S(1)} collective-permute-done((bf16[64,1408]{1,0:T(8,128)(2,1)S(1)}, bf16[64,1408]{1,0:T(8,128)(2,1)S(1)}, u32[]{:S(2)}, u32[]{:S(2)}) %collective-permute-start.9) | collective-permute-done | bytes 180256 | tf_op jit(solution)/shard_map/ppermute | solution.py:280
  28.6 1.5 %collective-permute-start.11 = (bf16[64,1408]{1,0:T(8,128)(2,1)S(1)}, bf16[64,1408]{1,0:T(8,128)(2,1)S(1)}, u32[]{:S(2)}, u32[]{:S(2)}) collective-permute-start(bf16[64,1408]{1,0:T(8,128)(2,1)S(1)} %collective-permute-done.9.refs_3_), channel_id=1, source_target_pairs={{0,4},{1,5},{4,8},{5,9},{8,12},{9,13},{12,14},{13,15},{14,10},{15,... | collective-permute-start | bytes 540680 | tf_op jit(solution)/shard_map/ppermute | solution.py:280
  30.7 1.4 %collective-permute-start.13 = (bf16[64,1408]{1,0:T(8,128)(2,1)S(1)}, bf16[64,1408]{1,0:T(8,128)(2,1)S(1)}, u32[]{:S(2)}, u32[]{:S(2)}) collective-permute-start(bf16[64,1408]{1,0:T(8,128)(2,1)S(1)} %collective-permute-done.12.refs_6_), channel_id=1, source_target_pairs={{4,0},{5,1},{8,4},{9,5},{12,8},{13,9},{14,12},{15,13},{10,14},{11,... | collective-permute-start | bytes 540680 | tf_op jit(solution)/shard_map/ppermute | solution.py:280
  32.8 3.8 %collective-permute-done.5.refs_6_ = bf16[64,1536]{1,0:T(8,128)(2,1)S(1)} collective-permute-done((bf16[64,1536]{1,0:T(8,128)(2,1)S(1)}, bf16[64,1536]{1,0:T(8,128)(2,1)S(1)}, u32[]{:S(2)}, u32[]{:S(2)}) %collective-permute-start.5) | collective-permute-done | bytes 196640 | tf_op jit(solution)/shard_map/ppermute | solution.py:280
  36.7 1.4 %collective-permute-done.6.refs_7_ = bf16[64,1536]{1,0:T(8,128)(2,1)S(1)} collective-permute-done((bf16[64,1536]{1,0:T(8,128)(2,1)S(1)}, bf16[64,1536]{1,0:T(8,128)(2,1)S(1)}, u32[]{:S(2)}, u32[]{:S(2)}) %collective-permute-start.6) | collective-permute-done | bytes 196640 | tf_op jit(solution)/shard_map/ppermute | solution.py:280
  38.0 2.0 %shard_map.83 = (bf16[144,1536]{1,0:T(8,128)(2,1)S(1)}, bf16[144,1536]{1,0:T(8,128)(2,1)S(1)}, bf16[288,512]{1,0:T(8,128)(2,1)S(1)}, bf16[512,288]{1,0:T(8,128)(2,1)S(1)}) custom-call(s32[1,2]{1,0:T(1,128)S(1)} %add_bitcast_fusion.experts_ref, bf16[64,1536]{1,0:T(8,128)(2,1)S(1)} %get-tuple-element.33.refs_0_, ...), custom_call_target="tpu_custom_call" | custom-call | flops 452984832 | bytes 1048576 | tf_op jit(solution)/shard_map/pallas_call | solution.py:315
  43.1 24.8 %shard_map.85 = (bf16[144,1536]{1,0:T(8,128)(2,1)S(1)}, bf16[144,1536]{1,0:T(8,128)(2,1)S(1)}, bf16[144,1408]{1,0:T(8,128)(2,1)S(1)}, bf16[144,1408]{1,0:T(8,128)(2,1)S(1)}) custom-call(s32[1,2]{1,0:T(1,128)S(1)} %add_bitcast_fusion.experts_ref, bf16[144,2944]{1,0:T(8,128)(2,1)S(1)} %get-tuple-element.38.own_rows, ...), custom_call_target="tpu_custom_call" | custom-call | flops 14332723200 | bytes 49766400 | tf_op jit(solution)/shard_map/pallas_call | solution.py:340
  68.4 1.2 %collective-permute-done.24.mate_ref = bf16[144,1408]{1,0:T(8,128)(2,1)S(1)} collective-permute-done((bf16[144,1408]{1,0:T(8,128)(2,1)S(1)}, bf16[144,1408]{1,0:T(8,128)(2,1)S(1)}, u32[]{:S(2)}, u32[]{:S(2)}) %collective-permute-start.24) | collective-permute-done | bytes 405536 | tf_op jit(solution)/shard_map/ppermute | solution.py:280
  71.7 1.1 %collective-permute-start.28 = (bf16[64,1408]{1,0:T(8,128)(2,1)S(1)}, bf16[64,1408]{1,0:T(8,128)(2,1)S(1)}, u32[]{:S(2)}, u32[]{:S(2)}) collective-permute-start(bf16[64,1408]{1,0:T(8,128)(2,1)S(1)} %get-tuple-element.60), channel_id=1, source_target_pairs={{4,0},{5,1},{8,4},{9,5},{12,8},{13,9},{14,12},{15,13},{10,14},{11,... | collective-permute-start | bytes 540680 | tf_op jit(solution)/shard_map/ppermute | solution.py:280
  75.9 2.2 %collective-permute-done.25 = bf16[64,1408]{1,0:T(8,128)(2,1)S(1)} collective-permute-done((bf16[64,1408]{1,0:T(8,128)(2,1)S(1)}, bf16[64,1408]{1,0:T(8,128)(2,1)S(1)}, u32[]{:S(2)}, u32[]{:S(2)}) %collective-permute-start.25) | collective-permute-done | bytes 180256 | tf_op jit(solution)/shard_map/ppermute | solution.py:280
  79.3 1.2 %collective-permute-start.29 = (bf16[64,1408]{1,0:T(8,128)(2,1)S(1)}, bf16[64,1408]{1,0:T(8,128)(2,1)S(1)}, u32[]{:S(2)}, u32[]{:S(2)}) collective-permute-start(bf16[64,1408]{1,0:T(8,128)(2,1)S(1)} %add_convert_fusion.7), channel_id=1, source_target_pairs={{4,0},{5,1},{8,4},{9,5},{12,8},{13,9},{14,12},{15,13},{10,14},{11,... | collective-permute-start | bytes 540680 | tf_op jit(solution)/shard_map/ppermute | solution.py:280
  80.4 2.0 %collective-permute-done.17 = bf16[64,1536]{1,0:T(8,128)(2,1)S(1)} collective-permute-done((bf16[64,1536]{1,0:T(8,128)(2,1)S(1)}, bf16[64,1536]{1,0:T(8,128)(2,1)S(1)}, u32[]{:S(2)}, u32[]{:S(2)}) %collective-permute-start.17) | collective-permute-done | bytes 196640 | tf_op jit(solution)/shard_map/ppermute | solution.py:280
  83.5 1.2 %collective-permute-start.22 = (bf16[64,1536]{1,0:T(8,128)(2,1)S(1)}, bf16[64,1536]{1,0:T(8,128)(2,1)S(1)}, u32[]{:S(2)}, u32[]{:S(2)}) collective-permute-start(bf16[64,1536]{1,0:T(8,128)(2,1)S(1)} %add_convert_fusion.1), channel_id=1, source_target_pairs={{4,0},{5,1},{8,4},{9,5},{12,8},{13,9},{14,12},{15,13},{10,14},{11,... | collective-permute-start | bytes 589832 | tf_op jit(solution)/shard_map/ppermute | solution.py:280
  84.6 1.6 %collective-permute-done.26 = bf16[64,1408]{1,0:T(8,128)(2,1)S(1)} collective-permute-done((bf16[64,1408]{1,0:T(8,128)(2,1)S(1)}, bf16[64,1408]{1,0:T(8,128)(2,1)S(1)}, u32[]{:S(2)}, u32[]{:S(2)}) %collective-permute-start.26) | collective-permute-done | bytes 180256 | tf_op jit(solution)/shard_map/ppermute | solution.py:280
  87.3 1.2 %collective-permute-start.30 = (bf16[64,1408]{1,0:T(8,128)(2,1)S(1)}, bf16[64,1408]{1,0:T(8,128)(2,1)S(1)}, u32[]{:S(2)}, u32[]{:S(2)}) collective-permute-start(bf16[64,1408]{1,0:T(8,128)(2,1)S(1)} %add_convert_fusion.6), channel_id=1, source_target_pairs={{4,0},{5,1},{8,4},{9,5},{12,8},{13,9},{14,12},{15,13},{10,14},{11,... | collective-permute-start | bytes 540680 | tf_op jit(solution)/shard_map/ppermute | solution.py:280
  88.5 2.0 %collective-permute-done.18 = bf16[64,1536]{1,0:T(8,128)(2,1)S(1)} collective-permute-done((bf16[64,1536]{1,0:T(8,128)(2,1)S(1)}, bf16[64,1536]{1,0:T(8,128)(2,1)S(1)}, u32[]{:S(2)}, u32[]{:S(2)}) %collective-permute-start.18) | collective-permute-done | bytes 196640 | tf_op jit(solution)/shard_map/ppermute | solution.py:280
  91.5 1.2 %collective-permute-start.23 = (bf16[64,1536]{1,0:T(8,128)(2,1)S(1)}, bf16[64,1536]{1,0:T(8,128)(2,1)S(1)}, u32[]{:S(2)}, u32[]{:S(2)}) collective-permute-start(bf16[64,1536]{1,0:T(8,128)(2,1)S(1)} %add_convert_fusion), channel_id=1, source_target_pairs={{4,0},{5,1},{8,4},{9,5},{12,8},{13,9},{14,12},{15,13},{10,14},{11,... | collective-permute-start | bytes 589832 | tf_op jit(solution)/shard_map/ppermute | solution.py:280
  92.7 2.6 %collective-permute-done.30 = bf16[64,1408]{1,0:T(8,128)(2,1)S(1)} collective-permute-done((bf16[64,1408]{1,0:T(8,128)(2,1)S(1)}, bf16[64,1408]{1,0:T(8,128)(2,1)S(1)}, u32[]{:S(2)}, u32[]{:S(2)}) %collective-permute-start.30) | collective-permute-done | bytes 180256 | tf_op jit(solution)/shard_map/ppermute | solution.py:280
  95.3 1.1 %collective-permute-start.31 = (bf16[64,1408]{1,0:T(8,128)(2,1)S(1)}, bf16[64,1408]{1,0:T(8,128)(2,1)S(1)}, u32[]{:S(2)}, u32[]{:S(2)}) collective-permute-start(bf16[64,1408]{1,0:T(8,128)(2,1)S(1)} %add_convert_fusion.5), channel_id=1, source_target_pairs={{4,0},{5,1},{8,4},{9,5},{12,8},{13,9},{14,12},{15,13},{10,14},{11,... | collective-permute-start | bytes 540680 | tf_op jit(solution)/shard_map/ppermute | solution.py:280
  96.5 1.3 %collective-permute-done.19 = bf16[64,1536]{1,0:T(8,128)(2,1)S(1)} collective-permute-done((bf16[64,1536]{1,0:T(8,128)(2,1)S(1)}, bf16[64,1536]{1,0:T(8,128)(2,1)S(1)}, u32[]{:S(2)}, u32[]{:S(2)}) %collective-permute-start.19) | collective-permute-done | bytes 196640 | tf_op jit(solution)/shard_map/ppermute | solution.py:280
  98.8 3.5 %collective-permute-done.31 = bf16[64,1408]{1,0:T(8,128)(2,1)S(1)} collective-permute-done((bf16[64,1408]{1,0:T(8,128)(2,1)S(1)}, bf16[64,1408]{1,0:T(8,128)(2,1)S(1)}, u32[]{:S(2)}, u32[]{:S(2)}) %collective-permute-start.31) | collective-permute-done | bytes 180256 | tf_op jit(solution)/shard_map/ppermute | solution.py:280
  102.3 1.6 %collective-permute-done.20 = bf16[64,1536]{1,0:T(8,128)(2,1)S(1)} collective-permute-done((bf16[64,1536]{1,0:T(8,128)(2,1)S(1)}, bf16[64,1536]{1,0:T(8,128)(2,1)S(1)}, u32[]{:S(2)}, u32[]{:S(2)}) %collective-permute-start.20) | collective-permute-done | bytes 196640 | tf_op jit(solution)/shard_map/ppermute | solution.py:280
  (63 shorter events, 19.8 us)
Async XLA Ops:
  2.7 7.9 %collective-permute-start = (bf16[64,1536]{1,0:T(8,128)(2,1)S(1)}, bf16[64,1536]{1,0:T(8,128)(2,1)S(1)}, u32[]{:S(2)}, u32[]{:S(2)}) collective-permute-start(bf16[64,1536]{1,0:T(8,128)(2,1)S(1)} %get-tuple-element.33.refs_0_), channel_id=1, source_target_pairs={{0,4},{1,5},{4,8},{5,9},{8,12},{9,13},{12,14},{13,15},{14,10},{15,... | collective-permute-start | bytes 589832 | tf_op jit(solution)/shard_map/ppermute | solution.py:280
  5.8 8.2 %collective-permute-start.8 = (bf16[64,1408]{1,0:T(8,128)(2,1)S(1)}, bf16[64,1408]{1,0:T(8,128)(2,1)S(1)}, u32[]{:S(2)}, u32[]{:S(2)}) collective-permute-start(bf16[64,1408]{1,0:T(8,128)(2,1)S(1)} %get-tuple-element.37.refs_0_), channel_id=1, source_target_pairs={{4,0},{5,1},{8,4},{9,5},{12,8},{13,9},{14,12},{15,13},{10,14},{11,... | collective-permute-start | bytes 540680 | tf_op jit(solution)/shard_map/ppermute | solution.py:280
  5.8 11.2 %collective-permute-start.1 = (bf16[64,1536]{1,0:T(8,128)(2,1)S(1)}, bf16[64,1536]{1,0:T(8,128)(2,1)S(1)}, u32[]{:S(2)}, u32[]{:S(2)}) collective-permute-start(bf16[64,1536]{1,0:T(8,128)(2,1)S(1)} %get-tuple-element.33.refs_0_), channel_id=1, source_target_pairs={{4,0},{5,1},{8,4},{9,5},{12,8},{13,9},{14,12},{15,13},{10,14},{11,... | collective-permute-start | bytes 589832 | tf_op jit(solution)/shard_map/ppermute | solution.py:280
  10.6 7.8 %collective-permute-start.2 = (bf16[64,1536]{1,0:T(8,128)(2,1)S(1)}, bf16[64,1536]{1,0:T(8,128)(2,1)S(1)}, u32[]{:S(2)}, u32[]{:S(2)}) collective-permute-start(bf16[64,1536]{1,0:T(8,128)(2,1)S(1)} %collective-permute-done.refs_1_), channel_id=1, source_target_pairs={{0,4},{1,5},{4,8},{5,9},{8,12},{9,13},{12,14},{13,15},{14,10},{15,... | collective-permute-start | bytes 589832 | tf_op jit(solution)/shard_map/ppermute | solution.py:280
  12.4 9.9 %collective-permute-start.7 = (bf16[64,1408]{1,0:T(8,128)(2,1)S(1)}, bf16[64,1408]{1,0:T(8,128)(2,1)S(1)}, u32[]{:S(2)}, u32[]{:S(2)}) collective-permute-start(bf16[64,1408]{1,0:T(8,128)(2,1)S(1)} %get-tuple-element.37.refs_0_), channel_id=1, source_target_pairs={{0,4},{1,5},{4,8},{5,9},{8,12},{9,13},{12,14},{13,15},{14,10},{15,... | collective-permute-start | bytes 540680 | tf_op jit(solution)/shard_map/ppermute | solution.py:280
  14.0 10.1 %collective-permute-start.10 = (bf16[64,1408]{1,0:T(8,128)(2,1)S(1)}, bf16[64,1408]{1,0:T(8,128)(2,1)S(1)}, u32[]{:S(2)}, u32[]{:S(2)}) collective-permute-start(bf16[64,1408]{1,0:T(8,128)(2,1)S(1)} %collective-permute-done.8.refs_2_), channel_id=1, source_target_pairs={{4,0},{5,1},{8,4},{9,5},{12,8},{13,9},{14,12},{15,13},{10,14},{11,... | collective-permute-start | bytes 540680 | tf_op jit(solution)/shard_map/ppermute | solution.py:280
  17.0 13.2 %collective-permute-start.3 = (bf16[64,1536]{1,0:T(8,128)(2,1)S(1)}, bf16[64,1536]{1,0:T(8,128)(2,1)S(1)}, u32[]{:S(2)}, u32[]{:S(2)}) collective-permute-start(bf16[64,1536]{1,0:T(8,128)(2,1)S(1)} %collective-permute-done.1.refs_2_), channel_id=1, source_target_pairs={{4,0},{5,1},{8,4},{9,5},{12,8},{13,9},{14,12},{15,13},{10,14},{11,... | collective-permute-start | bytes 589832 | tf_op jit(solution)/shard_map/ppermute | solution.py:280
  18.5 13.6 %collective-permute-start.4 = (bf16[64,1536]{1,0:T(8,128)(2,1)S(1)}, bf16[64,1536]{1,0:T(8,128)(2,1)S(1)}, u32[]{:S(2)}, u32[]{:S(2)}) collective-permute-start(bf16[64,1536]{1,0:T(8,128)(2,1)S(1)} %collective-permute-done.2.refs_3_), channel_id=1, source_target_pairs={{0,4},{1,5},{4,8},{5,9},{8,12},{9,13},{12,14},{13,15},{14,10},{15,... | collective-permute-start | bytes 589832 | tf_op jit(solution)/shard_map/ppermute | solution.py:280
  22.3 6.3 %collective-permute-start.9 = (bf16[64,1408]{1,0:T(8,128)(2,1)S(1)}, bf16[64,1408]{1,0:T(8,128)(2,1)S(1)}, u32[]{:S(2)}, u32[]{:S(2)}) collective-permute-start(bf16[64,1408]{1,0:T(8,128)(2,1)S(1)} %collective-permute-done.7.refs_1_), channel_id=1, source_target_pairs={{0,4},{1,5},{4,8},{5,9},{8,12},{9,13},{12,14},{13,15},{14,10},{15,... | collective-permute-start | bytes 540680 | tf_op jit(solution)/shard_map/ppermute | solution.py:280
  24.1 6.5 %collective-permute-start.12 = (bf16[64,1408]{1,0:T(8,128)(2,1)S(1)}, bf16[64,1408]{1,0:T(8,128)(2,1)S(1)}, u32[]{:S(2)}, u32[]{:S(2)}) collective-permute-start(bf16[64,1408]{1,0:T(8,128)(2,1)S(1)} %collective-permute-done.10.refs_4_), channel_id=1, source_target_pairs={{4,0},{5,1},{8,4},{9,5},{12,8},{13,9},{14,12},{15,13},{10,14},{11,... | collective-permute-start | bytes 540680 | tf_op jit(solution)/shard_map/ppermute | solution.py:280
  28.6 11.4 %collective-permute-start.11 = (bf16[64,1408]{1,0:T(8,128)(2,1)S(1)}, bf16[64,1408]{1,0:T(8,128)(2,1)S(1)}, u32[]{:S(2)}, u32[]{:S(2)}) collective-permute-start(bf16[64,1408]{1,0:T(8,128)(2,1)S(1)} %collective-permute-done.9.refs_3_), channel_id=1, source_target_pairs={{0,4},{1,5},{4,8},{5,9},{8,12},{9,13},{12,14},{13,15},{14,10},{15,... | collective-permute-start | bytes 540680 | tf_op jit(solution)/shard_map/ppermute | solution.py:280
  30.2 6.5 %collective-permute-start.5 = (bf16[64,1536]{1,0:T(8,128)(2,1)S(1)}, bf16[64,1536]{1,0:T(8,128)(2,1)S(1)}, u32[]{:S(2)}, u32[]{:S(2)}) collective-permute-start(bf16[64,1536]{1,0:T(8,128)(2,1)S(1)} %collective-permute-done.3.refs_4_), channel_id=1, source_target_pairs={{4,0},{5,1},{8,4},{9,5},{12,8},{13,9},{14,12},{15,13},{10,14},{11,... | collective-permute-start | bytes 589832 | tf_op jit(solution)/shard_map/ppermute | solution.py:280
  30.7 9.3 %collective-permute-start.13 = (bf16[64,1408]{1,0:T(8,128)(2,1)S(1)}, bf16[64,1408]{1,0:T(8,128)(2,1)S(1)}, u32[]{:S(2)}, u32[]{:S(2)}) collective-permute-start(bf16[64,1408]{1,0:T(8,128)(2,1)S(1)} %collective-permute-done.12.refs_6_), channel_id=1, source_target_pairs={{4,0},{5,1},{8,4},{9,5},{12,8},{13,9},{14,12},{15,13},{10,14},{11,... | collective-permute-start | bytes 540680 | tf_op jit(solution)/shard_map/ppermute | solution.py:280
  32.1 5.9 %collective-permute-start.6 = (bf16[64,1536]{1,0:T(8,128)(2,1)S(1)}, bf16[64,1536]{1,0:T(8,128)(2,1)S(1)}, u32[]{:S(2)}, u32[]{:S(2)}) collective-permute-start(bf16[64,1536]{1,0:T(8,128)(2,1)S(1)} %collective-permute-done.4.refs_5_), channel_id=1, source_target_pairs={{0,4},{1,5},{4,8},{5,9},{8,12},{9,13},{12,14},{13,15},{14,10},{15,... | collective-permute-start | bytes 589832 | tf_op jit(solution)/shard_map/ppermute | solution.py:280
  40.7 1.8 %collective-permute-start.15 = (bf16[144,1408]{1,0:T(8,128)(2,1)S(1)}, bf16[144,1408]{1,0:T(8,128)(2,1)S(1)}, u32[]{:S(2)}, u32[]{:S(2)}) collective-permute-start(bf16[144,1408]{1,0:T(8,128)(2,1)S(1)} %get-tuple-element.40), channel_id=1, source_target_pairs={{0,1},{1,0},{2,3},{3,2},{4,5},{5,4},{6,7},{7,6},{8,9},{9,8},{10,11... | collective-permute-start | bytes 1216520 | tf_op jit(solution)/shard_map/ppermute | solution.py:280
  40.7 2.4 %collective-permute-start.14 = (bf16[144,1536]{1,0:T(8,128)(2,1)S(1)}, bf16[144,1536]{1,0:T(8,128)(2,1)S(1)}, u32[]{:S(2)}, u32[]{:S(2)}) collective-permute-start(bf16[144,1536]{1,0:T(8,128)(2,1)S(1)} %get-tuple-element.39), channel_id=1, source_target_pairs={{0,1},{1,0},{2,3},{3,2},{4,5},{5,4},{6,7},{7,6},{8,9},{9,8},{10,11... | collective-permute-start | bytes 1327112 | tf_op jit(solution)/shard_map/ppermute | solution.py:280
  67.9 1.8 %collective-permute-start.24 = (bf16[144,1408]{1,0:T(8,128)(2,1)S(1)}, bf16[144,1408]{1,0:T(8,128)(2,1)S(1)}, u32[]{:S(2)}, u32[]{:S(2)}) collective-permute-start(bf16[144,1408]{1,0:T(8,128)(2,1)S(1)} %get-tuple-element.52), channel_id=1, source_target_pairs={{0,1},{1,0},{2,3},{3,2},{4,5},{5,4},{6,7},{7,6},{8,9},{9,8},{10,11... | collective-permute-start | bytes 1216520 | tf_op jit(solution)/shard_map/ppermute | solution.py:280
  68.1 4.7 %collective-permute-start.16 = (bf16[144,1536]{1,0:T(8,128)(2,1)S(1)}, bf16[144,1536]{1,0:T(8,128)(2,1)S(1)}, u32[]{:S(2)}, u32[]{:S(2)}) collective-permute-start(bf16[144,1536]{1,0:T(8,128)(2,1)S(1)} %get-tuple-element.42), channel_id=1, source_target_pairs={{0,1},{1,0},{2,3},{3,2},{4,5},{5,4},{6,7},{7,6},{8,9},{9,8},{10,11... | collective-permute-start | bytes 1327112 | tf_op jit(solution)/shard_map/ppermute | solution.py:280
  70.7 7.4 %collective-permute-start.25 = (bf16[64,1408]{1,0:T(8,128)(2,1)S(1)}, bf16[64,1408]{1,0:T(8,128)(2,1)S(1)}, u32[]{:S(2)}, u32[]{:S(2)}) collective-permute-start(bf16[64,1408]{1,0:T(8,128)(2,1)S(1)} %get-tuple-element.56), channel_id=1, source_target_pairs={{0,4},{1,5},{4,8},{5,9},{8,12},{9,13},{12,14},{13,15},{14,10},{15,... | collective-permute-start | bytes 540680 | tf_op jit(solution)/shard_map/ppermute | solution.py:280
  71.7 7.5 %collective-permute-start.28 = (bf16[64,1408]{1,0:T(8,128)(2,1)S(1)}, bf16[64,1408]{1,0:T(8,128)(2,1)S(1)}, u32[]{:S(2)}, u32[]{:S(2)}) collective-permute-start(bf16[64,1408]{1,0:T(8,128)(2,1)S(1)} %get-tuple-element.60), channel_id=1, source_target_pairs={{4,0},{5,1},{8,4},{9,5},{12,8},{13,9},{14,12},{15,13},{10,14},{11,... | collective-permute-start | bytes 540680 | tf_op jit(solution)/shard_map/ppermute | solution.py:280
  73.8 8.5 %collective-permute-start.17 = (bf16[64,1536]{1,0:T(8,128)(2,1)S(1)}, bf16[64,1536]{1,0:T(8,128)(2,1)S(1)}, u32[]{:S(2)}, u32[]{:S(2)}) collective-permute-start(bf16[64,1536]{1,0:T(8,128)(2,1)S(1)} %get-tuple-element.47), channel_id=1, source_target_pairs={{0,4},{1,5},{4,8},{5,9},{8,12},{9,13},{12,14},{13,15},{14,10},{15,... | collective-permute-start | bytes 589832 | tf_op jit(solution)/shard_map/ppermute | solution.py:280
  74.8 8.6 %collective-permute-start.21 = (bf16[64,1536]{1,0:T(8,128)(2,1)S(1)}, bf16[64,1536]{1,0:T(8,128)(2,1)S(1)}, u32[]{:S(2)}, u32[]{:S(2)}) collective-permute-start(bf16[64,1536]{1,0:T(8,128)(2,1)S(1)} %get-tuple-element.50), channel_id=1, source_target_pairs={{4,0},{5,1},{8,4},{9,5},{12,8},{13,9},{14,12},{15,13},{10,14},{11,... | collective-permute-start | bytes 589832 | tf_op jit(solution)/shard_map/ppermute | solution.py:280
  78.2 8.0 %collective-permute-start.26 = (bf16[64,1408]{1,0:T(8,128)(2,1)S(1)}, bf16[64,1408]{1,0:T(8,128)(2,1)S(1)}, u32[]{:S(2)}, u32[]{:S(2)}) collective-permute-start(bf16[64,1408]{1,0:T(8,128)(2,1)S(1)} %add_convert_fusion.9), channel_id=1, source_target_pairs={{0,4},{1,5},{4,8},{5,9},{8,12},{9,13},{12,14},{13,15},{14,10},{15,... | collective-permute-start | bytes 540680 | tf_op jit(solution)/shard_map/ppermute | solution.py:280
  79.3 8.0 %collective-permute-start.29 = (bf16[64,1408]{1,0:T(8,128)(2,1)S(1)}, bf16[64,1408]{1,0:T(8,128)(2,1)S(1)}, u32[]{:S(2)}, u32[]{:S(2)}) collective-permute-start(bf16[64,1408]{1,0:T(8,128)(2,1)S(1)} %add_convert_fusion.7), channel_id=1, source_target_pairs={{4,0},{5,1},{8,4},{9,5},{12,8},{13,9},{14,12},{15,13},{10,14},{11,... | collective-permute-start | bytes 540680 | tf_op jit(solution)/shard_map/ppermute | solution.py:280
  82.4 8.0 %collective-permute-start.18 = (bf16[64,1536]{1,0:T(8,128)(2,1)S(1)}, bf16[64,1536]{1,0:T(8,128)(2,1)S(1)}, u32[]{:S(2)}, u32[]{:S(2)}) collective-permute-start(bf16[64,1536]{1,0:T(8,128)(2,1)S(1)} %add_convert_fusion.4), channel_id=1, source_target_pairs={{0,4},{1,5},{4,8},{5,9},{8,12},{9,13},{12,14},{13,15},{14,10},{15,... | collective-permute-start | bytes 589832 | tf_op jit(solution)/shard_map/ppermute | solution.py:280
  83.5 8.0 %collective-permute-start.22 = (bf16[64,1536]{1,0:T(8,128)(2,1)S(1)}, bf16[64,1536]{1,0:T(8,128)(2,1)S(1)}, u32[]{:S(2)}, u32[]{:S(2)}) collective-permute-start(bf16[64,1536]{1,0:T(8,128)(2,1)S(1)} %add_convert_fusion.1), channel_id=1, source_target_pairs={{4,0},{5,1},{8,4},{9,5},{12,8},{13,9},{14,12},{15,13},{10,14},{11,... | collective-permute-start | bytes 589832 | tf_op jit(solution)/shard_map/ppermute | solution.py:280
  86.3 12.5 %collective-permute-start.27 = (bf16[64,1408]{1,0:T(8,128)(2,1)S(1)}, bf16[64,1408]{1,0:T(8,128)(2,1)S(1)}, u32[]{:S(2)}, u32[]{:S(2)}) collective-permute-start(bf16[64,1408]{1,0:T(8,128)(2,1)S(1)} %add_convert_fusion.8), channel_id=1, source_target_pairs={{0,4},{1,5},{4,8},{5,9},{8,12},{9,13},{12,14},{13,15},{14,10},{15,... | collective-permute-start | bytes 540680 | tf_op jit(solution)/shard_map/ppermute | solution.py:280
  87.3 8.0 %collective-permute-start.30 = (bf16[64,1408]{1,0:T(8,128)(2,1)S(1)}, bf16[64,1408]{1,0:T(8,128)(2,1)S(1)}, u32[]{:S(2)}, u32[]{:S(2)}) collective-permute-start(bf16[64,1408]{1,0:T(8,128)(2,1)S(1)} %add_convert_fusion.6), channel_id=1, source_target_pairs={{4,0},{5,1},{8,4},{9,5},{12,8},{13,9},{14,12},{15,13},{10,14},{11,... | collective-permute-start | bytes 540680 | tf_op jit(solution)/shard_map/ppermute | solution.py:280
  90.5 7.2 %collective-permute-start.19 = (bf16[64,1536]{1,0:T(8,128)(2,1)S(1)}, bf16[64,1536]{1,0:T(8,128)(2,1)S(1)}, u32[]{:S(2)}, u32[]{:S(2)}) collective-permute-start(bf16[64,1536]{1,0:T(8,128)(2,1)S(1)} %add_convert_fusion.3), channel_id=1, source_target_pairs={{0,4},{1,5},{4,8},{5,9},{8,12},{9,13},{12,14},{13,15},{14,10},{15,... | collective-permute-start | bytes 589832 | tf_op jit(solution)/shard_map/ppermute | solution.py:280
  91.5 10.8 %collective-permute-start.23 = (bf16[64,1536]{1,0:T(8,128)(2,1)S(1)}, bf16[64,1536]{1,0:T(8,128)(2,1)S(1)}, u32[]{:S(2)}, u32[]{:S(2)}) collective-permute-start(bf16[64,1536]{1,0:T(8,128)(2,1)S(1)} %add_convert_fusion), channel_id=1, source_target_pairs={{4,0},{5,1},{8,4},{9,5},{12,8},{13,9},{14,12},{15,13},{10,14},{11,... | collective-permute-start | bytes 589832 | tf_op jit(solution)/shard_map/ppermute | solution.py:280
  95.3 6.9 %collective-permute-start.31 = (bf16[64,1408]{1,0:T(8,128)(2,1)S(1)}, bf16[64,1408]{1,0:T(8,128)(2,1)S(1)}, u32[]{:S(2)}, u32[]{:S(2)}) collective-permute-start(bf16[64,1408]{1,0:T(8,128)(2,1)S(1)} %add_convert_fusion.5), channel_id=1, source_target_pairs={{4,0},{5,1},{8,4},{9,5},{12,8},{13,9},{14,12},{15,13},{10,14},{11,... | collective-permute-start | bytes 540680 | tf_op jit(solution)/shard_map/ppermute | solution.py:280
  97.8 6.2 %collective-permute-start.20 = (bf16[64,1536]{1,0:T(8,128)(2,1)S(1)}, bf16[64,1536]{1,0:T(8,128)(2,1)S(1)}, u32[]{:S(2)}, u32[]{:S(2)}) collective-permute-start(bf16[64,1536]{1,0:T(8,128)(2,1)S(1)} %add_convert_fusion.2), channel_id=1, source_target_pairs={{0,4},{1,5},{4,8},{5,9},{8,12},{9,13},{12,14},{13,15},{14,10},{15,... | collective-permute-start | bytes 589832 | tf_op jit(solution)/shard_map/ppermute | solution.py:280
  (4 other events, 98.4 us)

commit v3 on v2

--- a/solution.py
+++ b/solution.py
@@ -308,6 +308,7 @@
                 if hop < reach or way == c:
                     going[c][way] = send(going[c][way], pairs)
                     held[c].append(going[c][way])
+    held[0][-1], biases = lax.optimization_barrier((held[0][-1], biases))
     order = [0]
     for hop in range(1, reach):
         order += [-hop, hop]

time: 105 us -> 107 us (1.019)
  waiting for transfers between devices: 37.4 us -> 39.2 us
    ppermute x32, waiting for transfers between devices: 37.4 us -> 39.2 us  [ring_shards(): send = lambda value, pairs: lax.ppermute(value, 'ep', pairs)]
  transfers between devices with their start and end apart: 32 -> 32, of which waited for: 18 -> 16; matrix products, arithmetic and copies ran while one was open for 1% -> 1% of each run, Pallas kernels for 4% -> 4%
where the time goes in v3:
time: 107 us
  waiting for transfers between devices  39.2 us (37%)
  starting transfers between devices  33 us (31%)
  Pallas kernels  29.7 us (28%)
  other arithmetic  3.04 us (3%)
  local copies, waits for them, and re-layouts  1.71 us (2%)
    ppermute x32, waiting for transfers between devices, ring_shards(): send = lambda value, pairs: lax.ppermute(value, 'ep', pairs)  39.2 us
    ppermute x32, starting transfers between devices, ring_shards(): send = lambda value, pairs: lax.ppermute(value, 'ep', pairs)  33 us
    pallas_call x1, Pallas kernels, ring_shards(): pl.pallas_call(functools.partial(expert_kernel, top, steps_in, spans), gr...  24.8 us
  transfers between devices with their start and end apart: 32, of which 16 were waited for; matrix products, arithmetic and copies ran while one was open for 1% of the time, Pallas kernels for 4%

profile of v3, /device:TPU:0, one launch (start us, length us, event | category | flops | bytes accessed | tf_op | source)
XLA Modules:
  0.0 106.8 jit_solution(14609386901437327948)
XLA Ops:
  2.7 3.1 %collective-permute-start = (bf16[64,1536]{1,0:T(8,128)(2,1)S(1)}, bf16[64,1536]{1,0:T(8,128)(2,1)S(1)}, u32[]{:S(2)}, u32[]{:S(2)}) collective-permute-start(bf16[64,1536]{1,0:T(8,128)(2,1)S(1)} %get-tuple-element.35.refs_0_), channel_id=1, source_target_pairs={{0,4},{1,5},{4,8},{5,9},{8,12},{9,13},{12,14},{13,15},{14,10},{15,... | collective-permute-start | bytes 589832 | tf_op jit(solution)/shard_map/ppermute | solution.py:280
  5.8 1.9 %collective-permute-start.1 = (bf16[64,1536]{1,0:T(8,128)(2,1)S(1)}, bf16[64,1536]{1,0:T(8,128)(2,1)S(1)}, u32[]{:S(2)}, u32[]{:S(2)}) collective-permute-start(bf16[64,1536]{1,0:T(8,128)(2,1)S(1)} %get-tuple-element.35.refs_0_), channel_id=1, source_target_pairs={{4,0},{5,1},{8,4},{9,5},{12,8},{13,9},{14,12},{15,13},{10,14},{11,... | collective-permute-start | bytes 589832 | tf_op jit(solution)/shard_map/ppermute | solution.py:280
  7.7 2.9 %collective-permute-done.refs_1_ = bf16[64,1536]{1,0:T(8,128)(2,1)S(1)} collective-permute-done((bf16[64,1536]{1,0:T(8,128)(2,1)S(1)}, bf16[64,1536]{1,0:T(8,128)(2,1)S(1)}, u32[]{:S(2)}, u32[]{:S(2)}) %collective-permute-start) | collective-permute-done | bytes 196640 | tf_op jit(solution)/shard_map/ppermute | solution.py:280
  10.6 1.8 %collective-permute-start.2 = (bf16[64,1536]{1,0:T(8,128)(2,1)S(1)}, bf16[64,1536]{1,0:T(8,128)(2,1)S(1)}, u32[]{:S(2)}, u32[]{:S(2)}) collective-permute-start(bf16[64,1536]{1,0:T(8,128)(2,1)S(1)} %collective-permute-done.refs_1_), channel_id=1, source_target_pairs={{0,4},{1,5},{4,8},{5,9},{8,12},{9,13},{12,14},{13,15},{14,10},{15,... | collective-permute-start | bytes 589832 | tf_op jit(solution)/shard_map/ppermute | solution.py:280
  12.4 1.6 %collective-permute-start.7 = (bf16[64,1408]{1,0:T(8,128)(2,1)S(1)}, bf16[64,1408]{1,0:T(8,128)(2,1)S(1)}, u32[]{:S(2)}, u32[]{:S(2)}) collective-permute-start(bf16[64,1408]{1,0:T(8,128)(2,1)S(1)} %get-tuple-element.40.refs_0_), channel_id=1, source_target_pairs={{0,4},{1,5},{4,8},{5,9},{8,12},{9,13},{12,14},{13,15},{14,10},{15,... | collective-permute-start | bytes 540680 | tf_op jit(solution)/shard_map/ppermute | solution.py:280
  14.5 6.1 %collective-permute-done.7.refs_1_ = bf16[64,1408]{1,0:T(8,128)(2,1)S(1)} collective-permute-done((bf16[64,1408]{1,0:T(8,128)(2,1)S(1)}, bf16[64,1408]{1,0:T(8,128)(2,1)S(1)}, u32[]{:S(2)}, u32[]{:S(2)}) %collective-permute-start.7) | collective-permute-done | bytes 180256 | tf_op jit(solution)/shard_map/ppermute | solution.py:280
  20.6 1.5 %collective-permute-start.9 = (bf16[64,1408]{1,0:T(8,128)(2,1)S(1)}, bf16[64,1408]{1,0:T(8,128)(2,1)S(1)}, u32[]{:S(2)}, u32[]{:S(2)}) collective-permute-start(bf16[64,1408]{1,0:T(8,128)(2,1)S(1)} %collective-permute-done.7.refs_1_), channel_id=1, source_target_pairs={{0,4},{1,5},{4,8},{5,9},{8,12},{9,13},{12,14},{13,15},{14,10},{15,... | collective-permute-start | bytes 540680 | tf_op jit(solution)/shard_map/ppermute | solution.py:280
  22.6 1.4 %collective-permute-start.12 = (bf16[64,1408]{1,0:T(8,128)(2,1)S(1)}, bf16[64,1408]{1,0:T(8,128)(2,1)S(1)}, u32[]{:S(2)}, u32[]{:S(2)}) collective-permute-start(bf16[64,1408]{1,0:T(8,128)(2,1)S(1)} %collective-permute-done.10.refs_4_), channel_id=1, source_target_pairs={{4,0},{5,1},{8,4},{9,5},{12,8},{13,9},{14,12},{15,13},{10,14},{11,... | collective-permute-start | bytes 540680 | tf_op jit(solution)/shard_map/ppermute | solution.py:280
  24.6 3.3 %collective-permute-done.9.refs_3_ = bf16[64,1408]{1,0:T(8,128)(2,1)S(1)} collective-permute-done((bf16[64,1408]{1,0:T(8,128)(2,1)S(1)}, bf16[64,1408]{1,0:T(8,128)(2,1)S(1)}, u32[]{:S(2)}, u32[]{:S(2)}) %collective-permute-start.9) | collective-permute-done | bytes 180256 | tf_op jit(solution)/shard_map/ppermute | solution.py:280
  28.0 1.5 %collective-permute-start.11 = (bf16[64,1408]{1,0:T(8,128)(2,1)S(1)}, bf16[64,1408]{1,0:T(8,128)(2,1)S(1)}, u32[]{:S(2)}, u32[]{:S(2)}) collective-permute-start(bf16[64,1408]{1,0:T(8,128)(2,1)S(1)} %collective-permute-done.9.refs_3_), channel_id=1, source_target_pairs={{0,4},{1,5},{4,8},{5,9},{8,12},{9,13},{12,14},{13,15},{14,10},{15,... | collective-permute-start | bytes 540680 | tf_op jit(solution)/shard_map/ppermute | solution.py:280
  30.4 3.3 %collective-permute-done.12.refs_6_ = bf16[64,1408]{1,0:T(8,128)(2,1)S(1)} collective-permute-done((bf16[64,1408]{1,0:T(8,128)(2,1)S(1)}, bf16[64,1408]{1,0:T(8,128)(2,1)S(1)}, u32[]{:S(2)}, u32[]{:S(2)}) %collective-permute-start.12) | collective-permute-done | bytes 180256 | tf_op jit(solution)/shard_map/ppermute | solution.py:280
  34.3 1.4 %collective-permute-start.6 = (bf16[64,1536]{1,0:T(8,128)(2,1)S(1)}, bf16[64,1536]{1,0:T(8,128)(2,1)S(1)}, u32[]{:S(2)}, u32[]{:S(2)}) collective-permute-start(bf16[64,1536]{1,0:T(8,128)(2,1)S(1)} %collective-permute-done.4.refs_5_), channel_id=1, source_target_pairs={{0,4},{1,5},{4,8},{5,9},{8,12},{9,13},{12,14},{13,15},{14,10},{15,... | collective-permute-start | bytes 589832 | tf_op jit(solution)/shard_map/ppermute | solution.py:280
  36.6 3.4 %collective-permute-done.6.refs_7_ = bf16[64,1536]{1,0:T(8,128)(2,1)S(1)} collective-permute-done((bf16[64,1536]{1,0:T(8,128)(2,1)S(1)}, bf16[64,1536]{1,0:T(8,128)(2,1)S(1)}, u32[]{:S(2)}, u32[]{:S(2)}) %collective-permute-start.6) | collective-permute-done | bytes 196640 | tf_op jit(solution)/shard_map/ppermute | solution.py:280
  40.0 2.0 %shard_map.83 = (bf16[144,1536]{1,0:T(8,128)(2,1)S(1)}, bf16[144,1536]{1,0:T(8,128)(2,1)S(1)}, bf16[288,512]{1,0:T(8,128)(2,1)S(1)}, bf16[512,288]{1,0:T(8,128)(2,1)S(1)}) custom-call(s32[1,2]{1,0:T(1,128)S(1)} %add_bitcast_fusion.experts_ref, bf16[64,1536]{1,0:T(8,128)(2,1)S(1)} %get-tuple-element.35.refs_0_, ...), custom_call_target="tpu_custom_call" | custom-call | flops 452984832 | bytes 1048576 | tf_op jit(solution)/shard_map/pallas_call | solution.py:316
  43.2 1.4 %collective-permute-done.15.mate_second = bf16[144,1408]{1,0:T(8,128)(2,1)S(1)} collective-permute-done((bf16[144,1408]{1,0:T(8,128)(2,1)S(1)}, bf16[144,1408]{1,0:T(8,128)(2,1)S(1)}, u32[]{:S(2)}, u32[]{:S(2)}) %collective-permute-start.15) | collective-permute-done | bytes 405536 | tf_op jit(solution)/shard_map/ppermute | solution.py:280
  44.6 24.8 %shard_map.85 = (bf16[144,1536]{1,0:T(8,128)(2,1)S(1)}, bf16[144,1536]{1,0:T(8,128)(2,1)S(1)}, bf16[144,1408]{1,0:T(8,128)(2,1)S(1)}, bf16[144,1408]{1,0:T(8,128)(2,1)S(1)}) custom-call(s32[1,2]{1,0:T(1,128)S(1)} %add_bitcast_fusion.experts_ref, bf16[144,2944]{1,0:T(8,128)(2,1)S(1)} %get-tuple-element.41.own_rows, ...), custom_call_target="tpu_custom_call" | custom-call | flops 14332723200 | bytes 49766400 | tf_op jit(solution)/shard_map/pallas_call | solution.py:341
  69.9 1.2 %collective-permute-done.24.mate_ref = bf16[144,1408]{1,0:T(8,128)(2,1)S(1)} collective-permute-done((bf16[144,1408]{1,0:T(8,128)(2,1)S(1)}, bf16[144,1408]{1,0:T(8,128)(2,1)S(1)}, u32[]{:S(2)}, u32[]{:S(2)}) %collective-permute-start.24) | collective-permute-done | bytes 405536 | tf_op jit(solution)/shard_map/ppermute | solution.py:280
  72.2 1.5 %collective-permute-start.25 = (bf16[64,1408]{1,0:T(8,128)(2,1)S(1)}, bf16[64,1408]{1,0:T(8,128)(2,1)S(1)}, u32[]{:S(2)}, u32[]{:S(2)}) collective-permute-start(bf16[64,1408]{1,0:T(8,128)(2,1)S(1)} %get-tuple-element.60), channel_id=1, source_target_pairs={{0,4},{1,5},{4,8},{5,9},{8,12},{9,13},{12,14},{13,15},{14,10},{15,... | collective-permute-start | bytes 540680 | tf_op jit(solution)/shard_map/ppermute | solution.py:280
  75.3 1.5 %collective-permute-start.17 = (bf16[64,1536]{1,0:T(8,128)(2,1)S(1)}, bf16[64,1536]{1,0:T(8,128)(2,1)S(1)}, u32[]{:S(2)}, u32[]{:S(2)}) collective-permute-start(bf16[64,1536]{1,0:T(8,128)(2,1)S(1)} %get-tuple-element.51), channel_id=1, source_target_pairs={{0,4},{1,5},{4,8},{5,9},{8,12},{9,13},{12,14},{13,15},{14,10},{15,... | collective-permute-start | bytes 589832 | tf_op jit(solution)/shard_map/ppermute | solution.py:280
  77.4 2.2 %collective-permute-done.25 = bf16[64,1408]{1,0:T(8,128)(2,1)S(1)} collective-permute-done((bf16[64,1408]{1,0:T(8,128)(2,1)S(1)}, bf16[64,1408]{1,0:T(8,128)(2,1)S(1)}, u32[]{:S(2)}, u32[]{:S(2)}) %collective-permute-start.25) | collective-permute-done | bytes 180256 | tf_op jit(solution)/shard_map/ppermute | solution.py:280
  79.7 1.5 %collective-permute-start.26 = (bf16[64,1408]{1,0:T(8,128)(2,1)S(1)}, bf16[64,1408]{1,0:T(8,128)(2,1)S(1)}, u32[]{:S(2)}, u32[]{:S(2)}) collective-permute-start(bf16[64,1408]{1,0:T(8,128)(2,1)S(1)} %add_convert_fusion.9), channel_id=1, source_target_pairs={{0,4},{1,5},{4,8},{5,9},{8,12},{9,13},{12,14},{13,15},{14,10},{15,... | collective-permute-start | bytes 540680 | tf_op jit(solution)/shard_map/ppermute | solution.py:280
  81.9 2.0 %collective-permute-done.17 = bf16[64,1536]{1,0:T(8,128)(2,1)S(1)} collective-permute-done((bf16[64,1536]{1,0:T(8,128)(2,1)S(1)}, bf16[64,1536]{1,0:T(8,128)(2,1)S(1)}, u32[]{:S(2)}, u32[]{:S(2)}) %collective-permute-start.17) | collective-permute-done | bytes 196640 | tf_op jit(solution)/shard_map/ppermute | solution.py:280
  83.9 1.5 %collective-permute-start.18 = (bf16[64,1536]{1,0:T(8,128)(2,1)S(1)}, bf16[64,1536]{1,0:T(8,128)(2,1)S(1)}, u32[]{:S(2)}, u32[]{:S(2)}) collective-permute-start(bf16[64,1536]{1,0:T(8,128)(2,1)S(1)} %add_convert_fusion.4), channel_id=1, source_target_pairs={{0,4},{1,5},{4,8},{5,9},{8,12},{9,13},{12,14},{13,15},{14,10},{15,... | collective-permute-start | bytes 589832 | tf_op jit(solution)/shard_map/ppermute | solution.py:280
  86.1 1.6 %collective-permute-done.26 = bf16[64,1408]{1,0:T(8,128)(2,1)S(1)} collective-permute-done((bf16[64,1408]{1,0:T(8,128)(2,1)S(1)}, bf16[64,1408]{1,0:T(8,128)(2,1)S(1)}, u32[]{:S(2)}, u32[]{:S(2)}) %collective-permute-start.26) | collective-permute-done | bytes 180256 | tf_op jit(solution)/shard_map/ppermute | solution.py:280
  87.8 1.5 %collective-permute-start.27 = (bf16[64,1408]{1,0:T(8,128)(2,1)S(1)}, bf16[64,1408]{1,0:T(8,128)(2,1)S(1)}, u32[]{:S(2)}, u32[]{:S(2)}) collective-permute-start(bf16[64,1408]{1,0:T(8,128)(2,1)S(1)} %add_convert_fusion.8), channel_id=1, source_target_pairs={{0,4},{1,5},{4,8},{5,9},{8,12},{9,13},{12,14},{13,15},{14,10},{15,... | collective-permute-start | bytes 540680 | tf_op jit(solution)/shard_map/ppermute | solution.py:280
  90.0 2.0 %collective-permute-done.18 = bf16[64,1536]{1,0:T(8,128)(2,1)S(1)} collective-permute-done((bf16[64,1536]{1,0:T(8,128)(2,1)S(1)}, bf16[64,1536]{1,0:T(8,128)(2,1)S(1)}, u32[]{:S(2)}, u32[]{:S(2)}) %collective-permute-start.18) | collective-permute-done | bytes 196640 | tf_op jit(solution)/shard_map/ppermute | solution.py:280
  92.0 1.5 %collective-permute-start.19 = (bf16[64,1536]{1,0:T(8,128)(2,1)S(1)}, bf16[64,1536]{1,0:T(8,128)(2,1)S(1)}, u32[]{:S(2)}, u32[]{:S(2)}) collective-permute-start(bf16[64,1536]{1,0:T(8,128)(2,1)S(1)} %add_convert_fusion.3), channel_id=1, source_target_pairs={{0,4},{1,5},{4,8},{5,9},{8,12},{9,13},{12,14},{13,15},{14,10},{15,... | collective-permute-start | bytes 589832 | tf_op jit(solution)/shard_map/ppermute | solution.py:280
  94.2 3.1 %collective-permute-done.30 = bf16[64,1408]{1,0:T(8,128)(2,1)S(1)} collective-permute-done((bf16[64,1408]{1,0:T(8,128)(2,1)S(1)}, bf16[64,1408]{1,0:T(8,128)(2,1)S(1)}, u32[]{:S(2)}, u32[]{:S(2)}) %collective-permute-start.30) | collective-permute-done | bytes 180256 | tf_op jit(solution)/shard_map/ppermute | solution.py:280
  98.0 1.5 %collective-permute-done.19 = bf16[64,1536]{1,0:T(8,128)(2,1)S(1)} collective-permute-done((bf16[64,1536]{1,0:T(8,128)(2,1)S(1)}, bf16[64,1536]{1,0:T(8,128)(2,1)S(1)}, u32[]{:S(2)}, u32[]{:S(2)}) %collective-permute-start.19) | collective-permute-done | bytes 196640 | tf_op jit(solution)/shard_map/ppermute | solution.py:280
  99.5 1.5 %collective-permute-start.20 = (bf16[64,1536]{1,0:T(8,128)(2,1)S(1)}, bf16[64,1536]{1,0:T(8,128)(2,1)S(1)}, u32[]{:S(2)}, u32[]{:S(2)}) collective-permute-start(bf16[64,1536]{1,0:T(8,128)(2,1)S(1)} %add_convert_fusion.2), channel_id=1, source_target_pairs={{0,4},{1,5},{4,8},{5,9},{8,12},{9,13},{12,14},{13,15},{14,10},{15,... | collective-permute-start | bytes 589832 | tf_op jit(solution)/shard_map/ppermute | solution.py:280
  101.0 3.5 %collective-permute-done.31 = bf16[64,1408]{1,0:T(8,128)(2,1)S(1)} collective-permute-done((bf16[64,1408]{1,0:T(8,128)(2,1)S(1)}, bf16[64,1408]{1,0:T(8,128)(2,1)S(1)}, u32[]{:S(2)}, u32[]{:S(2)}) %collective-permute-start.31) | collective-permute-done | bytes 180256 | tf_op jit(solution)/shard_map/ppermute | solution.py:280
  104.5 1.4 %collective-permute-done.20 = bf16[64,1536]{1,0:T(8,128)(2,1)S(1)} collective-permute-done((bf16[64,1536]{1,0:T(8,128)(2,1)S(1)}, bf16[64,1536]{1,0:T(8,128)(2,1)S(1)}, u32[]{:S(2)}, u32[]{:S(2)}) %collective-permute-start.20) | collective-permute-done | bytes 196640 | tf_op jit(solution)/shard_map/ppermute | solution.py:280
  (63 shorter events, 16.5 us)
Async XLA Ops:
  2.7 7.9 %collective-permute-start = (bf16[64,1536]{1,0:T(8,128)(2,1)S(1)}, bf16[64,1536]{1,0:T(8,128)(2,1)S(1)}, u32[]{:S(2)}, u32[]{:S(2)}) collective-permute-start(bf16[64,1536]{1,0:T(8,128)(2,1)S(1)} %get-tuple-element.35.refs_0_), channel_id=1, source_target_pairs={{0,4},{1,5},{4,8},{5,9},{8,12},{9,13},{12,14},{13,15},{14,10},{15,... | collective-permute-start | bytes 589832 | tf_op jit(solution)/shard_map/ppermute | solution.py:280
  5.8 8.2 %collective-permute-start.8 = (bf16[64,1408]{1,0:T(8,128)(2,1)S(1)}, bf16[64,1408]{1,0:T(8,128)(2,1)S(1)}, u32[]{:S(2)}, u32[]{:S(2)}) collective-permute-start(bf16[64,1408]{1,0:T(8,128)(2,1)S(1)} %get-tuple-element.40.refs_0_), channel_id=1, source_target_pairs={{4,0},{5,1},{8,4},{9,5},{12,8},{13,9},{14,12},{15,13},{10,14},{11,... | collective-permute-start | bytes 540680 | tf_op jit(solution)/shard_map/ppermute | solution.py:280
  5.8 16.3 %collective-permute-start.1 = (bf16[64,1536]{1,0:T(8,128)(2,1)S(1)}, bf16[64,1536]{1,0:T(8,128)(2,1)S(1)}, u32[]{:S(2)}, u32[]{:S(2)}) collective-permute-start(bf16[64,1536]{1,0:T(8,128)(2,1)S(1)} %get-tuple-element.35.refs_0_), channel_id=1, source_target_pairs={{4,0},{5,1},{8,4},{9,5},{12,8},{13,9},{14,12},{15,13},{10,14},{11,... | collective-permute-start | bytes 589832 | tf_op jit(solution)/shard_map/ppermute | solution.py:280
  10.6 13.4 %collective-permute-start.2 = (bf16[64,1536]{1,0:T(8,128)(2,1)S(1)}, bf16[64,1536]{1,0:T(8,128)(2,1)S(1)}, u32[]{:S(2)}, u32[]{:S(2)}) collective-permute-start(bf16[64,1536]{1,0:T(8,128)(2,1)S(1)} %collective-permute-done.refs_1_), channel_id=1, source_target_pairs={{0,4},{1,5},{4,8},{5,9},{8,12},{9,13},{12,14},{13,15},{14,10},{15,... | collective-permute-start | bytes 589832 | tf_op jit(solution)/shard_map/ppermute | solution.py:280
  12.4 8.1 %collective-permute-start.7 = (bf16[64,1408]{1,0:T(8,128)(2,1)S(1)}, bf16[64,1408]{1,0:T(8,128)(2,1)S(1)}, u32[]{:S(2)}, u32[]{:S(2)}) collective-permute-start(bf16[64,1408]{1,0:T(8,128)(2,1)S(1)} %get-tuple-element.40.refs_0_), channel_id=1, source_target_pairs={{0,4},{1,5},{4,8},{5,9},{8,12},{9,13},{12,14},{13,15},{14,10},{15,... | collective-permute-start | bytes 540680 | tf_op jit(solution)/shard_map/ppermute | solution.py:280
  14.0 8.6 %collective-permute-start.10 = (bf16[64,1408]{1,0:T(8,128)(2,1)S(1)}, bf16[64,1408]{1,0:T(8,128)(2,1)S(1)}, u32[]{:S(2)}, u32[]{:S(2)}) collective-permute-start(bf16[64,1408]{1,0:T(8,128)(2,1)S(1)} %collective-permute-done.8.refs_2_), channel_id=1, source_target_pairs={{4,0},{5,1},{8,4},{9,5},{12,8},{13,9},{14,12},{15,13},{10,14},{11,... | collective-permute-start | bytes 540680 | tf_op jit(solution)/shard_map/ppermute | solution.py:280
  20.6 7.4 %collective-permute-start.9 = (bf16[64,1408]{1,0:T(8,128)(2,1)S(1)}, bf16[64,1408]{1,0:T(8,128)(2,1)S(1)}, u32[]{:S(2)}, u32[]{:S(2)}) collective-permute-start(bf16[64,1408]{1,0:T(8,128)(2,1)S(1)} %collective-permute-done.7.refs_1_), channel_id=1, source_target_pairs={{0,4},{1,5},{4,8},{5,9},{8,12},{9,13},{12,14},{13,15},{14,10},{15,... | collective-permute-start | bytes 540680 | tf_op jit(solution)/shard_map/ppermute | solution.py:280
  22.1 7.8 %collective-permute-start.3 = (bf16[64,1536]{1,0:T(8,128)(2,1)S(1)}, bf16[64,1536]{1,0:T(8,128)(2,1)S(1)}, u32[]{:S(2)}, u32[]{:S(2)}) collective-permute-start(bf16[64,1536]{1,0:T(8,128)(2,1)S(1)} %collective-permute-done.1.refs_2_), channel_id=1, source_target_pairs={{4,0},{5,1},{8,4},{9,5},{12,8},{13,9},{14,12},{15,13},{10,14},{11,... | collective-permute-start | bytes 589832 | tf_op jit(solution)/shard_map/ppermute | solution.py:280
  22.6 11.1 %collective-permute-start.12 = (bf16[64,1408]{1,0:T(8,128)(2,1)S(1)}, bf16[64,1408]{1,0:T(8,128)(2,1)S(1)}, u32[]{:S(2)}, u32[]{:S(2)}) collective-permute-start(bf16[64,1408]{1,0:T(8,128)(2,1)S(1)} %collective-permute-done.10.refs_4_), channel_id=1, source_target_pairs={{4,0},{5,1},{8,4},{9,5},{12,8},{13,9},{14,12},{15,13},{10,14},{11,... | collective-permute-start | bytes 540680 | tf_op jit(solution)/shard_map/ppermute | solution.py:280
  24.0 10.3 %collective-permute-start.4 = (bf16[64,1536]{1,0:T(8,128)(2,1)S(1)}, bf16[64,1536]{1,0:T(8,128)(2,1)S(1)}, u32[]{:S(2)}, u32[]{:S(2)}) collective-permute-start(bf16[64,1536]{1,0:T(8,128)(2,1)S(1)} %collective-permute-done.2.refs_3_), channel_id=1, source_target_pairs={{0,4},{1,5},{4,8},{5,9},{8,12},{9,13},{12,14},{13,15},{14,10},{15,... | collective-permute-start | bytes 589832 | tf_op jit(solution)/shard_map/ppermute | solution.py:280
  28.0 14.0 %collective-permute-start.11 = (bf16[64,1408]{1,0:T(8,128)(2,1)S(1)}, bf16[64,1408]{1,0:T(8,128)(2,1)S(1)}, u32[]{:S(2)}, u32[]{:S(2)}) collective-permute-start(bf16[64,1408]{1,0:T(8,128)(2,1)S(1)} %collective-permute-done.9.refs_3_), channel_id=1, source_target_pairs={{0,4},{1,5},{4,8},{5,9},{8,12},{9,13},{12,14},{13,15},{14,10},{15,... | collective-permute-start | bytes 540680 | tf_op jit(solution)/shard_map/ppermute | solution.py:280
  29.8 10.1 %collective-permute-start.5 = (bf16[64,1536]{1,0:T(8,128)(2,1)S(1)}, bf16[64,1536]{1,0:T(8,128)(2,1)S(1)}, u32[]{:S(2)}, u32[]{:S(2)}) collective-permute-start(bf16[64,1536]{1,0:T(8,128)(2,1)S(1)} %collective-permute-done.3.refs_4_), channel_id=1, source_target_pairs={{4,0},{5,1},{8,4},{9,5},{12,8},{13,9},{14,12},{15,13},{10,14},{11,... | collective-permute-start | bytes 589832 | tf_op jit(solution)/shard_map/ppermute | solution.py:280
  33.7 8.3 %collective-permute-start.13 = (bf16[64,1408]{1,0:T(8,128)(2,1)S(1)}, bf16[64,1408]{1,0:T(8,128)(2,1)S(1)}, u32[]{:S(2)}, u32[]{:S(2)}) collective-permute-start(bf16[64,1408]{1,0:T(8,128)(2,1)S(1)} %collective-permute-done.12.refs_6_), channel_id=1, source_target_pairs={{4,0},{5,1},{8,4},{9,5},{12,8},{13,9},{14,12},{15,13},{10,14},{11,... | collective-permute-start | bytes 540680 | tf_op jit(solution)/shard_map/ppermute | solution.py:280
  34.3 5.7 %collective-permute-start.6 = (bf16[64,1536]{1,0:T(8,128)(2,1)S(1)}, bf16[64,1536]{1,0:T(8,128)(2,1)S(1)}, u32[]{:S(2)}, u32[]{:S(2)}) collective-permute-start(bf16[64,1536]{1,0:T(8,128)(2,1)S(1)} %collective-permute-done.4.refs_5_), channel_id=1, source_target_pairs={{0,4},{1,5},{4,8},{5,9},{8,12},{9,13},{12,14},{13,15},{14,10},{15,... | collective-permute-start | bytes 589832 | tf_op jit(solution)/shard_map/ppermute | solution.py:280
  41.9 2.7 %collective-permute-start.14 = (bf16[144,1536]{1,0:T(8,128)(2,1)S(1)}, bf16[144,1536]{1,0:T(8,128)(2,1)S(1)}, u32[]{:S(2)}, u32[]{:S(2)}) collective-permute-start(bf16[144,1536]{1,0:T(8,128)(2,1)S(1)} %get-tuple-element.42), channel_id=1, source_target_pairs={{0,1},{1,0},{2,3},{3,2},{4,5},{5,4},{6,7},{7,6},{8,9},{9,8},{10,11... | collective-permute-start | bytes 1327112 | tf_op jit(solution)/shard_map/ppermute | solution.py:280
  42.7 1.9 %collective-permute-start.15 = (bf16[144,1408]{1,0:T(8,128)(2,1)S(1)}, bf16[144,1408]{1,0:T(8,128)(2,1)S(1)}, u32[]{:S(2)}, u32[]{:S(2)}) collective-permute-start(bf16[144,1408]{1,0:T(8,128)(2,1)S(1)} %get-tuple-element.43), channel_id=1, source_target_pairs={{0,1},{1,0},{2,3},{3,2},{4,5},{5,4},{6,7},{7,6},{8,9},{9,8},{10,11... | collective-permute-start | bytes 1216520 | tf_op jit(solution)/shard_map/ppermute | solution.py:280
  69.4 1.8 %collective-permute-start.24 = (bf16[144,1408]{1,0:T(8,128)(2,1)S(1)}, bf16[144,1408]{1,0:T(8,128)(2,1)S(1)}, u32[]{:S(2)}, u32[]{:S(2)}) collective-permute-start(bf16[144,1408]{1,0:T(8,128)(2,1)S(1)} %get-tuple-element.56), channel_id=1, source_target_pairs={{0,1},{1,0},{2,3},{3,2},{4,5},{5,4},{6,7},{7,6},{8,9},{9,8},{10,11... | collective-permute-start | bytes 1216520 | tf_op jit(solution)/shard_map/ppermute | solution.py:280
  69.8 4.5 %collective-permute-start.16 = (bf16[144,1536]{1,0:T(8,128)(2,1)S(1)}, bf16[144,1536]{1,0:T(8,128)(2,1)S(1)}, u32[]{:S(2)}, u32[]{:S(2)}) collective-permute-start(bf16[144,1536]{1,0:T(8,128)(2,1)S(1)} %get-tuple-element.46), channel_id=1, source_target_pairs={{0,1},{1,0},{2,3},{3,2},{4,5},{5,4},{6,7},{7,6},{8,9},{9,8},{10,11... | collective-permute-start | bytes 1327112 | tf_op jit(solution)/shard_map/ppermute | solution.py:280
  72.2 7.4 %collective-permute-start.25 = (bf16[64,1408]{1,0:T(8,128)(2,1)S(1)}, bf16[64,1408]{1,0:T(8,128)(2,1)S(1)}, u32[]{:S(2)}, u32[]{:S(2)}) collective-permute-start(bf16[64,1408]{1,0:T(8,128)(2,1)S(1)} %get-tuple-element.60), channel_id=1, source_target_pairs={{0,4},{1,5},{4,8},{5,9},{8,12},{9,13},{12,14},{13,15},{14,10},{15,... | collective-permute-start | bytes 540680 | tf_op jit(solution)/shard_map/ppermute | solution.py:280
  73.7 7.5 %collective-permute-start.28 = (bf16[64,1408]{1,0:T(8,128)(2,1)S(1)}, bf16[64,1408]{1,0:T(8,128)(2,1)S(1)}, u32[]{:S(2)}, u32[]{:S(2)}) collective-permute-start(bf16[64,1408]{1,0:T(8,128)(2,1)S(1)} %get-tuple-element.64), channel_id=1, source_target_pairs={{4,0},{5,1},{8,4},{9,5},{12,8},{13,9},{14,12},{15,13},{10,14},{11,... | collective-permute-start | bytes 540680 | tf_op jit(solution)/shard_map/ppermute | solution.py:280
  75.3 8.5 %collective-permute-start.17 = (bf16[64,1536]{1,0:T(8,128)(2,1)S(1)}, bf16[64,1536]{1,0:T(8,128)(2,1)S(1)}, u32[]{:S(2)}, u32[]{:S(2)}) collective-permute-start(bf16[64,1536]{1,0:T(8,128)(2,1)S(1)} %get-tuple-element.51), channel_id=1, source_target_pairs={{0,4},{1,5},{4,8},{5,9},{8,12},{9,13},{12,14},{13,15},{14,10},{15,... | collective-permute-start | bytes 589832 | tf_op jit(solution)/shard_map/ppermute | solution.py:280
  76.8 8.6 %collective-permute-start.21 = (bf16[64,1536]{1,0:T(8,128)(2,1)S(1)}, bf16[64,1536]{1,0:T(8,128)(2,1)S(1)}, u32[]{:S(2)}, u32[]{:S(2)}) collective-permute-start(bf16[64,1536]{1,0:T(8,128)(2,1)S(1)} %get-tuple-element.54), channel_id=1, source_target_pairs={{4,0},{5,1},{8,4},{9,5},{12,8},{13,9},{14,12},{15,13},{10,14},{11,... | collective-permute-start | bytes 589832 | tf_op jit(solution)/shard_map/ppermute | solution.py:280
  79.7 8.0 %collective-permute-start.26 = (bf16[64,1408]{1,0:T(8,128)(2,1)S(1)}, bf16[64,1408]{1,0:T(8,128)(2,1)S(1)}, u32[]{:S(2)}, u32[]{:S(2)}) collective-permute-start(bf16[64,1408]{1,0:T(8,128)(2,1)S(1)} %add_convert_fusion.9), channel_id=1, source_target_pairs={{0,4},{1,5},{4,8},{5,9},{8,12},{9,13},{12,14},{13,15},{14,10},{15,... | collective-permute-start | bytes 540680 | tf_op jit(solution)/shard_map/ppermute | solution.py:280
  81.2 8.0 %collective-permute-start.29 = (bf16[64,1408]{1,0:T(8,128)(2,1)S(1)}, bf16[64,1408]{1,0:T(8,128)(2,1)S(1)}, u32[]{:S(2)}, u32[]{:S(2)}) collective-permute-start(bf16[64,1408]{1,0:T(8,128)(2,1)S(1)} %add_convert_fusion.7), channel_id=1, source_target_pairs={{4,0},{5,1},{8,4},{9,5},{12,8},{13,9},{14,12},{15,13},{10,14},{11,... | collective-permute-start | bytes 540680 | tf_op jit(solution)/shard_map/ppermute | solution.py:280
  83.9 8.0 %collective-permute-start.18 = (bf16[64,1536]{1,0:T(8,128)(2,1)S(1)}, bf16[64,1536]{1,0:T(8,128)(2,1)S(1)}, u32[]{:S(2)}, u32[]{:S(2)}) collective-permute-start(bf16[64,1536]{1,0:T(8,128)(2,1)S(1)} %add_convert_fusion.4), channel_id=1, source_target_pairs={{0,4},{1,5},{4,8},{5,9},{8,12},{9,13},{12,14},{13,15},{14,10},{15,... | collective-permute-start | bytes 589832 | tf_op jit(solution)/shard_map/ppermute | solution.py:280
  85.4 8.0 %collective-permute-start.22 = (bf16[64,1536]{1,0:T(8,128)(2,1)S(1)}, bf16[64,1536]{1,0:T(8,128)(2,1)S(1)}, u32[]{:S(2)}, u32[]{:S(2)}) collective-permute-start(bf16[64,1536]{1,0:T(8,128)(2,1)S(1)} %add_convert_fusion.1), channel_id=1, source_target_pairs={{4,0},{5,1},{8,4},{9,5},{12,8},{13,9},{14,12},{15,13},{10,14},{11,... | collective-permute-start | bytes 589832 | tf_op jit(solution)/shard_map/ppermute | solution.py:280
  87.8 13.2 %collective-permute-start.27 = (bf16[64,1408]{1,0:T(8,128)(2,1)S(1)}, bf16[64,1408]{1,0:T(8,128)(2,1)S(1)}, u32[]{:S(2)}, u32[]{:S(2)}) collective-permute-start(bf16[64,1408]{1,0:T(8,128)(2,1)S(1)} %add_convert_fusion.8), channel_id=1, source_target_pairs={{0,4},{1,5},{4,8},{5,9},{8,12},{9,13},{12,14},{13,15},{14,10},{15,... | collective-permute-start | bytes 540680 | tf_op jit(solution)/shard_map/ppermute | solution.py:280
  89.3 8.0 %collective-permute-start.30 = (bf16[64,1408]{1,0:T(8,128)(2,1)S(1)}, bf16[64,1408]{1,0:T(8,128)(2,1)S(1)}, u32[]{:S(2)}, u32[]{:S(2)}) collective-permute-start(bf16[64,1408]{1,0:T(8,128)(2,1)S(1)} %add_convert_fusion.6), channel_id=1, source_target_pairs={{4,0},{5,1},{8,4},{9,5},{12,8},{13,9},{14,12},{15,13},{10,14},{11,... | collective-permute-start | bytes 540680 | tf_op jit(solution)/shard_map/ppermute | solution.py:280
  92.0 7.5 %collective-permute-start.19 = (bf16[64,1536]{1,0:T(8,128)(2,1)S(1)}, bf16[64,1536]{1,0:T(8,128)(2,1)S(1)}, u32[]{:S(2)}, u32[]{:S(2)}) collective-permute-start(bf16[64,1536]{1,0:T(8,128)(2,1)S(1)} %add_convert_fusion.3), channel_id=1, source_target_pairs={{0,4},{1,5},{4,8},{5,9},{8,12},{9,13},{12,14},{13,15},{14,10},{15,... | collective-permute-start | bytes 589832 | tf_op jit(solution)/shard_map/ppermute | solution.py:280
  93.5 11.0 %collective-permute-start.23 = (bf16[64,1536]{1,0:T(8,128)(2,1)S(1)}, bf16[64,1536]{1,0:T(8,128)(2,1)S(1)}, u32[]{:S(2)}, u32[]{:S(2)}) collective-permute-start(bf16[64,1536]{1,0:T(8,128)(2,1)S(1)} %add_convert_fusion), channel_id=1, source_target_pairs={{4,0},{5,1},{8,4},{9,5},{12,8},{13,9},{14,12},{15,13},{10,14},{11,... | collective-permute-start | bytes 589832 | tf_op jit(solution)/shard_map/ppermute | solution.py:280
  97.3 7.2 %collective-permute-start.31 = (bf16[64,1408]{1,0:T(8,128)(2,1)S(1)}, bf16[64,1408]{1,0:T(8,128)(2,1)S(1)}, u32[]{:S(2)}, u32[]{:S(2)}) collective-permute-start(bf16[64,1408]{1,0:T(8,128)(2,1)S(1)} %add_convert_fusion.5), channel_id=1, source_target_pairs={{4,0},{5,1},{8,4},{9,5},{12,8},{13,9},{14,12},{15,13},{10,14},{11,... | collective-permute-start | bytes 540680 | tf_op jit(solution)/shard_map/ppermute | solution.py:280
  99.5 6.4 %collective-permute-start.20 = (bf16[64,1536]{1,0:T(8,128)(2,1)S(1)}, bf16[64,1536]{1,0:T(8,128)(2,1)S(1)}, u32[]{:S(2)}, u32[]{:S(2)}) collective-permute-start(bf16[64,1536]{1,0:T(8,128)(2,1)S(1)} %add_convert_fusion.2), channel_id=1, source_target_pairs={{0,4},{1,5},{4,8},{5,9},{8,12},{9,13},{12,14},{13,15},{14,10},{15,... | collective-permute-start | bytes 589832 | tf_op jit(solution)/shard_map/ppermute | solution.py:280
  (4 other events, 90.4 us)
